TPU v7x, 32 devices: a whole 2x2x4 slice. The times are simulated.
32 devices in a mesh: dp: 8 (over z, y), fsdp: 4 (over x, core).
Axes of the slice: x: 2, y: 2, z: 4, core: 2. Of those that a mesh axis runs over, the one named last changes fastest.
Arguments:
- clean_latent: float32 [32, 320, 20], P(('dp', 'fsdp')), may hold values from -6 to 6
- noise: float32 [32, 320, 20], P(('dp', 'fsdp')), may hold values from -6 to 6
- text_feats: bfloat16 [32, 256, 1024], P(('dp', 'fsdp')), may hold values from -6 to 6
- text_lengths: int32 [32], P(('dp', 'fsdp')), may hold values from 5 to 256, as said below
- timesteps: int32 [32], P(('dp', 'fsdp')), may hold values from 0 to 999
- valid_frames: int32 [32], P(('dp', 'fsdp')), may hold values from 1 to 320, as said below
- w_in: float32 [2, 768, 10752], P(None, ('dp', 'fsdp')), may hold values from -0.21875 to 0.21875
- w_text: float32 [2, 1024, 1536], P(None, ('dp', 'fsdp')), may hold values from -0.1875 to 0.1875
- w_out: float32 [2, 4608, 768], P(None, ('dp', 'fsdp')), may hold values from -0.4375 to 0.4375
- gains: float32 [2, 768], P(None, ('dp', 'fsdp')), may hold values from 0.5 to 1.5
- w_lead: float32 [276, 768], P(None, ('dp', 'fsdp')), may hold values from -0.5 to 0.5
- w_head: float32 [768, 2324], P(('dp', 'fsdp')), may hold values from -0.21875 to 0.21875
- first_in: float32 [2, 768, 10752], P(None, ('dp', 'fsdp')), as said below
- second_in: float32 [2, 768, 10752], P(None, ('dp', 'fsdp')), as said below
- first_text: float32 [2, 1024, 1536], P(None, ('dp', 'fsdp')), as said below
- second_text: float32 [2, 1024, 1536], P(None, ('dp', 'fsdp')), as said below
- first_out: float32 [2, 4608, 768], P(None, ('dp', 'fsdp')), as said below
- second_out: float32 [2, 4608, 768], P(None, ('dp', 'fsdp')), as said below
- first_gains: float32 [2, 768], P(None, ('dp', 'fsdp')), as said below
- second_gains: float32 [2, 768], P(None, ('dp', 'fsdp')), as said below
- first_lead: float32 [276, 768], P(None, ('dp', 'fsdp')), as said below
- second_lead: float32 [276, 768], P(None, ('dp', 'fsdp')), as said below
- first_head: float32 [768, 2324], P(('dp', 'fsdp')), as said below
- second_head: float32 [768, 2324], P(('dp', 'fsdp')), as said below
Outputs:
- loss_sum: float32 [], replicated
- frame_count: float32 [], replicated
- grad_norm: float32 [], replicated
- moment_in: float32 [2, 768, 10752], P(None, ('dp', 'fsdp'))
- square_in: float32 [2, 768, 10752], P(None, ('dp', 'fsdp'))
- weight_in: float32 [2, 768, 10752], P(None, ('dp', 'fsdp'))
- moment_text: float32 [2, 1024, 1536], P(None, ('dp', 'fsdp'))
- square_text: float32 [2, 1024, 1536], P(None, ('dp', 'fsdp'))
- weight_text: float32 [2, 1024, 1536], P(None, ('dp', 'fsdp'))
- moment_out: float32 [2, 4608, 768], P(None, ('dp', 'fsdp'))
- square_out: float32 [2, 4608, 768], P(None, ('dp', 'fsdp'))
- weight_out: float32 [2, 4608, 768], P(None, ('dp', 'fsdp'))
- moment_gains: float32 [2, 768], P(None, ('dp', 'fsdp'))
- square_gains: float32 [2, 768], P(None, ('dp', 'fsdp'))
- weight_gains: float32 [2, 768], P(None, ('dp', 'fsdp'))
- moment_lead: float32 [276, 768], P(None, ('dp', 'fsdp'))
- square_lead: float32 [276, 768], P(None, ('dp', 'fsdp'))
- weight_lead: float32 [276, 768], P(None, ('dp', 'fsdp'))
- moment_head: float32 [768, 2324], P(('dp', 'fsdp'))
- square_head: float32 [768, 2324], P(('dp', 'fsdp'))
- weight_head: float32 [768, 2324], P(('dp', 'fsdp'))
Inputs may be any that keep to these rules, and one draw needn't show every extreme that they name: `text_lengths`: the first clip's caption has 5 tokens and the second's 256. `valid_frames`: the last clip has all 320 frames. `first_in`: entries of both signs. `second_in`: Positive. `first_text`: entries of both signs. `second_text`: Positive. `first_out`: entries of both signs. `second_out`: Positive. `first_gains`: entries of both signs. `second_gains`: Positive. `first_lead`: entries of both signs. `second_lead`: Positive. `first_head`: entries of both signs. `second_head`: Positive.
All inputs are finite; a program needn't handle non-finite values.
Results may differ from a plain program's by a relative error of at most 0.013.
The roundings to bfloat16 on the way count: a program that leaves them out, or rounds other values in their place, can miss the bound.
Values may be sent and summed in bfloat16 or wider, within the bound.
A program may use at most 448 MiB of HBM per device.

v0:
```python
import math

import jax
import jax.numpy as jnp
from jax import lax
from jax.sharding import PartitionSpec as P

D = 768
HEADS = 12
HEAD_DIM = 64
FF = 3072
FREQS = 256
LAYERS = 2
STEP = 10


EPSILON = 1e-06
NEGATIVE = -1e30
BETA_ONE = 0.5
BETA_TWO = 0.5
LEARN_RATE = 0.02
GAIN_RATE = 0.3
WEIGHT_DECAY = 0.01
ADAM_EPSILON = 1e-08
CLIP_NORM = 1.0


def for_sending(value):
    return jax.tree.map(lambda a: a.astype(jnp.bfloat16) if a.dtype == jnp.float32 else a, value)


def norm_rows(values):
    centred = values - jnp.mean(values, -1, keepdims=True)
    return centred * lax.rsqrt(jnp.mean(centred * centred, -1, keepdims=True) + EPSILON)


def modulate(stream, shift, scale_part):
    return norm_rows(stream) * (1.0 + scale_part[:, None, :]) + shift[:, None, :]


def gained_norm(stream, gain):
    return norm_rows(stream) * gain


def dense(left, right):
    return jnp.dot(left, right, preferred_element_type=jnp.float32)


def weight_grad(left, right):
    return jnp.einsum("...i,...j->ij", left, right, preferred_element_type=jnp.float32)


def to_low(values):
    return values.astype(jnp.bfloat16)


def split_heads(values):
    return values.reshape(values.shape[0], values.shape[1], HEADS, HEAD_DIM)


def attention(queries, keys, values, keep):
    scores = jnp.einsum(
        "bqhd,bkhd->bhqk",
        split_heads(queries),
        split_heads(keys),
        preferred_element_type=jnp.float32,
    ) * HEAD_DIM ** (-0.5)
    scores = jnp.where(keep[:, None, None, :], scores, NEGATIVE)
    shifted = jnp.exp(scores - jnp.max(scores, -1, keepdims=True))
    probs = shifted / jnp.sum(shifted, -1, keepdims=True)
    mixed = jnp.einsum(
        "bhqk,bkhd->bqhd", to_low(probs), split_heads(values), preferred_element_type=jnp.float32
    )
    return (to_low(mixed.reshape(queries.shape)), probs)


def attention_back(queries, keys, values, probs, grad_mixed):
    grad_heads = split_heads(to_low(grad_mixed))
    grad_values = jnp.einsum(
        "bhqk,bqhd->bkhd", to_low(probs), grad_heads, preferred_element_type=jnp.float32
    )
    grad_probs = jnp.einsum(
        "bqhd,bkhd->bhqk", grad_heads, split_heads(values), preferred_element_type=jnp.float32
    )
    grad_scores = to_low(probs * (grad_probs - jnp.sum(probs * grad_probs, -1, keepdims=True)))
    grad_queries = jnp.einsum(
        "bhqk,bkhd->bqhd", grad_scores, split_heads(keys), preferred_element_type=jnp.float32
    ) * HEAD_DIM ** (-0.5)
    grad_keys = jnp.einsum(
        "bhqk,bqhd->bkhd", grad_scores, split_heads(queries), preferred_element_type=jnp.float32
    ) * HEAD_DIM ** (-0.5)
    return (
        grad_queries.reshape(queries.shape),
        grad_keys.reshape(keys.shape),
        grad_values.reshape(values.shape),
    )


def noise_level(steps):
    phase = (steps.astype(jnp.float32) / 1000.0 + 0.008) / 1.008 * (math.pi / 2)
    return jnp.cos(phase) ** 2


def time_features(steps):
    half_width = FREQS // 2
    frequency = jnp.exp(-math.log(10000.0) * jnp.arange(half_width, dtype=jnp.float32) / half_width)
    angles = steps.astype(jnp.float32)[:, None] * frequency[None, :]
    return jnp.concatenate([jnp.cos(angles), jnp.sin(angles)], -1)


def gather_layer(w_in, w_text, w_out, gains, index, site_again):
    shards = (w_in[index], w_text[index], w_out[index])
    flats = tuple((to_low(item).reshape(-1) for item in shards)) + (to_low(gains[index]),)
    if site_again:
        whole = jax.tree.map(
            lambda part, own: part.astype(own.dtype),
            lax.all_gather(for_sending(flats), ("dp", "fsdp"), axis=0, tiled=True),
            flats,
        )
    else:
        whole = jax.tree.map(
            lambda part, own: part.astype(own.dtype),
            lax.all_gather(for_sending(flats), ("dp", "fsdp"), axis=0, tiled=True),
            flats,
        )
    return (
        whole[0].reshape(-1, shards[0].shape[1]),
        whole[1].reshape(-1, shards[1].shape[1]),
        whole[2].reshape(-1, shards[2].shape[1]),
        whole[3],
    )


def layer_forward(stream, cond_low, text_low, frame_keep, text_keep, weights):
    w_joint, w_textkv, w_back, gain = weights
    modulation = dense(cond_low, w_joint[:, 4 * D + FF :])
    normed_one, pull_one = jax.vjp(modulate, stream, modulation[:, :D], modulation[:, D : 2 * D])
    input_one = to_low(normed_one)
    self_proj = to_low(dense(input_one, w_joint[:, : 3 * D]))
    mixed_one, probs_one = attention(
        self_proj[..., :D], self_proj[..., D : 2 * D], self_proj[..., 2 * D :], frame_keep
    )
    branch_one = dense(mixed_one, w_back[:D])
    stream_two = stream + modulation[:, None, 2 * D : 3 * D] * branch_one
    normed_two, pull_two = jax.vjp(gained_norm, stream_two, gain.astype(jnp.float32))
    input_two = to_low(normed_two)
    cross_query = to_low(dense(input_two, w_joint[:, 3 * D : 4 * D]))
    cross_kv = to_low(dense(text_low, w_textkv))
    mixed_two, probs_two = attention(cross_query, cross_kv[..., :D], cross_kv[..., D:], text_keep)
    stream_three = stream_two + dense(mixed_two, w_back[D : 2 * D])
    normed_three, pull_three = jax.vjp(
        modulate, stream_three, modulation[:, 3 * D : 4 * D], modulation[:, 4 * D : 5 * D]
    )
    input_three = to_low(normed_three)
    hidden_act, pull_act = jax.vjp(jax.nn.gelu, dense(input_three, w_joint[:, 4 * D : 4 * D + FF]))
    hidden_low = to_low(hidden_act)
    branch_three = dense(hidden_low, w_back[2 * D :])
    result = stream_three + modulation[:, None, 5 * D :] * branch_three
    saved = (
        modulation,
        pull_one,
        input_one,
        self_proj,
        mixed_one,
        probs_one,
        branch_one,
        pull_two,
        input_two,
        cross_query,
        cross_kv,
        mixed_two,
        probs_two,
        pull_three,
        input_three,
        pull_act,
        hidden_low,
        branch_three,
    )
    return (result, saved)


def layer_backward(stream, grad_out, cond_low, text_low, frame_keep, text_keep, weights):
    w_joint, w_textkv, w_back, gain = weights
    _, saved = layer_forward(stream, cond_low, text_low, frame_keep, text_keep, weights)
    (
        modulation,
        pull_one,
        input_one,
        self_proj,
        mixed_one,
        probs_one,
        branch_one,
        pull_two,
        input_two,
        cross_query,
        cross_kv,
        mixed_two,
        probs_two,
        pull_three,
        input_three,
        pull_act,
        hidden_low,
        branch_three,
    ) = saved
    grad_three = to_low(grad_out * modulation[:, None, 5 * D :])
    grad_gate_two = jnp.sum(grad_out * branch_three, 1)
    grad_down = weight_grad(hidden_low, grad_three)
    (grad_pre,) = pull_act(dense(grad_three, w_back[2 * D :].T))
    grad_pre = to_low(grad_pre)
    grad_up = weight_grad(input_three, grad_pre)
    grad_inner, grad_shift_two, grad_scale_two = pull_three(
        dense(grad_pre, w_joint[:, 4 * D : 4 * D + FF].T)
    )
    grad_stream = grad_out + grad_inner
    grad_cross_out = to_low(grad_stream)
    grad_co = weight_grad(mixed_two, grad_cross_out)
    grad_cq, grad_ck, grad_cv = attention_back(
        cross_query,
        cross_kv[..., :D],
        cross_kv[..., D:],
        probs_two,
        dense(grad_cross_out, w_back[D : 2 * D].T),
    )
    grad_cq = to_low(grad_cq)
    grad_text_w = weight_grad(text_low, to_low(jnp.concatenate([grad_ck, grad_cv], -1)))
    grad_query_w = weight_grad(input_two, grad_cq)
    grad_inner, grad_gain = pull_two(dense(grad_cq, w_joint[:, 3 * D : 4 * D].T))
    grad_stream = grad_stream + grad_inner
    grad_one = to_low(grad_stream * modulation[:, None, 2 * D : 3 * D])
    grad_gate_one = jnp.sum(grad_stream * branch_one, 1)
    grad_ao = weight_grad(mixed_one, grad_one)
    grad_q, grad_k, grad_v = attention_back(
        self_proj[..., :D],
        self_proj[..., D : 2 * D],
        self_proj[..., 2 * D :],
        probs_one,
        dense(grad_one, w_back[:D].T),
    )
    grad_self = to_low(jnp.concatenate([grad_q, grad_k, grad_v], -1))
    grad_self_w = weight_grad(input_one, grad_self)
    grad_inner, grad_shift_one, grad_scale_one = pull_one(dense(grad_self, w_joint[:, : 3 * D].T))
    grad_stream = grad_stream + grad_inner
    grad_mod = to_low(
        jnp.concatenate(
            [
                grad_shift_one,
                grad_scale_one,
                grad_gate_one,
                grad_shift_two,
                grad_scale_two,
                grad_gate_two,
            ],
            -1,
        )
    )
    grad_mod_w = weight_grad(cond_low, grad_mod)
    grad_cond = dense(grad_mod, w_joint[:, 4 * D + FF :].T)
    grads = (
        jnp.concatenate([grad_self_w, grad_query_w, grad_up, grad_mod_w], 1),
        grad_text_w,
        jnp.concatenate([grad_ao, grad_co, grad_down], 0),
        grad_gain,
    )
    return (grad_stream, grad_cond, grads)


def adam_update(weight, grad, first, second, rate):
    first_new = BETA_ONE * first + (1.0 - BETA_ONE) * grad
    second_new = BETA_TWO * second + (1.0 - BETA_TWO) * grad * grad
    first_hat = first_new / (1.0 - BETA_ONE**STEP)
    second_hat = second_new / (1.0 - BETA_TWO**STEP)
    weight_new = weight - rate * (
        first_hat / (jnp.sqrt(second_hat) + ADAM_EPSILON) + WEIGHT_DECAY * weight
    )
    return (first_new, second_new, weight_new)


def body(
    clean_latent,
    noise,
    text_feats,
    text_lengths,
    timesteps,
    valid_frames,
    w_in,
    w_text,
    w_out,
    gains,
    w_lead,
    w_head,
    first_in,
    second_in,
    first_text,
    second_text,
    first_out,
    second_out,
    first_gains,
    second_gains,
    first_lead,
    second_lead,
    first_head,
    second_head,
):
    frame_keep = lax.broadcasted_iota(jnp.int32, clean_latent.shape[:2], 1) < valid_frames[:, None]
    text_keep = lax.broadcasted_iota(jnp.int32, text_feats.shape[:2], 1) < text_lengths[:, None]
    frame_count = lax.psum(jnp.sum(valid_frames).astype(jnp.float32), ("dp", "fsdp"))
    lead_rows = w_lead.shape[0]
    head_cols = w_head.shape[1]
    lead_flat, head_flat = (
        lax.all_gather(to_low(w_lead).T.reshape(-1), ("dp", "fsdp"), axis=0, tiled=True),
        lax.all_gather(to_low(w_head).reshape(-1), ("dp", "fsdp"), axis=0, tiled=True),
    )
    lead_full = lead_flat.reshape(-1, lead_rows).T
    head_full = head_flat.reshape(-1, head_cols)
    level = noise_level(timesteps)[:, None, None]
    noisy_low = to_low(jnp.sqrt(level) * clean_latent + jnp.sqrt(1.0 - level) * noise)
    sinus_low = to_low(time_features(timesteps))
    act_time, pull_time = jax.vjp(jax.nn.silu, dense(sinus_low, lead_full[:FREQS]))
    act_low = to_low(act_time)
    cond, pull_cond = jax.vjp(jax.nn.silu, dense(act_low, head_full[:, :D]))
    cond_low = to_low(cond)
    stream = dense(noisy_low, lead_full[FREQS:])
    kept_inputs = []
    for index in range(LAYERS):
        weights = gather_layer(w_in, w_text, w_out, gains, index, False)
        kept_inputs.append(stream)
        stream, _ = layer_forward(stream, cond_low, text_feats, frame_keep, text_keep, weights)
    final_mod = dense(cond_low, head_full[:, D : 3 * D])
    normed_final, pull_final = jax.vjp(modulate, stream, final_mod[:, :D], final_mod[:, D:])
    final_low = to_low(normed_final)
    error = dense(final_low, head_full[:, 3 * D :]) - noise
    loss_sum = lax.psum(
        jnp.sum(jnp.where(frame_keep[..., None], error * error, 0.0)), ("dp", "fsdp")
    )
    grad_pred = to_low(jnp.where(frame_keep[..., None], error * (2.0 / frame_count), 0.0))
    grad_pred_w = weight_grad(final_low, grad_pred)
    grad_stream, grad_shift_f, grad_scale_f = pull_final(dense(grad_pred, head_full[:, 3 * D :].T))
    grad_final_mod = to_low(jnp.concatenate([grad_shift_f, grad_scale_f], -1))
    grad_final_w = weight_grad(cond_low, grad_final_mod)
    grad_cond = dense(grad_final_mod, head_full[:, D : 3 * D].T)
    layer_shards = [None] * LAYERS
    for index in reversed(range(LAYERS)):
        weights = gather_layer(w_in, w_text, w_out, gains, index, True)
        grad_stream, grad_cond_part, grads = layer_backward(
            kept_inputs[index], grad_stream, cond_low, text_feats, frame_keep, text_keep, weights
        )
        grad_cond = grad_cond + grad_cond_part
        flats = (grads[0].reshape(-1), grads[1].reshape(-1), grads[2].reshape(-1), grads[3])
        summed = (
            lax.psum_scatter(flats[0], ("dp", "fsdp"), scatter_dimension=0, tiled=True),
            lax.psum_scatter(flats[1], ("dp", "fsdp"), scatter_dimension=0, tiled=True),
            lax.psum_scatter(flats[2], ("dp", "fsdp"), scatter_dimension=0, tiled=True),
            lax.psum_scatter(flats[3], ("dp", "fsdp"), scatter_dimension=0, tiled=True),
        )
        layer_shards[index] = (
            summed[0].reshape(w_in.shape[1:]),
            summed[1].reshape(w_text.shape[1:]),
            summed[2].reshape(w_out.shape[1:]),
            summed[3],
        )
    (grad_temb,) = pull_cond(grad_cond)
    grad_temb = to_low(grad_temb)
    grad_time_two = weight_grad(act_low, grad_temb)
    (grad_pre_time,) = pull_time(dense(grad_temb, head_full[:, :D].T))
    grad_time_one = weight_grad(sinus_low, to_low(grad_pre_time))
    grad_input_w = weight_grad(noisy_low, to_low(grad_stream))
    lead_grad = jnp.concatenate([grad_time_one, grad_input_w], 0)
    head_grad = jnp.concatenate([grad_time_two, grad_final_w, grad_pred_w], 1)
    lead_sum, head_sum = (
        lax.psum_scatter(lead_grad.T.reshape(-1), ("dp", "fsdp"), scatter_dimension=0, tiled=True),
        lax.psum_scatter(head_grad.reshape(-1), ("dp", "fsdp"), scatter_dimension=0, tiled=True),
    )
    lead_shard = lead_sum.reshape(w_lead.shape[1], w_lead.shape[0]).T
    head_shard = head_sum.reshape(w_head.shape)
    grad_list = [
        jnp.stack([layer_shards[index][member] for index in range(LAYERS)]) for member in range(4)
    ]
    grad_list = grad_list + [lead_shard, head_shard]
    local_squares = sum((jnp.sum(item * item) for item in grad_list))
    grad_norm = jnp.sqrt(lax.psum(local_squares, ("dp", "fsdp")))
    factor = CLIP_NORM / jnp.maximum(grad_norm, CLIP_NORM)
    params = (w_in, w_text, w_out, gains, w_lead, w_head)
    firsts = (first_in, first_text, first_out, first_gains, first_lead, first_head)
    seconds = (second_in, second_text, second_out, second_gains, second_lead, second_head)
    rates = (LEARN_RATE, LEARN_RATE, LEARN_RATE, GAIN_RATE, LEARN_RATE, LEARN_RATE)
    results = []
    for weight, grad, first, second, rate in zip(params, grad_list, firsts, seconds, rates):
        results.extend(adam_update(weight, grad * factor, first, second, rate))
    return (
        loss_sum,
        frame_count,
        grad_norm,
        results[0],
        results[1],
        results[2],
        results[3],
        results[4],
        results[5],
        results[6],
        results[7],
        results[8],
        results[9],
        results[10],
        results[11],
        results[12],
        results[13],
        results[14],
        results[15],
        results[16],
        results[17],
    )


def solution(mesh):
    return jax.shard_map(
        body,
        mesh=mesh,
        in_specs=(
            P(("dp", "fsdp"), None, None),
            P(("dp", "fsdp"), None, None),
            P(("dp", "fsdp"), None, None),
            P(("dp", "fsdp")),
            P(("dp", "fsdp")),
            P(("dp", "fsdp")),
            P(None, ("dp", "fsdp"), None),
            P(None, ("dp", "fsdp"), None),
            P(None, ("dp", "fsdp"), None),
            P(None, ("dp", "fsdp")),
            P(None, ("dp", "fsdp")),
            P(("dp", "fsdp"), None),
            P(None, ("dp", "fsdp"), None),
            P(None, ("dp", "fsdp"), None),
            P(None, ("dp", "fsdp"), None),
            P(None, ("dp", "fsdp"), None),
            P(None, ("dp", "fsdp"), None),
            P(None, ("dp", "fsdp"), None),
            P(None, ("dp", "fsdp")),
            P(None, ("dp", "fsdp")),
            P(None, ("dp", "fsdp")),
            P(None, ("dp", "fsdp")),
            P(("dp", "fsdp"), None),
            P(("dp", "fsdp"), None),
        ),
        out_specs=(
            P(),
            P(),
            P(),
            P(None, ("dp", "fsdp"), None),
            P(None, ("dp", "fsdp"), None),
            P(None, ("dp", "fsdp"), None),
            P(None, ("dp", "fsdp"), None),
            P(None, ("dp", "fsdp"), None),
            P(None, ("dp", "fsdp"), None),
            P(None, ("dp", "fsdp"), None),
            P(None, ("dp", "fsdp"), None),
            P(None, ("dp", "fsdp"), None),
            P(None, ("dp", "fsdp")),
            P(None, ("dp", "fsdp")),
            P(None, ("dp", "fsdp")),
            P(None, ("dp", "fsdp")),
            P(None, ("dp", "fsdp")),
            P(None, ("dp", "fsdp")),
            P(("dp", "fsdp"), None),
            P(("dp", "fsdp"), None),
            P(("dp", "fsdp"), None),
        ),
        check_vma=False,
    )
```

profile of v0, /device:TPU:0, one launch (start us, length us, event | category | flops | bytes accessed | tf_op | source)
XLA Modules:
  0.0 2855.9 jit_solution(4557905073872561609)
XLA Ops:
  29.1 42.0 %all-reduce.17 = (bf16[768]{0:T(1024)(128)(2,1)S(1)}, bf16[768]{0:T(1024)(128)(2,1)S(1)}) all-reduce(bf16[768]{0:T(1024)(128)(2,1)S(1)} %dynamic-update-slice.2, bf16[768]{0:T(1024)(128)(2,1)S(1)} %dynamic-update-slice.3), channel_id=2, replica_groups=mesh['dp'=8,'fsdp'=4] {'dp','fsdp'}, use_global_device_ids=true, to_apply=%add.2 | all-reduce | flops 1536 | bytes 6144
  72.4 40.5 %psum.22 = f32[]{:T(128)} all-reduce(f32[]{:T(128)S(6)} %convert_element_type.474), channel_id=1, replica_groups=mesh['dp'=8,'fsdp'=4] {'dp','fsdp'}, use_global_device_ids=true, to_apply=%region_24.25 | all-reduce | flops 1 | bytes 8 | tf_op jit(solution)/shard_map/psum | solution.py:306
  113.7 46.3 %all-reduce.24.cloned.1.call-done = (bf16[211968]{0:T(1024)(128)(2,1)}, bf16[1784832]{0:T(1024)(128)(2,1)}) async-done(((bf16[211968]{0:T(1024)(128)(2,1)}, bf16[1784832]{0:T(1024)(128)(2,1)}), (bf16[211968]{0:T(1024)(128)(2,1)}, bf16[1784832]{0:T(1024)(128)(2,1)})) %all-reduce.24.cloned.1.call-update) | async-done | bytes 3993616
  163.2 9.6 reshape.1752
  178.6 43.0 %all-gather.13.cloned.1.call-done = bf16[1572864]{0:T(1024)(128)(2,1)} async-done(((bf16[49152]{0:T(1024)(128)(2,1)}), bf16[1572864]{0:T(1024)(128)(2,1)}) %all-gather.13.cloned.1.call-update) | async-done | bytes 3145744 | tf_op jit(solution)/shard_map/all_gather | solution.py:123
  221.6 6.8 reshape.1758
  232.5 50.4 %all-gather.19.cloned.1.call-done = bf16[1572864]{0:T(1024)(128)(2,1)} async-done(((bf16[49152]{0:T(1024)(128)(2,1)}), bf16[1572864]{0:T(1024)(128)(2,1)}) %all-gather.19.cloned.1.call-update) | async-done | bytes 3145744 | tf_op jit(solution)/shard_map/all_gather | solution.py:123
  282.8 6.8 reshape.1766
  294.4 63.1 %all-gather.11.cloned.1.call-done = bf16[3538944]{0:T(1024)(128)(2,1)} async-done(((bf16[110592]{0:T(1024)(128)(2,1)}), bf16[3538944]{0:T(1024)(128)(2,1)}) %all-gather.11.cloned.1.call-update) | async-done | bytes 7077904 | tf_op jit(solution)/shard_map/all_gather | solution.py:123
  372.9 9.7 slice.327
  382.6 49.3 %all-gather.17.cloned.1.call-done = bf16[3538944]{0:T(1024)(128)(2,1)} async-done(((bf16[110592]{0:T(1024)(128)(2,1)}), bf16[3538944]{0:T(1024)(128)(2,1)}) %all-gather.17.cloned.1.call-update) | async-done | bytes 7077904 | tf_op jit(solution)/shard_map/all_gather | solution.py:123
  447.3 9.3 slice.352
  456.6 90.9 %all-gather.9.cloned.1.call-done = bf16[8257536]{0:T(1024)(128)(2,1)} async-done(((bf16[258048]{0:T(1024)(128)(2,1)}), bf16[8257536]{0:T(1024)(128)(2,1)}) %all-gather.9.cloned.1.call-update) | async-done | bytes 16515088 | tf_op jit(solution)/shard_map/all_gather | solution.py:123
  547.5 27.4 reshape.1753
  617.3 45.7 %all-gather.15.cloned.1.call-done = bf16[8257536]{0:T(1024)(128)(2,1)} async-done(((bf16[258048]{0:T(1024)(128)(2,1)}), bf16[8257536]{0:T(1024)(128)(2,1)}) %all-gather.15.cloned.1.call-update) | async-done | bytes 16515088 | tf_op jit(solution)/shard_map/all_gather | solution.py:123
  663.0 27.3 reshape.1762
  913.7 10.1 reshape.1782
  931.3 10.0 pad_maximum_fusion.3
  941.3 15.4 reshape.1780
  956.8 10.0 pad_maximum_fusion.2
  966.8 15.3 reshape.1779
  985.9 6.6 copy.148
  992.4 7.0 reshape.1778
  1009.8 6.9 reshape.1777
  1016.7 12.8 broadcast_multiply_fusion
  1029.4 21.5 pad_maximum_fusion.1
  1050.9 30.5 %reshape.1776 = f32[8257536]{0:T(1024)} reshape(f32[768,10752]{1,0:T(8,128)} %pad_maximum_fusion.1) | data formatting | bytes 66060288 | tf_op jit(solution)/shard_map/reshape | solution.py:348
  1081.4 21.6 pad_maximum_fusion
  1103.0 30.4 %reshape.1775 = f32[8257536]{0:T(1024)} reshape(f32[768,10752]{1,0:T(8,128)} %pad_maximum_fusion) | data formatting | bytes 66060288 | tf_op jit(solution)/shard_map/reshape | solution.py:348
  1134.1 40.9 %all-reduce.15 = (f32[768]{0:T(1024)S(1)}, f32[768]{0:T(1024)S(1)}) all-reduce(f32[768]{0:T(1024)S(1)} %copy-done.204, f32[768]{0:T(1024)S(1)} %copy-done.205), channel_id=11, replica_groups=mesh['dp'=8,'fsdp'=4] {'dp','fsdp'}, use_global_device_ids=true, to_apply=%region_65.66.clone | all-reduce | flops 1536 | bytes 12288
  1176.3 1590.1 %all-reduce.22.cloned.1.call-done = (f32[8257536]{0:T(1024)}, f32[8257536]{0:T(1024)}, f32[1572864]{0:T(1024)}, f32[1572864]{0:T(1024)}, f32[3538944]{0:T(1024)}...) async-done(((f32[8257536]{0:T(1024)}, f32[8257536]{0:T(1024)}, f32[1572864]{0:T(1024)}, f32[1572864]{0:T(1024)}, f32[3538944]{0:T(1024)}, ...) | async-done | bytes 114941968
  2790.3 39.8 %all-reduce.14 = (f32[]{:T(128)}, f32[]{:T(128)}) all-reduce(f32[]{:T(128)} %get-tuple-element.170, f32[]{:T(128)S(6)} %add.499), channel_id=1, replica_groups=mesh['dp'=8,'fsdp'=4] {'dp','fsdp'}, use_global_device_ids=true, to_apply=%region_23.24 | all-reduce | flops 2 | bytes 16 | tf_op jit(solution)/shard_map/psum | solution.py:332
  (761 shorter events, 392.7 us)
Async XLA Ops:
  7.2 221.2 %copy-start = (bf16[1,256,1024]{2,1,0:T(8,128)(2,1)S(1)}, bf16[1,256,1024]{2,1,0:T(8,128)(2,1)}, u32[]{:S(2)}) copy-start(bf16[1,256,1024]{2,1,0:T(8,128)(2,1)} %param.26) | copy-start | bytes 1572868
  7.2 152.8 %all-reduce.24.cloned.1.call-start = ((), (), s32[]{:S(2)}) async-start(), calls=%async_computation.7 | async-start | bytes 7987200
  15.5 206.1 %all-gather.13.cloned.1.call-start = ((), (), s32[]{:S(2)}) async-start(), calls=%async_computation.2 | async-start | bytes 3244032 | tf_op jit(solution)/shard_map/all_gather | solution.py:123
  19.1 263.8 %all-gather.19.cloned.1.call-start = ((), (), s32[]{:S(2)}) async-start(), calls=%async_computation.5 | async-start | bytes 3244032 | tf_op jit(solution)/shard_map/all_gather | solution.py:123
  20.8 336.7 %all-gather.11.cloned.1.call-start = ((), (), s32[]{:S(2)}) async-start(), calls=%async_computation.1 | async-start | bytes 7299072 | tf_op jit(solution)/shard_map/all_gather | solution.py:123
  21.9 410.0 %all-gather.17.cloned.1.call-start = ((), (), s32[]{:S(2)}) async-start(), calls=%async_computation.4 | async-start | bytes 7299072 | tf_op jit(solution)/shard_map/all_gather | solution.py:123
  22.9 90.8 %copy-start.122 = (f32[1,320,20]{1,0,2:T(1,128)S(1)}, f32[1,320,20]{1,0,2:T(1,128)}, u32[]{:S(2)}) copy-start(f32[1,320,20]{1,0,2:T(1,128)} %param.25) | copy-start | bytes 76804
  22.9 90.8 %copy-start.163 = (f32[1,320,20]{1,0,2:T(1,128)S(1)}, f32[1,320,20]{1,0,2:T(1,128)}, u32[]{:S(2)}) copy-start(f32[1,320,20]{1,0,2:T(1,128)} %param.24) | copy-start | bytes 76804
  22.9 524.6 %all-gather.9.cloned.1.call-start = ((), (), s32[]{:S(2)}) async-start(), calls=%async_computation | async-start | bytes 17031168 | tf_op jit(solution)/shard_map/all_gather | solution.py:123
  24.8 638.2 %all-gather.15.cloned.1.call-start = ((), (), s32[]{:S(2)}) async-start(), calls=%async_computation.3 | async-start | bytes 17031168 | tf_op jit(solution)/shard_map/all_gather | solution.py:123
  26.4 2739.9 %all-reduce.22.cloned.1.call-start = ((), (), s32[]{:S(2)}) async-start(), calls=%async_computation.6 | async-start | bytes 229883904
  28.6 559.6 %copy-start.199 = (pred[320]{0:T(512)(128)(4,1)}, pred[320]{0:T(512)(128)(4,1)S(1)}, u32[]{:S(2)}) copy-start(pred[320]{0:T(512)(128)(4,1)S(1)} %iota_compare_fusion) | copy-start | bytes 964
  71.2 527.5 %copy-start.151 = (f32[768]{0:T(1024)}, f32[768]{0:T(1024)S(1)}, u32[]{:S(2)}) copy-start(f32[768]{0:T(1024)S(1)} %convert_element_type.505) | copy-start | bytes 9220
  71.8 529.1 %copy-start.220 = (pred[256]{0:T(512)(128)(4,1)}, pred[256]{0:T(512)(128)(4,1)S(1)}, u32[]{:S(2)}) copy-start(pred[256]{0:T(512)(128)(4,1)S(1)} %iota_compare_fusion.1) | copy-start | bytes 772
  113.7 61.4 %copy-start.124 = (bf16[1,320,20]{1,0,2:T(2,128)(2,1)}, bf16[1,320,20]{1,0,2:T(2,128)(2,1)S(1)}, u32[]{:S(2)}) copy-start(bf16[1,320,20]{1,0,2:T(2,128)(2,1)S(1)} %add_convert_fusion.7) | copy-start | bytes 38404
  174.4 54.0 %copy-start.146 = (f32[768]{0:T(1024)}, f32[768]{0:T(1024)S(1)}, u32[]{:S(2)}) copy-start(f32[768]{0:T(1024)S(1)} %convolution_reduce_fusion.2) | copy-start | bytes 9220
  175.5 421.3 %copy-start.2 = (f32[320,768]{1,0:T(8,128)}, f32[320,768]{1,0:T(8,128)S(1)}, u32[]{:S(2)}) copy-start(f32[320,768]{1,0:T(8,128)S(1)} %get-tuple-element.153) | copy-start | bytes 2949124
  175.5 404.0 %copy-start.129 = (f32[320]{0:T(512)}, f32[320]{0:T(512)S(1)}, u32[]{:S(2)}) copy-start(f32[320]{0:T(512)S(1)} %broadcast_multiply_fusion.11) | copy-start | bytes 3844
  175.8 52.6 %copy-start.174 = (f32[320]{0:T(512)}, f32[320]{0:T(512)S(1)}, u32[]{:S(2)}) copy-start(f32[320]{0:T(512)S(1)} %multiply_reduce_fusion.29) | copy-start | bytes 3844
  175.8 403.7 %copy-start.135 = (f32[320]{0:T(512)}, f32[320]{0:T(512)S(1)}, u32[]{:S(2)}) copy-start(f32[320]{0:T(512)S(1)} %fusion.177) | copy-start | bytes 3844
  231.5 369.4 %copy-start.90 = (bf16[1,256,768]{1,2,0:T(8,128)(2,1)}, bf16[1,256,768]{1,2,0:T(8,128)(2,1)S(1)}, u32[]{:S(2)}) copy-start(bf16[1,256,768]{1,2,0:T(8,128)(2,1)S(1)} %copy.126) | copy-start | bytes 1179652
  607.9 192.8 %copy-start.127 = (f32[320]{0:T(512)}, f32[320]{0:T(512)S(1)}, u32[]{:S(2)}) copy-start(f32[320]{0:T(512)S(1)} %broadcast_multiply_fusion.9) | copy-start | bytes 3844
  608.2 192.6 %copy-start.131 = (f32[320]{0:T(512)}, f32[320]{0:T(512)S(1)}, u32[]{:S(2)}) copy-start(f32[320]{0:T(512)S(1)} %fusion.179) | copy-start | bytes 3844
  617.0 77.4 %copy-start.16 = (f32[320,768]{1,0:T(8,128)}, f32[320,768]{1,0:T(8,128)S(1)}, u32[]{:S(2)}) copy-start(f32[320,768]{1,0:T(8,128)S(1)} %get-tuple-element.121) | copy-start | bytes 2949124
  617.3 73.0 %copy-start.180 = (f32[320]{0:T(512)}, f32[320]{0:T(512)S(1)}, u32[]{:S(2)}) copy-start(f32[320]{0:T(512)S(1)} %multiply_reduce_fusion.26) | copy-start | bytes 3844
  617.3 77.1 %copy-start.138 = (f32[320]{0:T(512)}, f32[320]{0:T(512)S(1)}, u32[]{:S(2)}) copy-start(f32[320]{0:T(512)S(1)} %fusion.180) | copy-start | bytes 3844
  827.3 43.8 %copy-start.80 = (bf16[12,64,320]{2,1,0:T(8,128)(2,1)}, bf16[12,64,320]{2,1,0:T(8,128)(2,1)S(1)}, u32[]{:S(2)}) copy-start(bf16[12,64,320]{2,1,0:T(8,128)(2,1)S(1)} %fusion.77) | copy-start | bytes 1474564
  828.3 42.8 %copy-start.81 = (bf16[12,64,320]{2,1,0:T(8,128)(2,1)}, bf16[12,64,320]{2,1,0:T(8,128)(2,1)S(1)}, u32[]{:S(2)}) copy-start(bf16[12,64,320]{2,1,0:T(8,128)(2,1)S(1)} %fusion.78) | copy-start | bytes 1474564
  829.6 41.5 %copy-start.106 = (bf16[12,64,320]{2,1,0:T(8,128)(2,1)}, bf16[12,64,320]{2,1,0:T(8,128)(2,1)S(1)}, u32[]{:S(2)}) copy-start(bf16[12,64,320]{2,1,0:T(8,128)(2,1)S(1)} %fusion.82) | copy-start | bytes 1474564
  2778.4 57.0 %copy-start.216 = (f32[2,24]{1,0:T(2,128)S(1)}, f32[2,24]{1,0:T(2,128)}, u32[]{:S(2)}) copy-start(f32[2,24]{1,0:T(2,128)} %param.33) | copy-start | bytes 580
  2778.4 57.0 %copy-start.217 = (f32[2,24]{1,0:T(2,128)S(1)}, f32[2,24]{1,0:T(2,128)}, u32[]{:S(2)}) copy-start(f32[2,24]{1,0:T(2,128)} %param.43) | copy-start | bytes 580
  2778.4 57.0 %copy-start.218 = (f32[2,24]{1,0:T(2,128)S(1)}, f32[2,24]{1,0:T(2,128)}, u32[]{:S(2)}) copy-start(f32[2,24]{1,0:T(2,128)} %param.42) | copy-start | bytes 580
  (213 other events, 1095.0 us)
Sparse Core Ops, SparseCore 0:
  15.6 144.3 all-reduce.23
  163.4 58.1 all-gather.12
  225.1 57.7 all-gather.18
  286.2 71.2 all-gather.10
  360.8 71.0 all-gather.16
  435.2 112.2 all-gather.8
  551.0 111.9 all-gather.14
  1133.5 1632.7 all-reduce.21
where the time goes:
time: 2870 us; the launch traced here: 2860 us
  waiting for transfers between devices  1980 us (69%)
  local copies, waits for them, and re-layouts  338 us (12%)
  matrix products  226 us (8%)
  blocking collectives  163 us (6%)
  other arithmetic  123 us (4%)
    unnamed x10, waiting for transfers between devices  1640 us
    all_gather x6, waiting for transfers between devices, gather_layer(): lax.all_gather(for_sending(flats), ('dp', 'fsdp'), axis=0, tiled=True)  342 us
    dot_general x38, matrix products, dense(): return jnp.dot(left, right, preferred_element_type=jnp.float32)  109 us
    unnamed x2, blocking collectives  82.9 us
    reshape x2, local copies, waits for them, and re-layouts, body(): grads[0].reshape(-1)  60.9 us
  transfers between devices with their start and end apart: 8, of which 8 were waited for; matrix products, arithmetic and copies ran while one was open for 6% of the time, Pallas kernels for 0%

commit v1 on v0

v1 whole, which is shorter than its diff:
```python
import functools
import math

import jax
import jax.numpy as jnp
from jax import lax
from jax.experimental import pallas as pl
from jax.experimental.pallas import tpu as pltpu
from jax.sharding import PartitionSpec as P

D = 768
HEADS = 12
HEAD_DIM = 64
FF = 3072
FREQS = 256
LAYERS = 2
STEP = 10
MOD = 6 * D
JOINT = 4 * D + FF

EPSILON = 1e-06
NEGATIVE = -1e30
BETA_ONE = 0.5
BETA_TWO = 0.5
LEARN_RATE = 0.02
GAIN_RATE = 0.3
WEIGHT_DECAY = 0.01
ADAM_EPSILON = 1e-08
CLIP_NORM = 1.0

ALL = ("dp", "fsdp")
MESH = pl.DeviceIdType.MESH
VMEM_LIMIT = 60 * 1024 * 1024


def place(ways):
    dp_ways, fsdp_ways = ways
    row, col = lax.axis_index("dp"), lax.axis_index("fsdp")
    sizes = (dp_ways // 2, 2, fsdp_ways // 2)
    spot = (row // 2, lax.rem(row, 2), col // 2)
    return sizes, spot, lax.rem(col, 2)


def device_at(spot, core):
    z, y, x = spot
    return (z * 2 + y, x * 2 + core)


def moved(spot, axis, size, steps):
    spot = list(spot)
    spot[axis] = lax.rem(spot[axis] + steps, size)
    return tuple(spot)


def greet_peers(sizes, spot, core):
    barrier = pltpu.get_barrier_semaphore()
    count = 1
    pl.semaphore_signal(barrier, inc=1, device_id=device_at(spot, 1 - core), device_id_type=MESH)
    for axis in range(3):
        for steps in range(1, sizes[axis]):
            count += 1
            pl.semaphore_signal(
                barrier,
                inc=1,
                device_id=device_at(moved(spot, axis, sizes[axis], steps), core),
                device_id_type=MESH,
            )
    pl.semaphore_wait(barrier, count)


def remote(source, target, send, recv, device):
    return pltpu.make_async_remote_copy(
        src_ref=source, dst_ref=target, send_sem=send, recv_sem=recv, device_id=device, device_id_type=MESH
    )


def exchange_kernel(ways, shared, x_ref, out_ref, send_sem, recv_sem):
    dp_ways, fsdp_ways = ways
    count = dp_ways * fsdp_ways
    me = lax.axis_index("dp") * fsdp_ways + lax.axis_index("fsdp")

    def device(index):
        return (index // fsdp_ways, lax.rem(index, fsdp_ways))

    barrier = pltpu.get_barrier_semaphore()
    for step in range(1, count):
        pl.semaphore_signal(
            barrier, inc=1, device_id=device(lax.rem(me + step, count)), device_id_type=MESH
        )
    pl.semaphore_wait(barrier, count - 1)

    def copy(step):
        other = lax.rem(me + step, count)
        return remote(
            x_ref if shared else x_ref.at[other],
            out_ref.at[me],
            send_sem.at[step],
            recv_sem.at[step],
            device(other),
        )

    for step in range(1, count):
        copy(step).start()
    out_ref[me] = x_ref[...] if shared else x_ref[me]
    for step in range(1, count):
        origin = lax.rem(me + count - step, count)
        remote(
            x_ref if shared else x_ref.at[0],
            out_ref.at[origin],
            send_sem.at[step],
            recv_sem.at[step],
            device(origin),
        ).wait_recv()
    for step in range(1, count):
        copy(step).wait_send()


def exchange(values, ways, shared, number):
    count = ways[0] * ways[1]
    tile = values.shape if shared else values.shape[1:]
    return pl.pallas_call(
        functools.partial(exchange_kernel, ways, shared),
        out_shape=jax.ShapeDtypeStruct((count,) + tile, values.dtype),
        in_specs=[pl.BlockSpec(memory_space=pltpu.VMEM)],
        out_specs=pl.BlockSpec(memory_space=pltpu.VMEM),
        scratch_shapes=[pltpu.SemaphoreType.DMA((count,)), pltpu.SemaphoreType.DMA((count,))],
        compiler_params=pltpu.CompilerParams(
            collective_id=number, has_side_effects=True, vmem_limit_bytes=VMEM_LIMIT
        ),
    )(values)


def gather_kernel(ways, rows, halves, items, layers, *refs):
    members = len(rows)
    shards = refs[:members]
    fulls = refs[members : members + members * layers]
    rest = refs[members + members * layers :]
    stages = rest[:members]
    blocks = rest[members : 2 * members]
    pre_send, pre_recv, own_sem, put_sem, z_send, z_recv, a_send, a_recv, b_send, b_recv, c_send, c_recv = rest[2 * members :]
    sizes, spot, core = place(ways)
    z, y, x = spot
    partner = device_at(spot, 1 - core)
    greet_peers(sizes, spot, core)

    def full(layer, member):
        return fulls[layer * members + member]

    pre = []
    for layer in range(layers):
        for member in range(members):
            height, half = rows[member], halves[member]
            place_in = stages[member].at[layer, pl.ds(pl.multiple_of(core * height, 8), height)]
            mine = shards[member].at[layer, :, pl.ds(pl.multiple_of(core * half, 128), half)]
            other = shards[member].at[layer, :, pl.ds(pl.multiple_of((1 - core) * half, 128), half)]
            index = layer * members + member
            sent = remote(other, place_in, pre_send.at[index], pre_recv.at[index], partner)
            sent.start()
            kept = pltpu.make_async_copy(mine, place_in, own_sem.at[index])
            kept.start()
            pre.append((sent, kept))
    arrived = set()
    puts = []

    def ready(layer, member):
        if (layer, member) in arrived:
            return
        arrived.add((layer, member))
        index = layer * members + member
        height = rows[member]
        sent, kept = pre[index]
        kept.wait()
        theirs = stages[member].at[layer, pl.ds(pl.multiple_of((1 - core) * height, 8), height)]
        remote(theirs, theirs, pre_send.at[index], pre_recv.at[index], partner).wait_recv()
        blocks[member][layer] = stages[member][layer].astype(jnp.bfloat16)
        half = halves[member]
        put = pltpu.make_async_copy(
            blocks[member].at[layer],
            full(layer, member).at[z, y, x, :, pl.ds(pl.multiple_of(core * half, 128), half)],
            put_sem.at[index],
        )
        put.start()
        puts.append((index, put))

    def columns(member, start, size, side):
        return pl.ds(pl.multiple_of(side * halves[member] + start, 128), size)

    sent_all = []

    def z_start(i):
        layer, member, start, size, order = items[i]
        ready(layer, member)
        for steps in range(1, sizes[0]):
            copy = remote(
                blocks[member].at[layer, :, pl.ds(start, size)],
                full(layer, member).at[z, y, x, :, columns(member, start, size, core)],
                z_send.at[i, steps - 1],
                z_recv.at[i, steps - 1],
                device_at(moved(spot, 0, sizes[0], steps), core),
            )
            copy.start()
            sent_all.append(copy)

    def z_wait(i):
        layer, member, start, size, order = items[i]
        for steps in range(1, sizes[0]):
            origin = lax.rem(z + sizes[0] - steps, sizes[0])
            land = full(layer, member).at[origin, y, x, :, columns(member, start, size, core)]
            remote(land, land, z_send.at[i, steps - 1], z_recv.at[i, steps - 1], partner).wait_recv()

    put_done = set()

    def own_put(layer, member):
        index = layer * members + member
        if index not in put_done:
            put_done.add(index)
            dict(puts)[index].wait()

    def region(i, first_index, second_index, side):
        layer, member, start, size, order = items[i]
        cols = columns(member, start, size, side)
        if order == 0:
            return full(layer, member).at[:, second_index, first_index, :, cols]
        return full(layer, member).at[:, first_index, second_index, :, cols]

    def line(i, second_index, side):
        layer, member, start, size, order = items[i]
        cols = columns(member, start, size, side)
        if order == 0:
            return full(layer, member).at[:, second_index, :, :, cols]
        return full(layer, member).at[:, :, second_index, :, cols]

    def axes(i):
        return (2, 1) if items[i][4] == 0 else (1, 2)

    def a_start(i):
        layer, member = items[i][:2]
        own_put(layer, member)
        first, second = axes(i)
        for steps in range(1, sizes[first]):
            mine = region(i, spot[first], spot[second], core)
            copy = remote(
                mine, mine, a_send.at[i, steps - 1], a_recv.at[i, steps - 1],
                device_at(moved(spot, first, sizes[first], steps), core),
            )
            copy.start()
            sent_all.append(copy)

    def a_wait(i):
        first, second = axes(i)
        for steps in range(1, sizes[first]):
            origin = lax.rem(spot[first] + sizes[first] - steps, sizes[first])
            land = region(i, origin, spot[second], core)
            remote(land, land, a_send.at[i, steps - 1], a_recv.at[i, steps - 1], partner).wait_recv()

    def b_start(i):
        first, second = axes(i)
        mine = line(i, spot[second], core)
        for steps in range(1, sizes[second]):
            copy = remote(
                mine, mine, b_send.at[i, steps - 1], b_recv.at[i, steps - 1],
                device_at(moved(spot, second, sizes[second], steps), core),
            )
            copy.start()
            sent_all.append(copy)
        copy = remote(mine, mine, c_send.at[i, 0], c_recv.at[i, 0], partner)
        copy.start()
        sent_all.append(copy)

    def b_wait(i):
        first, second = axes(i)
        for steps in range(1, sizes[second]):
            origin = lax.rem(spot[second] + sizes[second] - steps, sizes[second])
            land = line(i, origin, core)
            remote(land, land, b_send.at[i, steps - 1], b_recv.at[i, steps - 1], partner).wait_recv()
            copy = remote(land, land, c_send.at[i, steps], c_recv.at[i, steps], partner)
            copy.start()
            sent_all.append(copy)

    def c_wait(i):
        first, second = axes(i)
        for steps in range(sizes[second]):
            origin = lax.rem(spot[second] + sizes[second] - steps, sizes[second])
            land = line(i, origin, 1 - core)
            remote(land, land, c_send.at[i, steps], c_recv.at[i, steps], partner).wait_recv()

    total = len(items)
    ahead, lag_b, lag_c = 4, 2, 4
    for i in range(min(ahead, total)):
        z_start(i)
    for i in range(total + lag_c):
        if i < total:
            z_wait(i)
            if i + ahead < total:
                z_start(i + ahead)
            a_start(i)
        if 0 <= i - lag_b < total:
            a_wait(i - lag_b)
            b_start(i - lag_b)
        if 0 <= i - lag_c < total:
            b_wait(i - lag_c)
    for i in range(total):
        c_wait(i)
    for sent, _ in pre:
        sent.wait_send()
    for copy in sent_all:
        copy.wait_send()


def gather_weights(shards, halves, ways, number, items):
    layers = shards[0].shape[0]
    rows = [s.shape[1] for s in shards]
    members = len(shards)
    sizes = (ways[0] // 2, 2, ways[1] // 2)
    count = layers * members
    n = len(items)
    sem = pltpu.SemaphoreType.DMA
    out = pl.pallas_call(
        functools.partial(gather_kernel, ways, rows, halves, items, layers),
        out_shape=[
            jax.ShapeDtypeStruct(sizes + (2 * rows[m], 2 * halves[m]), jnp.bfloat16)
            for _ in range(layers)
            for m in range(members)
        ],
        in_specs=[pl.BlockSpec(memory_space=pl.ANY)] * members,
        out_specs=[pl.BlockSpec(memory_space=pl.ANY)] * count,
        scratch_shapes=[pltpu.VMEM((layers, 2 * rows[m], halves[m]), jnp.float32) for m in range(members)]
        + [pltpu.VMEM((layers, 2 * rows[m], halves[m]), jnp.bfloat16) for m in range(members)]
        + [sem((count,))] * 4
        + [sem((n, sizes[0]))] * 2
        + [sem((n, max(sizes)))] * 6,
        compiler_params=pltpu.CompilerParams(
            collective_id=number, has_side_effects=True, vmem_limit_bytes=VMEM_LIMIT
        ),
    )(*shards)
    return [
        [out[l * members + m].reshape(-1, 2 * halves[m]) for m in range(members)] for l in range(layers)
    ]


def plan(halves, layers):
    items = []
    for layer in range(layers):
        flip = layer % 2
        for member, width in enumerate(halves):
            size = width // 4 if width % 512 == 0 else (width // 2 if width % 256 == 0 else 128)
            for start in range(0, width, size):
                items.append((layer, member, start, size, (len(items) + 0) % 2))
    return items


def scatter_kernel(ways, rows, halves, items, layers, *refs):
    members = len(rows)
    n = len(items)
    grads = refs[: members * layers]
    outs = refs[members * layers : members * layers + members]
    rest = list(refs[members * layers + members :])

    def take(count):
        taken = rest[:count]
        del rest[:count]
        return taken

    locals_ = take(members)
    whole, part_a, part_b, part_z, sums = (take(n) for _ in range(5))
    l_sem, c_send, c_recv, a_send, a_recv, b_send, b_recv, z_send, z_recv, e_send, e_recv, o_sem = rest
    sizes, spot, core = place(ways)
    z, y, x = spot
    partner = device_at(spot, 1 - core)
    greet_peers(sizes, spot, core)
    sent_all = []
    seen = {}
    slots = []
    for layer, member, *_ in items:
        slots.append(seen.get(member, 0) % 2)
        seen[member] = seen.get(member, 0) + 1

    def columns(i, side):
        _, member, start, size, _ = items[i]
        return pl.ds(pl.multiple_of(side * halves[member] + start, 128), size)

    def grad(i):
        return grads[items[i][0] * members + items[i][1]]

    def local(i):
        return locals_[items[i][1]].at[slots[i]]

    def axes(i):
        return (2, 1) if items[i][4] == 0 else (1, 2)

    def l_copy(i):
        return pltpu.make_async_copy(grad(i).at[:, :, :, :, columns(i, core)], local(i), l_sem.at[i])

    def c_copy(i):
        return remote(
            grad(i).at[:, :, :, :, columns(i, 1 - core)], whole[i], c_send.at[i], c_recv.at[i], partner
        )

    def line(i, second_index):
        if items[i][4] == 0:
            return whole[i].at[:, second_index]
        return whole[i].at[:, :, second_index]

    def send(copy):
        copy.start()
        sent_all.append(copy)

    def add_local(i):
        kept = local(i)

        @pl.loop(0, sizes[0])
        def _(index):
            whole[i][index] = (
                whole[i][index].astype(jnp.float32) + kept[index].astype(jnp.float32)
            ).astype(jnp.bfloat16)

    def a_start(i):
        first, second = axes(i)
        for steps in range(1, sizes[second]):
            target = moved(spot, second, sizes[second], steps)
            send(
                remote(
                    line(i, target[second]), part_a[i].at[steps - 1],
                    a_send.at[i, steps - 1], a_recv.at[i, steps - 1], device_at(target, core),
                )
            )

    def a_finish(i):
        first, second = axes(i)
        for steps in range(1, sizes[second]):
            land = part_a[i].at[steps - 1]
            remote(land, land, a_send.at[i, steps - 1], a_recv.at[i, steps - 1], partner).wait_recv()
        mine = line(i, spot[second])

        @pl.loop(0, sizes[0])
        def _(index):
            total = mine[index].astype(jnp.float32)
            for steps in range(1, sizes[second]):
                total = total + part_a[i][steps - 1, index].astype(jnp.float32)
            mine[index] = total.astype(jnp.bfloat16)

    def b_start(i):
        first, second = axes(i)
        for steps in range(1, sizes[first]):
            target = moved(spot, first, sizes[first], steps)
            send(
                remote(
                    whole[i].at[:, target[1], target[2]], part_b[i].at[steps - 1],
                    b_send.at[i, steps - 1], b_recv.at[i, steps - 1], device_at(target, core),
                )
            )

    def b_finish(i):
        first, second = axes(i)
        for steps in range(1, sizes[first]):
            land = part_b[i].at[steps - 1]
            remote(land, land, b_send.at[i, steps - 1], b_recv.at[i, steps - 1], partner).wait_recv()
        mine = whole[i].at[:, y, x]

        @pl.loop(0, sizes[0])
        def _(index):
            total = mine[index].astype(jnp.float32)
            for steps in range(1, sizes[first]):
                total = total + part_b[i][steps - 1, index].astype(jnp.float32)
            mine[index] = total.astype(jnp.bfloat16)

    def z_start(i):
        for steps in range(1, sizes[0]):
            target = moved(spot, 0, sizes[0], steps)
            send(
                remote(
                    whole[i].at[target[0], y, x], part_z[i].at[steps - 1],
                    z_send.at[i, steps - 1], z_recv.at[i, steps - 1], device_at(target, core),
                )
            )

    def owned(i, side):
        layer, member = items[i][:2]
        height = rows[member]
        return sums[i].at[pl.ds(pl.multiple_of(side * height, 8), height)]

    def e_copy(i):
        layer, member = items[i][:2]
        return remote(
            owned(i, 1 - core), outs[member].at[layer, :, columns(i, core)],
            e_send.at[i], e_recv.at[i], partner,
        )

    def o_copy(i):
        layer, member = items[i][:2]
        return pltpu.make_async_copy(
            owned(i, core), outs[member].at[layer, :, columns(i, core)], o_sem.at[i]
        )

    def z_finish(i):
        for steps in range(1, sizes[0]):
            land = part_z[i].at[steps - 1]
            remote(land, land, z_send.at[i, steps - 1], z_recv.at[i, steps - 1], partner).wait_recv()
        total = whole[i][z, y, x].astype(jnp.float32)
        for steps in range(1, sizes[0]):
            total = total + part_z[i][steps - 1].astype(jnp.float32)
        sums[i][...] = total
        e_copy(i).start()
        o_copy(i).start()

    ahead = 3
    lag_a, lag_b, lag_z = 2, 4, 6
    for i in range(min(2, n)):
        l_copy(i).start()
    for i in range(min(ahead, n)):
        send(c_copy(i))
    for i in range(n + lag_z):
        if i < n:
            c_copy(i).wait_recv()
            l_copy(i).wait()
            add_local(i)
            a_start(i)
            if i + 2 < n:
                l_copy(i + 2).start()
            if i + ahead < n:
                send(c_copy(i + ahead))
        if 0 <= i - lag_a < n:
            a_finish(i - lag_a)
            b_start(i - lag_a)
        if 0 <= i - lag_b < n:
            b_finish(i - lag_b)
            z_start(i - lag_b)
        if 0 <= i - lag_z < n:
            z_finish(i - lag_z)
    for i in range(n):
        e_copy(i).wait()
        o_copy(i).wait()
    for copy in sent_all:
        copy.wait_send()


def scatter_grads(grads, rows, halves, ways, number, items):
    layers, members = len(grads), len(rows)
    sizes = (ways[0] // 2, 2, ways[1] // 2)
    n = len(items)
    sem = pltpu.SemaphoreType.DMA
    low = jnp.bfloat16

    def axis_sizes(order):
        return (sizes[2], sizes[1]) if order == 0 else (sizes[1], sizes[2])

    most = [max(s for _, m, _, s, _ in items if m == member) for member in range(members)]
    scratch = [pltpu.VMEM((2,) + sizes + (2 * rows[m], most[m]), low) for m in range(members)]
    scratch += [pltpu.VMEM(sizes + (2 * rows[m], s), low) for _, m, _, s, _ in items]
    scratch += [
        pltpu.VMEM((axis_sizes(o)[1] - 1, sizes[0], axis_sizes(o)[0], 2 * rows[m], s), low)
        for _, m, _, s, o in items
    ]
    scratch += [
        pltpu.VMEM((axis_sizes(o)[0] - 1, sizes[0], 2 * rows[m], s), low) for _, m, _, s, o in items
    ]
    scratch += [pltpu.VMEM((sizes[0] - 1, 2 * rows[m], s), low) for _, m, _, s, _ in items]
    scratch += [pltpu.VMEM((2 * rows[m], s), jnp.float32) for _, m, _, s, _ in items]
    scratch += [sem((n,))] * 3 + [sem((n, max(sizes)))] * 6 + [sem((n,))] * 3
    flat = [
        grads[l][m].reshape(sizes + (2 * rows[m], 2 * halves[m]))
        for l in range(layers)
        for m in range(members)
    ]
    return pl.pallas_call(
        functools.partial(scatter_kernel, ways, rows, halves, items, layers),
        out_shape=[
            jax.ShapeDtypeStruct((layers, rows[m], 2 * halves[m]), jnp.float32) for m in range(members)
        ],
        in_specs=[pl.BlockSpec(memory_space=pl.ANY)] * len(flat),
        out_specs=[pl.BlockSpec(memory_space=pl.ANY)] * members,
        scratch_shapes=scratch,
        compiler_params=pltpu.CompilerParams(
            collective_id=number, has_side_effects=True, vmem_limit_bytes=VMEM_LIMIT
        ),
    )(*flat)


def to_low(values):
    return values.astype(jnp.bfloat16)


def norm_rows(values):
    centred = values - jnp.mean(values, -1, keepdims=True)
    return centred * lax.rsqrt(jnp.mean(centred * centred, -1, keepdims=True) + EPSILON)


def modulate(stream, shift, scale_part):
    return norm_rows(stream) * (1.0 + scale_part) + shift


def gained_norm(stream, gain):
    return norm_rows(stream) * gain


def dense(left, right):
    return jnp.dot(left, right, preferred_element_type=jnp.float32)


def dense_back(left, right):
    return lax.dot_general(left, right, (((1,), (1,)), ((), ())), preferred_element_type=jnp.float32)


def weight_grad(left, right):
    return lax.dot_general(left, right, (((0,), (0,)), ((), ())), preferred_element_type=jnp.float32)


def split_heads(values):
    return values.reshape(values.shape[0], HEADS, HEAD_DIM)


def attention(queries, keys, values, keep):
    scores = jnp.einsum(
        "qhd,khd->hqk", split_heads(queries), split_heads(keys), preferred_element_type=jnp.float32
    ) * HEAD_DIM ** (-0.5)
    scores = jnp.where(keep[None, None, :], scores, NEGATIVE)
    shifted = jnp.exp(scores - jnp.max(scores, -1, keepdims=True))
    probs = shifted / jnp.sum(shifted, -1, keepdims=True)
    mixed = jnp.einsum(
        "hqk,khd->qhd", to_low(probs), split_heads(values), preferred_element_type=jnp.float32
    )
    return (to_low(mixed.reshape(queries.shape)), probs)


def attention_back(queries, keys, values, probs, grad_mixed):
    grad_heads = split_heads(to_low(grad_mixed))
    grad_values = jnp.einsum(
        "hqk,qhd->khd", to_low(probs), grad_heads, preferred_element_type=jnp.float32
    )
    grad_probs = jnp.einsum(
        "qhd,khd->hqk", grad_heads, split_heads(values), preferred_element_type=jnp.float32
    )
    grad_scores = to_low(probs * (grad_probs - jnp.sum(probs * grad_probs, -1, keepdims=True)))
    grad_queries = jnp.einsum(
        "hqk,khd->qhd", grad_scores, split_heads(keys), preferred_element_type=jnp.float32
    ) * HEAD_DIM ** (-0.5)
    grad_keys = jnp.einsum(
        "hqk,qhd->khd", grad_scores, split_heads(queries), preferred_element_type=jnp.float32
    ) * HEAD_DIM ** (-0.5)
    return (
        grad_queries.reshape(queries.shape),
        grad_keys.reshape(keys.shape),
        grad_values.reshape(values.shape),
    )


def noise_level(steps):
    phase = (steps.astype(jnp.float32) / 1000.0 + 0.008) / 1.008 * (math.pi / 2)
    return jnp.cos(phase) ** 2


def time_features(steps):
    half_width = FREQS // 2
    frequency = jnp.exp(-math.log(10000.0) * jnp.arange(half_width, dtype=jnp.float32) / half_width)
    angles = steps.astype(jnp.float32)[:, None] * frequency[None, :]
    return jnp.concatenate([jnp.cos(angles), jnp.sin(angles)], -1)


def layer_forward(stream, modulation, text_low, frame_keep, text_keep, weights):
    w_joint, w_textkv, w_back, gain = weights
    normed_one, pull_one = jax.vjp(modulate, stream, modulation[:D], modulation[D : 2 * D])
    input_one = to_low(normed_one)
    self_proj = to_low(dense(input_one, w_joint[:, : 3 * D]))
    mixed_one, probs_one = attention(
        self_proj[:, :D], self_proj[:, D : 2 * D], self_proj[:, 2 * D :], frame_keep
    )
    branch_one = dense(mixed_one, w_back[:D])
    stream_two = stream + modulation[2 * D : 3 * D] * branch_one
    normed_two, pull_two = jax.vjp(gained_norm, stream_two, gain)
    input_two = to_low(normed_two)
    cross_query = to_low(dense(input_two, w_joint[:, 3 * D : 4 * D]))
    cross_kv = to_low(dense(text_low, w_textkv))
    mixed_two, probs_two = attention(cross_query, cross_kv[:, :D], cross_kv[:, D:], text_keep)
    stream_three = stream_two + dense(mixed_two, w_back[D : 2 * D])
    normed_three, pull_three = jax.vjp(
        modulate, stream_three, modulation[3 * D : 4 * D], modulation[4 * D : 5 * D]
    )
    input_three = to_low(normed_three)
    hidden_act, pull_act = jax.vjp(jax.nn.gelu, dense(input_three, w_joint[:, 4 * D :]))
    hidden_low = to_low(hidden_act)
    branch_three = dense(hidden_low, w_back[2 * D :])
    result = stream_three + modulation[5 * D :] * branch_three
    saved = (
        pull_one,
        input_one,
        self_proj,
        mixed_one,
        probs_one,
        branch_one,
        pull_two,
        input_two,
        cross_query,
        cross_kv,
        mixed_two,
        probs_two,
        pull_three,
        input_three,
        pull_act,
        hidden_low,
        branch_three,
    )
    return (result, saved)


def layer_backward(saved, grad_out, modulation, text_low, weights):
    w_joint, w_textkv, w_back, gain = weights
    (
        pull_one,
        input_one,
        self_proj,
        mixed_one,
        probs_one,
        branch_one,
        pull_two,
        input_two,
        cross_query,
        cross_kv,
        mixed_two,
        probs_two,
        pull_three,
        input_three,
        pull_act,
        hidden_low,
        branch_three,
    ) = saved
    grad_three = to_low(grad_out * modulation[5 * D :])
    grad_gate_two = jnp.sum(grad_out * branch_three, 0)
    grad_down = weight_grad(hidden_low, grad_three)
    (grad_pre,) = pull_act(dense_back(grad_three, w_back[2 * D :]))
    grad_pre = to_low(grad_pre)
    grad_up = weight_grad(input_three, grad_pre)
    grad_inner, grad_shift_two, grad_scale_two = pull_three(dense_back(grad_pre, w_joint[:, 4 * D :]))
    grad_stream = grad_out + grad_inner
    grad_cross_out = to_low(grad_stream)
    grad_co = weight_grad(mixed_two, grad_cross_out)
    grad_cq, grad_ck, grad_cv = attention_back(
        cross_query,
        cross_kv[:, :D],
        cross_kv[:, D:],
        probs_two,
        dense_back(grad_cross_out, w_back[D : 2 * D]),
    )
    grad_cq = to_low(grad_cq)
    grad_text_w = weight_grad(text_low, to_low(jnp.concatenate([grad_ck, grad_cv], -1)))
    grad_query_w = weight_grad(input_two, grad_cq)
    grad_inner, grad_gain = pull_two(dense_back(grad_cq, w_joint[:, 3 * D : 4 * D]))
    grad_stream = grad_stream + grad_inner
    grad_one = to_low(grad_stream * modulation[2 * D : 3 * D])
    grad_gate_one = jnp.sum(grad_stream * branch_one, 0)
    grad_ao = weight_grad(mixed_one, grad_one)
    grad_q, grad_k, grad_v = attention_back(
        self_proj[:, :D],
        self_proj[:, D : 2 * D],
        self_proj[:, 2 * D :],
        probs_one,
        dense_back(grad_one, w_back[:D]),
    )
    grad_self = to_low(jnp.concatenate([grad_q, grad_k, grad_v], -1))
    grad_self_w = weight_grad(input_one, grad_self)
    grad_inner, grad_shift_one, grad_scale_one = pull_one(dense_back(grad_self, w_joint[:, : 3 * D]))
    grad_stream = grad_stream + grad_inner
    grad_mod = jnp.concatenate(
        [grad_shift_one, grad_scale_one, grad_gate_one, grad_shift_two, grad_scale_two, grad_gate_two]
    )
    grads = (
        to_low(jnp.concatenate([grad_self_w, grad_query_w, grad_up], 1)),
        to_low(grad_text_w),
        to_low(jnp.concatenate([grad_ao, grad_co, grad_down], 0)),
    )
    return (grad_stream, grad_mod, grads, grad_gain)


def adam_update(weight, grad, first, second, rate):
    first_new = BETA_ONE * first + (1.0 - BETA_ONE) * grad
    second_new = BETA_TWO * second + (1.0 - BETA_TWO) * grad * grad
    first_hat = first_new / (1.0 - BETA_ONE**STEP)
    second_hat = second_new / (1.0 - BETA_TWO**STEP)
    weight_new = weight - rate * (
        first_hat / (jnp.sqrt(second_hat) + ADAM_EPSILON) + WEIGHT_DECAY * weight
    )
    return (first_new, second_new, weight_new)


def tiles(values, lead=()):
    flat = values.reshape(lead + (-1,))
    short = -flat.shape[-1] % 1024
    flat = jnp.pad(flat, [(0, 0)] * len(lead) + [(0, short)])
    return flat.reshape(lead + (-1, 128))


def body(
    ways,
    clean_latent,
    noise,
    text_feats,
    text_lengths,
    timesteps,
    valid_frames,
    w_in,
    w_text,
    w_out,
    gains,
    w_lead,
    w_head,
    first_in,
    second_in,
    first_text,
    second_text,
    first_out,
    second_out,
    first_gains,
    second_gains,
    first_lead,
    second_lead,
    first_head,
    second_head,
):
    count = ways[0] * ways[1]
    own = w_head.shape[0]
    channels = noise.shape[-1]
    clean_latent, noise, text_low = clean_latent[0], noise[0], text_feats[0]
    frames, caption = clean_latent.shape[0], text_low.shape[0]
    frame_keep = lax.iota(jnp.int32, frames) < valid_frames[0]
    text_keep = lax.iota(jnp.int32, caption) < text_lengths[0]
    rows = [w_in.shape[1], w_text.shape[1], w_out.shape[1]]
    halves = [JOINT // 2, D, D // 2]
    aligned = all(height % 8 == 0 for height in rows) and ways[0] % 2 == 0 and ways[1] % 2 == 0
    items = plan(halves, LAYERS)

    def to_all(values, number):
        if aligned:
            return exchange(values, ways, True, number)
        return lax.all_gather(values, ALL, axis=0, tiled=False)

    def to_each(values, number):
        if aligned:
            return exchange(values, ways, False, number)
        return lax.all_to_all(values, ALL, 0, 0, tiled=True)

    sinus = time_features(timesteps)
    lead_low, head_low = to_low(w_lead), to_low(w_head)
    small = jnp.concatenate(
        [
            lead_low[FREQS:].astype(jnp.float32).reshape(-1),
            head_low[:, 3 * D :].astype(jnp.float32).reshape(-1),
            to_low(gains).astype(jnp.float32).reshape(-1),
        ]
    )
    facts = jnp.concatenate([to_low(sinus).astype(jnp.float32)[0], valid_frames.astype(jnp.float32)])
    packed = to_all(jnp.concatenate([tiles(facts), tiles(small)], 0), 3).reshape(count, -1)
    facts_size = 1024
    sinus_all = to_low(packed[:, :FREQS])
    frame_count = jnp.sum(packed[:, FREQS])
    small_all = packed[:, facts_size:]
    at = channels * own
    lead_in = to_low(small_all[:, :at].reshape(count, channels, own).transpose(1, 0, 2).reshape(channels, D))
    head_pred = to_low(small_all[:, at : 2 * at].reshape(D, channels))
    gains_all = small_all[:, 2 * at : 2 * at + LAYERS * own].reshape(count, LAYERS, own)
    gains_all = gains_all.transpose(1, 0, 2).reshape(LAYERS, D)

    act_time, pull_time = jax.vjp(jax.nn.silu, dense(sinus_all, lead_low[:FREQS]))
    act_low = to_low(act_time)
    temb_part = dense(act_low, head_low[:, :D]).reshape(count, count, own).transpose(1, 0, 2)
    temb = jnp.sum(to_each(tiles(temb_part, (count,)), 4), 0).reshape(-1)[:D].reshape(count, own)
    cond, pull_cond = jax.vjp(jax.nn.silu, temb)
    cond_low = to_low(cond)
    mod_low = jnp.concatenate(
        [to_low(w_in[layer, :, JOINT:]) for layer in range(LAYERS)] + [head_low[:, D : 3 * D]], 1
    )
    mod_part = dense(cond_low, mod_low)
    mods = jnp.sum(to_each(tiles(mod_part, (count,)), 5), 0).reshape(-1)[: mod_low.shape[1]]

    if aligned:
        weights = gather_weights([w_in, w_text, w_out], halves, ways, 1, items)
    else:
        weights = [
            [
                lax.all_gather(to_low(shard[layer]), ALL, axis=0, tiled=True)
                for shard in (w_in[:, :, :JOINT], w_text, w_out)
            ]
            for layer in range(LAYERS)
        ]

    level = noise_level(timesteps)
    noisy_low = to_low(jnp.sqrt(level) * clean_latent + jnp.sqrt(1.0 - level) * noise)
    stream = dense(noisy_low, lead_in)
    saved = []
    for layer in range(LAYERS):
        stream, kept = layer_forward(
            stream,
            mods[layer * MOD : (layer + 1) * MOD],
            text_low,
            frame_keep,
            text_keep,
            (*weights[layer], gains_all[layer]),
        )
        saved.append(kept)
    final_mod = mods[LAYERS * MOD :]
    normed_final, pull_final = jax.vjp(modulate, stream, final_mod[:D], final_mod[D:])
    final_low = to_low(normed_final)
    error = dense(final_low, head_pred) - noise
    loss_part = jnp.sum(jnp.where(frame_keep[:, None], error * error, 0.0))
    grad_pred = to_low(jnp.where(frame_keep[:, None], error * (2.0 / frame_count), 0.0))
    grad_pred_w = weight_grad(final_low, grad_pred)
    grad_stream, grad_shift_f, grad_scale_f = pull_final(dense_back(grad_pred, head_pred))
    grad_mods = [None] * LAYERS + [jnp.concatenate([grad_shift_f, grad_scale_f])]
    big = [None] * LAYERS
    grad_gains = [None] * LAYERS
    for layer in reversed(range(LAYERS)):
        grad_stream, grad_mods[layer], big[layer], grad_gains[layer] = layer_backward(
            saved[layer],
            grad_stream,
            mods[layer * MOD : (layer + 1) * MOD],
            text_low,
            (*weights[layer], gains_all[layer]),
        )
    grad_in_w = weight_grad(noisy_low, to_low(grad_stream))

    mods_all = to_all(tiles(to_low(jnp.concatenate(grad_mods)).astype(jnp.float32)), 6)
    mods_all = to_low(mods_all.reshape(count, -1)[:, : mod_low.shape[1]])
    grad_mod_w = weight_grad(cond_low, mods_all)
    (grad_temb,) = pull_cond(dense_back(mods_all, mod_low))
    small_grads = jnp.concatenate(
        [
            grad_in_w.reshape(channels, count, own).transpose(1, 0, 2).reshape(count, -1),
            grad_pred_w.reshape(count, -1),
            jnp.stack(grad_gains).reshape(LAYERS, count, own).transpose(1, 0, 2).reshape(count, -1),
        ],
        1,
    )
    temb_tile = tiles(to_low(grad_temb).astype(jnp.float32))
    sent = jnp.concatenate(
        [jnp.broadcast_to(temb_tile[None], (count,) + temb_tile.shape), tiles(small_grads, (count,))], 1
    )
    got = to_each(sent, 7).reshape(count, -1)
    temb_all = to_low(got[:, :D].reshape(count, count, own).transpose(1, 0, 2).reshape(count, D))
    small_sum = jnp.sum(got[:, temb_tile.size :], 0)
    grad_time_two = weight_grad(act_low, temb_all)
    (grad_pre_time,) = pull_time(dense_back(temb_all, head_low[:, :D]))
    grad_time_one = weight_grad(sinus_all, to_low(grad_pre_time))

    if aligned:
        sums = scatter_grads(big, rows, halves, ways, 2, items)
    else:
        sums = [
            jnp.stack(
                [
                    lax.psum_scatter(big[layer][member], ALL, scatter_dimension=0, tiled=True)
                    for layer in range(LAYERS)
                ]
            ).astype(jnp.float32)
            for member in range(3)
        ]
    mod_grads = grad_mod_w[:, : LAYERS * MOD].reshape(own, LAYERS, MOD).transpose(1, 0, 2)
    grad_list = [
        jnp.concatenate([sums[0], mod_grads], 2),
        sums[1],
        sums[2],
        small_sum[2 * at : 2 * at + LAYERS * own].reshape(LAYERS, own),
        jnp.concatenate([grad_time_one, small_sum[:at].reshape(channels, own)], 0),
        jnp.concatenate(
            [grad_time_two, grad_mod_w[:, LAYERS * MOD :], small_sum[at : 2 * at].reshape(own, channels)], 1
        ),
    ]
    local_squares = sum((jnp.sum(item * item) for item in grad_list))
    totals = jnp.sum(to_all(tiles(jnp.stack([loss_part, local_squares])), 8), 0).reshape(-1)
    loss_sum = totals[0]
    grad_norm = jnp.sqrt(totals[1])
    factor = CLIP_NORM / jnp.maximum(grad_norm, CLIP_NORM)
    params = (w_in, w_text, w_out, gains, w_lead, w_head)
    firsts = (first_in, first_text, first_out, first_gains, first_lead, first_head)
    seconds = (second_in, second_text, second_out, second_gains, second_lead, second_head)
    rates = (LEARN_RATE, LEARN_RATE, LEARN_RATE, GAIN_RATE, LEARN_RATE, LEARN_RATE)
    results = []
    for weight, grad, first, second, rate in zip(params, grad_list, firsts, seconds, rates):
        results.extend(adam_update(weight, grad * factor, first, second, rate))
    return (loss_sum, frame_count, grad_norm, *results)


def solution(mesh):
    ways = (mesh.shape["dp"], mesh.shape["fsdp"])
    clips = [P(ALL, None, None)] * 3 + [P(ALL)] * 3
    weights = [P(None, ALL, None)] * 3 + [P(None, ALL)] * 2 + [P(ALL, None)]
    moments = [spec for spec in weights for _ in range(2)]
    results = [spec for spec in weights for _ in range(3)]
    return jax.shard_map(
        functools.partial(body, ways),
        mesh=mesh,
        in_specs=tuple(clips + weights + moments),
        out_specs=tuple([P()] * 3 + results),
        check_vma=False,
    )
```

time: 2870 us -> 870 us (0.30)
  waiting for transfers between devices: 1980 us -> 0 us
  Pallas kernels: 0 us -> 515 us
  local copies, waits for them, and re-layouts: 338 us -> 60.1 us
  blocking collectives: 163 us -> 0 us
  other arithmetic: 123 us -> 76.3 us
  matrix products: 226 us -> 193 us
    unnamed x10 -> x0, waiting for transfers between devices: 1640 us -> none
    pallas_call x0 -> x8, Pallas kernels: none -> 515 us  [the longest x1 200 us: gather_weights(): pl.pallas_call(functools.partial(gather_kernel, ways, rows, halves, items...]
    all_gather x6 -> x0, waiting for transfers between devices: 342 us -> none  [gather_layer(): lax.all_gather(for_sending(flats), ('dp', 'fsdp'), axis=0, tiled=True)]
    reshape x16 -> x15, local copies, waits for them, and re-layouts: 200 us -> 1.89 us  [the longest x2 0.39 us: tiles(): flat = values.reshape(lead + (-1,))]
    unnamed x2 -> x0, blocking collectives: 82.9 us -> none
    psum x2 -> x0, blocking collectives: 80.3 us -> none  [the longest x1 40.5 us: body(): lax.psum(jnp.sum(valid_frames).astype(jnp.float32), ('dp', 'fsdp'))]
    dot_general x38 -> x19, matrix products: 109 us -> 47 us  [dense(): return jnp.dot(left, right, preferred_element_type=jnp.float32)]
    slice x27 -> x25, local copies, waits for them, and re-layouts: 65.6 us -> 12.3 us  [the longest x4 6.02 us: layer_forward(): self_proj[:, D:2 * D]]
  transfers between devices with their start and end apart: 8 -> 0, of which waited for: 8 -> 0; matrix products, arithmetic and copies ran while one was open for 6% -> 0% of each run, Pallas kernels for 0% -> 0%
where the time goes in v1:
time: 870 us; the launch traced here: 859 us
  Pallas kernels  515 us (59%)
  matrix products  193 us (22%)
  other arithmetic  76.3 us (9%)
  local copies, waits for them, and re-layouts  60.1 us (7%)
  between operations  13.8 us (2%)
    pallas_call x1, Pallas kernels, gather_weights(): pl.pallas_call(functools.partial(gather_kernel, ways, rows, halves, items...  200 us
    pallas_call x1, Pallas kernels, scatter_grads(): pl.pallas_call(functools.partial(scatter_kernel, ways, rows, halves, item...  189 us
    pallas_call x6, Pallas kernels, exchange(): pl.pallas_call(functools.partial(exchange_kernel, ways, shared), out_shap...  126 us
    dot_general x19, matrix products, dense(): return jnp.dot(left, right, preferred_element_type=jnp.float32)  47 us
    dot_general x14, matrix products, dense_back(): lax.dot_general(left, right, (((1,), (1,)), ((), ())), preferred_element_...  45.1 us
    dot_general x19, matrix products, weight_grad(): lax.dot_general(left, right, (((0,), (0,)), ((), ())), preferred_element_...  43.5 us
    unnamed x621, local copies, waits for them, and re-layouts  26.9 us
    sub x4, matrix products, attention(): shifted = jnp.exp(scores - jnp.max(scores, -1, keepdims=True))  17.8 us

profile of v1, /device:TPU:0, one launch (start us, length us, event | category | flops | bytes accessed | tf_op | source)
XLA Modules:
  0.0 858.5 jit_solution(16559934408482136589)
XLA Ops:
  5.6 13.7 %shard_map.391 = f32[32,16,128]{2,1,0:T(8,128)} custom-call(f32[16,128]{1,0:T(8,128)} %pad_maximum_fusion.19.x_ref), custom_call_target="tpu_custom_call" | custom-call | tf_op jit(solution)/shard_map/pallas_call | solution.py:121
  24.7 11.7 %shard_map.392 = f32[32,8,128]{2,1,0:T(8,128)} custom-call(f32[32,8,128]{2,1,0:T(8,128)} %bitcast.419), custom_call_target="tpu_custom_call" | custom-call | tf_op jit(solution)/shard_map/pallas_call | solution.py:121
  41.9 32.5 %shard_map.393 = f32[32,88,128]{2,1,0:T(8,128)} custom-call(f32[32,88,128]{2,1,0:T(8,128)} %bitcast.331), custom_call_target="tpu_custom_call" | custom-call | tf_op jit(solution)/shard_map/pallas_call | solution.py:121
  76.5 199.6 %shard_map.394 = (bf16[4,2,2,48,6144]{4,3,2,1,0:T(8,128)(2,1)}, bf16[4,2,2,64,1536]{4,3,2,1,0:T(8,128)(2,1)}, bf16[4,2,2,288,768]{4,3,2,1,0:T(8,128)(2,1)}, bf16...) custom-call(f32[2,24,10752]{2,1,0:T(8,128)} %refs_0_.1, ...), custom_call_target="tpu_custom_call" | custom-call | tf_op jit(solution)/shard_map/pallas_call | solution.py:318
  282.4 5.3 fusion.258
  312.9 4.3 fusion.20
  329.4 6.1 fusion.261
  362.5 4.3 fusion.12
  366.9 3.8 fusion.245
  380.6 7.5 fusion.35
  397.8 4.1 multiply_reduce_fusion.3
  415.1 4.0 multiply_reduce_fusion.1
  424.3 5.1 multiply_reduce_fusion.12
  432.3 4.0 fusion.28
  443.9 4.1 multiply_reduce_fusion.2
  461.3 4.1 multiply_reduce_fusion
  471.1 4.0 multiply_reduce_fusion.7
  476.5 3.9 fusion.114
  490.7 36.5 %shard_map.396 = f32[32,88,128]{2,1,0:T(8,128)} custom-call(f32[88,128]{1,0:T(8,128)} %bitcast_convert_fusion.x_ref), custom_call_target="tpu_custom_call" | custom-call | tf_op jit(solution)/shard_map/pallas_call | solution.py:121
  532.0 21.2 %shard_map.397 = f32[32,16,128]{2,1,0:T(8,128)} custom-call(f32[32,16,128]{2,1,0:T(8,128)} %pad_maximum_fusion.12.x_ref), custom_call_target="tpu_custom_call" | custom-call | tf_op jit(solution)/shard_map/pallas_call | solution.py:121
  564.6 5.2 convolution_convert_fusion.2
  581.3 4.1 convolution_convert_fusion
  588.6 4.9 convolution_convert_fusion.3
  593.6 4.2 pad_maximum_fusion.1.refs_3_
  603.7 3.7 pad_maximum_fusion.2
  613.4 4.1 convolution_convert_fusion.1
  620.7 4.8 convolution_convert_fusion.5
  625.6 4.1 pad_maximum_fusion.refs_0_
  629.6 189.1 %shard_map.395 = (f32[2,24,6144]{2,1,0:T(8,128)}, f32[2,32,1536]{2,1,0:T(8,128)}, f32[2,144,768]{2,1,0:T(8,128)}) custom-call(bf16[4,2,2,48,6144]{4,3,2,1,0:T(8,128)(2,1)} %pad_maximum_fusion.refs_0_, bf16[4,2,2,64,1536]{4,3,2,1,0:T(8,128)(2,1)} %bitcast.324, bf16[4,2,2,288,768]{4,3,2,1,0:T(8,128)(2,1)} %bitcast.322, ...), custom_call_target="tpu_custom_call" | custom-call | tf_op jit(solution)/shard_map/pallas_call | solution.py:565
  829.0 10.8 %shard_map.398 = f32[32,8,128]{2,1,0:T(8,128)} custom-call(f32[8,128]{1,0:T(8,128)} %fusion.188.x_ref), custom_call_target="tpu_custom_call" | custom-call | tf_op jit(solution)/shard_map/pallas_call | solution.py:121
  848.0 4.1 multiply_subtract_fusion.1
  853.4 3.9 multiply_subtract_fusion
  (844 shorter events, 222.3 us)
Async XLA Ops:
  0.7 298.9 %copy-start = (bf16[1,256,1024]{2,1,0:T(8,128)(2,1)S(1)}, bf16[1,256,1024]{2,1,0:T(8,128)(2,1)}, u32[]{:S(2)}) copy-start(bf16[1,256,1024]{2,1,0:T(8,128)(2,1)} %param.26) | copy-start | bytes 1572868
  3.1 36.2 %copy-start.108 = (bf16[24,2324]{1,0:T(8,128)(2,1)}, bf16[24,2324]{1,0:T(8,128)(2,1)S(1)}, u32[]{:S(2)}) copy-start(bf16[24,2324]{1,0:T(8,128)(2,1)S(1)} %convert_element_type.323) | copy-start | bytes 334660
  22.4 270.4 %copy-start.1 = (f32[320,768]{1,0:T(8,128)}, f32[320,768]{1,0:T(8,128)S(1)}, u32[]{:S(2)}) copy-start(f32[320,768]{1,0:T(8,128)S(1)} %get-tuple-element.141) | copy-start | bytes 2949124
  22.4 253.7 %copy-start.151 = (f32[320]{0:T(512)}, f32[320]{0:T(512)S(1)}, u32[]{:S(2)}) copy-start(f32[320]{0:T(512)S(1)} %broadcast_multiply_fusion.6) | copy-start | bytes 3844
  22.6 17.7 %copy-start.197 = (f32[320]{0:T(512)}, f32[320]{0:T(512)S(1)}, u32[]{:S(2)}) copy-start(f32[320]{0:T(512)S(1)} %multiply_reduce_fusion.29) | copy-start | bytes 3844
  22.7 253.4 %copy-start.222 = (f32[320]{0:T(512)}, f32[320]{0:T(512)S(1)}, u32[]{:S(2)}) copy-start(f32[320]{0:T(512)S(1)} %fusion.202) | copy-start | bytes 3844
  22.8 17.6 %copy-start.122 = (f32[32,24]{0,1:T(8,128)}, f32[32,24]{0,1:T(8,128)S(1)}, u32[]{:S(2)}) copy-start(f32[32,24]{0,1:T(8,128)S(1)} %fusion.168) | copy-start | bytes 9220
  76.4 203.1 %copy-start.128 = (f32[768]{0:T(1024)}, f32[768]{0:T(1024)S(1)}, u32[]{:S(2)}) copy-start(f32[768]{0:T(1024)S(1)} %get-tuple-element.132) | copy-start | bytes 9220
  76.4 203.1 %copy-start.253 = (f32[768]{0:T(1024)}, f32[768]{0:T(1024)S(1)}, u32[]{:S(2)}) copy-start(f32[768]{0:T(1024)S(1)} %get-tuple-element.131) | copy-start | bytes 9220
  76.4 216.4 %copy-start.131 = (f32[768]{0:T(1024)}, f32[768]{0:T(1024)S(1)}, u32[]{:S(2)}) copy-start(f32[768]{0:T(1024)S(1)} %get-tuple-element.133) | copy-start | bytes 9220
  76.4 236.4 %copy-start.124 = (f32[768]{0:T(1024)}, f32[768]{0:T(1024)S(1)}, u32[]{:S(2)}) copy-start(f32[768]{0:T(1024)S(1)} %get-tuple-element.129) | copy-start | bytes 9220
  76.4 236.4 %copy-start.251 = (f32[768]{0:T(1024)}, f32[768]{0:T(1024)S(1)}, u32[]{:S(2)}) copy-start(f32[768]{0:T(1024)S(1)} %get-tuple-element.128) | copy-start | bytes 9220
  76.4 244.4 %copy-start.138 = (f32[768]{0:T(1024)}, f32[768]{0:T(1024)S(1)}, u32[]{:S(2)}) copy-start(f32[768]{0:T(1024)S(1)} %get-tuple-element.126) | copy-start | bytes 9220
  76.5 286.0 %copy-start.134 = (f32[768]{0:T(1024)}, f32[768]{0:T(1024)S(1)}, u32[]{:S(2)}) copy-start(f32[768]{0:T(1024)S(1)} %get-tuple-element.123) | copy-start | bytes 9220
  320.6 19.8 %copy-start.10 = (f32[320,768]{1,0:T(8,128)}, f32[320,768]{1,0:T(8,128)S(1)}, u32[]{:S(2)}) copy-start(f32[320,768]{1,0:T(8,128)S(1)} %get-tuple-element.99) | copy-start | bytes 2949124
  377.0 11.1 %slice-start.14 = ((s8[9437184]{0:T(1024)(128)(4,1)}), s8[4194304]{0:T(1024)(128)(4,1)S(1)}, s32[]{:S(2)}) async-start(s8[9437184]{0:T(1024)(128)(4,1)} %bitcast.449), calls=%async_computation.14 | async-start | bytes 8388608
  380.4 11.4 %copy-start.47 = (f32[320,768]{1,0:T(8,128)}, f32[320,768]{1,0:T(8,128)S(1)}, u32[]{:S(2)}) copy-start(f32[320,768]{1,0:T(8,128)S(1)} %get-tuple-element.93) | copy-start | bytes 2949124
  380.5 11.2 %copy-start.184 = (f32[320]{0:T(512)}, f32[320]{0:T(512)S(1)}, u32[]{:S(2)}) copy-start(f32[320]{0:T(512)S(1)} %negate_multiply_fusion.6) | copy-start | bytes 3844
  391.7 10.2 %copy-start.187 = (f32[320]{0:T(512)}, f32[320]{0:T(512)S(1)}, u32[]{:S(2)}) copy-start(f32[320]{0:T(512)S(1)} %negate_multiply_fusion.5) | copy-start | bytes 3844
  392.7 16.5 %copy-start.24 = (f32[320,768]{1,0:T(8,128)}, f32[320,768]{1,0:T(8,128)S(1)}, u32[]{:S(2)}) copy-start(f32[320,768]{1,0:T(8,128)S(1)} %get-tuple-element.113) | copy-start | bytes 2949124
  440.4 15.1 %copy-start.22 = (f32[320,768]{1,0:T(8,128)}, f32[320,768]{1,0:T(8,128)S(1)}, u32[]{:S(2)}) copy-start(f32[320,768]{1,0:T(8,128)S(1)} %add_add_fusion.15) | copy-start | bytes 2949124
  482.7 46.1 %copy-start.91 = (bf16[24,4608]{1,0:T(8,128)(2,1)S(1)}, bf16[24,4608]{1,0:T(8,128)(2,1)}, u32[]{:S(2)}) copy-start(bf16[24,4608]{1,0:T(8,128)(2,1)} %copy-done.90) | copy-start | bytes 663556
  482.7 46.1 %copy-start.119 = (f32[32,24]{0,1:T(8,128)S(1)}, f32[32,24]{0,1:T(8,128)}, u32[]{:S(2)}) copy-start(f32[32,24]{0,1:T(8,128)} %copy-done.118) | copy-start | bytes 9220
  528.8 35.8 %copy-start.48 = (f32[320,768]{1,0:T(8,128)S(1)}, f32[320,768]{1,0:T(8,128)}, u32[]{:S(2)}) copy-start(f32[320,768]{1,0:T(8,128)} %copy-done.47) | copy-start | bytes 2949124
  528.8 35.8 %copy-start.186 = (f32[320]{0:T(512)S(1)}, f32[320]{0:T(512)}, u32[]{:S(2)}) copy-start(f32[320]{0:T(512)} %copy-done.184) | copy-start | bytes 3844
  528.8 35.8 %copy-start.262 = (f32[768]{0:T(1024)S(1)}, f32[768]{0:T(1024)}, u32[]{:S(2)}) copy-start(f32[768]{0:T(1024)} %get-tuple-element.124) | copy-start | bytes 9220
  559.2 10.7 %copy-start.240 = (f32[1024]{0:T(1024)}, f32[1024]{0:T(1024)S(1)}, u32[]{:S(2)}) copy-start(f32[1024]{0:T(1024)S(1)} %slice_reduce_fusion) | copy-start | bytes 12292
  559.4 10.5 %copy-start.120 = (f32[24,20]{1,0:T(8,128)}, f32[24,20]{1,0:T(8,128)S(1)}, u32[]{:S(2)}) copy-start(f32[24,20]{1,0:T(8,128)S(1)} %reshape.697) | copy-start | bytes 5764
  629.6 190.9 %slice-start.4 = ((f32[24,10752]{1,0:T(8,128)}), f32[24,9216]{1,0:T(8,128)S(1)}, s32[]{:S(2)}) async-start(f32[24,10752]{1,0:T(8,128)} %copy-done.32), calls=%async_computation.4 | async-start | bytes 1769472 | tf_op jit(solution)/shard_map/slice | solution.py:954
  820.6 26.1 %copy-start.269 = (f32[2,24]{1,0:T(2,128)S(1)}, f32[2,24]{1,0:T(2,128)}, u32[]{:S(2)}) copy-start(f32[2,24]{1,0:T(2,128)} %param.33) | copy-start | bytes 580
  820.6 26.1 %copy-start.270 = (f32[2,24]{1,0:T(2,128)S(1)}, f32[2,24]{1,0:T(2,128)}, u32[]{:S(2)}) copy-start(f32[2,24]{1,0:T(2,128)} %param.43) | copy-start | bytes 580
  842.0 10.1 %copy-start.81 = (f32[2,32,1536]{2,1,0:T(8,128)S(1)}, f32[2,32,1536]{2,1,0:T(8,128)}, u32[]{:S(2)}) copy-start(f32[2,32,1536]{2,1,0:T(8,128)} %refs_1_.1) | copy-start | bytes 1179652
  (268 other events, 1181.5 us)

commit v2 on v1

v2 whole, which is shorter than its diff:
```python
import functools
import math

import jax
import jax.numpy as jnp
from jax import lax
from jax.experimental import pallas as pl
from jax.experimental.pallas import tpu as pltpu
from jax.sharding import PartitionSpec as P

D = 768
HEADS = 12
HEAD_DIM = 64
FF = 3072
FREQS = 256
LAYERS = 2
STEP = 10
MOD = 6 * D
JOINT = 4 * D + FF

EPSILON = 1e-06
NEGATIVE = -1e30
BETA_ONE = 0.5
BETA_TWO = 0.5
LEARN_RATE = 0.02
GAIN_RATE = 0.3
WEIGHT_DECAY = 0.01
ADAM_EPSILON = 1e-08
CLIP_NORM = 1.0

ALL = ("dp", "fsdp")
MESH = pl.DeviceIdType.MESH
VMEM_LIMIT = 60 * 1024 * 1024


def place(ways):
    dp_ways, fsdp_ways = ways
    row, col = lax.axis_index("dp"), lax.axis_index("fsdp")
    sizes = (dp_ways // 2, 2, fsdp_ways // 2)
    spot = (row // 2, lax.rem(row, 2), col // 2)
    return sizes, spot, lax.rem(col, 2)


def device_at(spot, core):
    z, y, x = spot
    return (z * 2 + y, x * 2 + core)


def moved(spot, axis, size, steps):
    spot = list(spot)
    spot[axis] = lax.rem(spot[axis] + steps, size)
    return tuple(spot)


def greet_peers(sizes, spot, core):
    barrier = pltpu.get_barrier_semaphore()
    count = 1
    pl.semaphore_signal(barrier, inc=1, device_id=device_at(spot, 1 - core), device_id_type=MESH)
    for axis in range(3):
        for steps in range(1, sizes[axis]):
            count += 1
            pl.semaphore_signal(
                barrier,
                inc=1,
                device_id=device_at(moved(spot, axis, sizes[axis], steps), core),
                device_id_type=MESH,
            )
    pl.semaphore_wait(barrier, count)


def remote(source, target, send, recv, device):
    return pltpu.make_async_remote_copy(
        src_ref=source, dst_ref=target, send_sem=send, recv_sem=recv, device_id=device, device_id_type=MESH
    )


def exchange_kernel(ways, shared, x_ref, out_ref, send_sem, recv_sem):
    dp_ways, fsdp_ways = ways
    count = dp_ways * fsdp_ways
    me = lax.axis_index("dp") * fsdp_ways + lax.axis_index("fsdp")

    def device(index):
        return (index // fsdp_ways, lax.rem(index, fsdp_ways))

    barrier = pltpu.get_barrier_semaphore()
    for step in range(1, count):
        pl.semaphore_signal(
            barrier, inc=1, device_id=device(lax.rem(me + step, count)), device_id_type=MESH
        )
    pl.semaphore_wait(barrier, count - 1)

    def copy(step):
        other = lax.rem(me + step, count)
        return remote(
            x_ref if shared else x_ref.at[other],
            out_ref.at[me],
            send_sem.at[step],
            recv_sem.at[step],
            device(other),
        )

    for step in range(1, count):
        copy(step).start()
    out_ref[me] = x_ref[...] if shared else x_ref[me]
    for step in range(1, count):
        origin = lax.rem(me + count - step, count)
        remote(
            x_ref if shared else x_ref.at[0],
            out_ref.at[origin],
            send_sem.at[step],
            recv_sem.at[step],
            device(origin),
        ).wait_recv()
    for step in range(1, count):
        copy(step).wait_send()


def exchange(values, ways, shared, number):
    count = ways[0] * ways[1]
    tile = values.shape if shared else values.shape[1:]
    return pl.pallas_call(
        functools.partial(exchange_kernel, ways, shared),
        out_shape=jax.ShapeDtypeStruct((count,) + tile, values.dtype),
        in_specs=[pl.BlockSpec(memory_space=pltpu.VMEM)],
        out_specs=pl.BlockSpec(memory_space=pltpu.VMEM),
        scratch_shapes=[pltpu.SemaphoreType.DMA((count,)), pltpu.SemaphoreType.DMA((count,))],
        compiler_params=pltpu.CompilerParams(
            collective_id=number, has_side_effects=True, vmem_limit_bytes=VMEM_LIMIT
        ),
    )(values)


def gather_kernel(ways, rows, halves, items, layers, *refs):
    members = len(rows)
    shards = refs[:members]
    fulls = refs[members : members + members * layers]
    rest = refs[members + members * layers :]
    stages = rest[:members]
    blocks = rest[members : 2 * members]
    pre_send, pre_recv, own_sem, put_sem, *sends, c_send, c_recv = rest[2 * members :]
    sends, recvs = sends[0::2], sends[1::2]
    sizes, spot, core = place(ways)
    z, y, x = spot
    partner = device_at(spot, 1 - core)
    greet_peers(sizes, spot, core)

    def full(layer, member):
        return fulls[layer * members + member]

    pre = []
    for layer in range(layers):
        for member in range(members):
            height, half = rows[member], halves[member]
            place_in = stages[member].at[layer, pl.ds(pl.multiple_of(core * height, 8), height)]
            mine = shards[member].at[layer, :, pl.ds(pl.multiple_of(core * half, 128), half)]
            other = shards[member].at[layer, :, pl.ds(pl.multiple_of((1 - core) * half, 128), half)]
            index = layer * members + member
            sent = remote(other, place_in, pre_send.at[index], pre_recv.at[index], partner)
            sent.start()
            kept = pltpu.make_async_copy(mine, place_in, own_sem.at[index])
            kept.start()
            pre.append((sent, kept))
    arrived = set()
    put_done = set()
    sent_all = []

    def columns(i, side):
        _, member, start, size, _ = items[i]
        return pl.ds(pl.multiple_of(side * halves[member] + start, 128), size)

    def put(layer, member):
        half = halves[member]
        return pltpu.make_async_copy(
            blocks[member].at[layer],
            full(layer, member).at[z, y, x, :, pl.ds(pl.multiple_of(core * half, 128), half)],
            put_sem.at[layer * members + member],
        )

    def ready(layer, member):
        if (layer, member) in arrived:
            return
        arrived.add((layer, member))
        index = layer * members + member
        height = rows[member]
        sent, kept = pre[index]
        kept.wait()
        theirs = stages[member].at[layer, pl.ds(pl.multiple_of((1 - core) * height, 8), height)]
        remote(theirs, theirs, pre_send.at[index], pre_recv.at[index], partner).wait_recv()
        blocks[member][layer] = stages[member][layer].astype(jnp.bfloat16)
        put(layer, member).start()

    def own_put(layer, member):
        if (layer, member) not in put_done:
            put_done.add((layer, member))
            put(layer, member).wait()

    def region(i, phase, origin, side):
        layer, member, start, size, order = items[i]
        index = [slice(None) if order.index(axis) < phase else spot[axis] for axis in range(3)]
        if phase < 3 and origin is not None:
            index[order[phase]] = origin
        return full(layer, member).at[(*index, slice(None), columns(i, side))]

    def send(copy):
        copy.start()
        sent_all.append(copy)

    def start(i, phase):
        layer, member, first, size, order = items[i]
        axis = order[phase]
        if phase == 0:
            ready(layer, member)
            source = blocks[member].at[layer, :, pl.ds(first, size)]
        else:
            own_put(layer, member)
            source = region(i, phase, None, core)
        for steps in range(1, sizes[axis]):
            send(
                remote(
                    source, region(i, phase, spot[axis], core),
                    sends[phase].at[i, steps - 1], recvs[phase].at[i, steps - 1],
                    device_at(moved(spot, axis, sizes[axis], steps), core),
                )
            )
        if phase == 2:
            send(remote(source, source, c_send.at[i, 0], c_recv.at[i, 0], partner))

    def finish(i, phase):
        axis = items[i][4][phase]
        for steps in range(1, sizes[axis]):
            land = region(i, phase, lax.rem(spot[axis] + sizes[axis] - steps, sizes[axis]), core)
            remote(land, land, sends[phase].at[i, steps - 1], recvs[phase].at[i, steps - 1], partner).wait_recv()
            if phase == 2:
                send(remote(land, land, c_send.at[i, steps], c_recv.at[i, steps], partner))

    def c_wait(i):
        axis = items[i][4][2]
        for steps in range(sizes[axis]):
            land = region(i, 2, lax.rem(spot[axis] + sizes[axis] - steps, sizes[axis]), 1 - core)
            remote(land, land, c_send.at[i, steps], c_recv.at[i, steps], partner).wait_recv()

    for i, phase in schedule(items, GATHER_LAGS):
        if phase > 0:
            finish(i, phase - 1)
        if phase < 3:
            start(i, phase)
    for i in range(len(items)):
        c_wait(i)
    for layer in range(layers):
        for member in range(members):
            own_put(layer, member)
    for sent, _ in pre:
        sent.wait_send()
    for copy in sent_all:
        copy.wait_send()


def gather_weights(shards, halves, ways, number, items):
    layers = shards[0].shape[0]
    rows = [s.shape[1] for s in shards]
    members = len(shards)
    sizes = (ways[0] // 2, 2, ways[1] // 2)
    count = layers * members
    n = len(items)
    sem = pltpu.SemaphoreType.DMA
    out = pl.pallas_call(
        functools.partial(gather_kernel, ways, rows, halves, items, layers),
        out_shape=[
            jax.ShapeDtypeStruct(sizes + (2 * rows[m], 2 * halves[m]), jnp.bfloat16)
            for _ in range(layers)
            for m in range(members)
        ],
        in_specs=[pl.BlockSpec(memory_space=pl.ANY)] * members,
        out_specs=[pl.BlockSpec(memory_space=pl.ANY)] * count,
        scratch_shapes=[pltpu.VMEM((layers, 2 * rows[m], halves[m]), jnp.float32) for m in range(members)]
        + [pltpu.VMEM((layers, 2 * rows[m], halves[m]), jnp.bfloat16) for m in range(members)]
        + [sem((count,))] * 4
        + [sem((n, max(sizes)))] * 8,
        compiler_params=pltpu.CompilerParams(
            collective_id=number, has_side_effects=True, vmem_limit_bytes=VMEM_LIMIT
        ),
    )(*shards)
    return [
        [out[l * members + m].reshape(-1, 2 * halves[m]) for m in range(members)] for l in range(layers)
    ]


ORDERS = ((0, 2, 1), (0, 1, 2), (2, 0, 1), (1, 0, 2))
GATHER_LAGS = ((-3.0, 0.0, 2.0, 4.0), (-3.0, 0.0, 2.0, 4.0))
SCATTER_LAGS = ((-2.0, 0.0, 2.0, 4.0, 6.0), (-2.0, 0.0, 2.0, 4.0, 6.0))
GATHER_PATTERN = (0, 1)
SCATTER_PATTERN = (0, 1)


def schedule(items, lags):
    steps = []
    for i, item in enumerate(items):
        own = lags[0 if item[4][0] == 0 else 1]
        steps.extend((i + lag, -phase, i) for phase, lag in enumerate(own))
    return [(i, -phase) for _, phase, i in sorted(steps)]


def plan(halves, layers, pattern):
    items = []
    for layer in layers:
        for member, width in enumerate(halves):
            size = width // 4 if width % 512 == 0 else (width // 2 if width % 256 == 0 else 128)
            for start in range(0, width, size):
                items.append((layer, member, start, size, ORDERS[pattern[len(items) % len(pattern)]]))
    return items


ACTS = ("n1", "n2", "n3", "mixed1", "mixed2", "hidden", "g_self", "g_cq", "g_pre", "g_ckv", "g_one", "g_cross", "g_three")


def scatter_kernel(ways, rows, halves, items, layers, *refs):
    members = len(rows)
    n = len(items)
    rest = list(refs)

    def take(count):
        taken = rest[:count]
        del rest[:count]
        return taken

    (text_in,) = take(1)
    acts = [dict(zip(ACTS, take(len(ACTS)))) for _ in range(layers)]
    outs = take(members)
    lefts, rights, text, right_text, hidden, mixes, right_out = take(7)
    ring = take(members)
    whole = take(n)
    parts = [take(n) for _ in range(3)]
    sums = take(n)
    load_sem, c_send, c_recv, *sems, e_send, e_recv, o_sem = rest
    sends, recvs = sems[0::2], sems[1::2]
    sizes, spot, core = place(ways)
    partner = device_at(spot, 1 - core)
    greet_peers(sizes, spot, core)
    frames = hidden.shape[0]
    sent_all = []

    def send(copy):
        copy.start()
        sent_all.append(copy)

    def loads(layer, member):
        a = acts[layer]
        if member == 0:
            pairs = [(a["n1"], lefts.at[0]), (a["n2"], lefts.at[1]), (a["n3"], lefts.at[2])]
            pairs += [(a["g_self"].at[:, j * D : (j + 1) * D], rights.at[j]) for j in range(3)]
            pairs += [(a["g_cq"], rights.at[3])]
            pairs += [(a["g_pre"].at[:, j * D : (j + 1) * D], rights.at[4 + j]) for j in range(4)]
        elif member == 1:
            pairs = [(a["g_ckv"].at[:, j * D : (j + 1) * D], right_text.at[j]) for j in range(2)]
            if layer == items[0][0]:
                pairs.append((text_in, text))
        else:
            pairs = [(a["mixed1"], mixes.at[0]), (a["mixed2"], mixes.at[1]), (a["hidden"], hidden)]
            for j, name in enumerate(("g_one", "g_cross", "g_three")):
                pairs += [(a[name].at[:, side * (D // 2) : (side + 1) * (D // 2)], right_out.at[side, j]) for side in range(2)]
        return [
            pltpu.make_async_copy(source, target, load_sem.at[layer, member, j])
            for j, (source, target) in enumerate(pairs)
        ]

    def load(layer, member):
        for copy in loads(layer, member):
            copy.start()

    loaded = set()

    def need(layer, member):
        if (layer, member) not in loaded:
            loaded.add((layer, member))
            for copy in loads(layer, member):
                copy.wait()

    def product(i, side, store):
        layer, member, start, size, _ = items[i]
        need(layer, member)
        if member == 0:
            j = start // D
            at = pl.ds(start % D, size)
            left = jnp.where(side == 1, 2, 0 if j < 3 else 1)
            right = rights[side * 4 + j, :, at]
            for row in range(0, D, 384):
                store(pl.ds(row, 384), dot_tn(lefts[left, :, row : row + 384], right))
        elif member == 1:
            right = right_text[side, :, pl.ds(start, size)]
            for row in range(0, text.shape[1], 512):
                store(pl.ds(row, 512), dot_tn(text[:, row : row + 512], right))
        else:
            cols = pl.ds(start, size)
            for j in range(2):
                store(pl.ds(j * D, D), dot_tn(mixes[j], right_out[side, j, :, cols]))

            @pl.loop(0, 4)
            def _(j):
                at = pl.multiple_of(j * D, D)
                store(pl.ds(pl.multiple_of(2 * D + j * D, D), D), dot_tn(hidden[:, pl.ds(at, D)], right_out[side, 2, :, cols]))

    def columns(i, side):
        _, member, start, size, _ = items[i]
        return pl.ds(pl.multiple_of(side * halves[member] + start, 128), size)

    def blocks(ref, i):
        return ref.reshape(sizes + (2 * rows[items[i][1]], items[i][3]))

    ring_at, used = [], {}
    for i, (_, member, *_) in enumerate(items):
        ring_at.append(used.setdefault(member, []))
        ring_at[-1] = len(used[member])
        used[member].append(i)

    def c_copy(i):
        member, size = items[i][1], items[i][3]
        slot = ring_at[i] % 2
        return remote(ring[member].at[slot, :, pl.ds(0, size)], whole[i], c_send.at[i], c_recv.at[i], partner)

    def give(i):
        member, size = items[i][1], items[i][3]
        slot = ring_at[i] % 2
        if ring_at[i] >= 2:
            c_copy(used[member][ring_at[i] - 2]).wait_send()
        target = ring[member].at[slot]

        def store(at, value):
            target[at, pl.ds(0, size)] = value.astype(jnp.bfloat16)

        product(i, 1 - core, store)
        c_copy(i).start()

    def combine(i):
        c_copy(i).wait_recv()
        target = whole[i]

        def store(at, value):
            target[at, :] = (target[at, :].astype(jnp.float32) + value).astype(jnp.bfloat16)

        product(i, core, store)
        layer, member = items[i][:2]
        if i == used_last[layer, member] and (layer, member) in after:
            load(*after[layer, member])

    used_last, after, seen_layers = {}, {}, []
    for i, item in enumerate(items):
        used_last[item[:2]] = i
        if item[0] not in seen_layers:
            seen_layers.append(item[0])
    for early, late in zip(seen_layers, seen_layers[1:]):
        for member in range(members):
            after[early, member] = (late, member)

    def way(i):
        return items[i][4][::-1]

    def region(i, phase, place_on):
        order = way(i)
        index = [spot[axis] if axis in order[:phase] else slice(None) for axis in range(3)]
        index[order[phase]] = place_on
        return blocks(whole[i], i).at[tuple(index)]

    def start(i, phase):
        axis = way(i)[phase]
        for steps in range(1, sizes[axis]):
            target = moved(spot, axis, sizes[axis], steps)
            send(
                remote(
                    region(i, phase, target[axis]), parts[phase][i].at[steps - 1],
                    sends[phase].at[i, steps - 1], recvs[phase].at[i, steps - 1], device_at(target, core),
                )
            )

    def owned(i, side):
        height = rows[items[i][1]]
        return sums[i].at[pl.ds(pl.multiple_of(side * height, 8), height)]

    def e_copy(i):
        layer, member = items[i][:2]
        return remote(
            owned(i, 1 - core), outs[member].at[layer, :, columns(i, core)], e_send.at[i], e_recv.at[i], partner
        )

    def o_copy(i):
        layer, member = items[i][:2]
        return pltpu.make_async_copy(owned(i, core), outs[member].at[layer, :, columns(i, core)], o_sem.at[i])

    def finish(i, phase):
        axis = way(i)[phase]
        for steps in range(1, sizes[axis]):
            land = parts[phase][i].at[steps - 1]
            remote(land, land, sends[phase].at[i, steps - 1], recvs[phase].at[i, steps - 1], partner).wait_recv()
        mine = region(i, phase, spot[axis])
        landed = parts[phase][i]

        def total(index):
            value = mine[index].astype(jnp.float32)
            for steps in range(1, sizes[axis]):
                value = value + landed[(steps - 1, *index)].astype(jnp.float32)
            return value

        if phase == 2:
            sums[i][...] = total((Ellipsis,))
            e_copy(i).start()
            o_copy(i).start()
        else:
            left = [sizes[other] for other in range(3) if other not in way(i)[: phase + 1]]

            @pl.loop(0, left[0])
            def _(index):
                mine[index] = total((index,)).astype(jnp.bfloat16)

    for member in range(members):
        load(items[0][0], member)
    for i, step in schedule(items, SCATTER_LAGS):
        if step == 0:
            give(i)
            continue
        if step == 1:
            combine(i)
        else:
            finish(i, step - 2)
        if step < 4:
            start(i, step - 1)
    for i in range(n):
        e_copy(i).wait()
        o_copy(i).wait()
    for member in range(members):
        for i in used[member][-2:]:
            c_copy(i).wait_send()
    for copy in sent_all:
        copy.wait_send()


def scatter_grads(kept, text, rows, halves, ways, number, items):
    layers, members = len(kept), len(rows)
    sizes = (ways[0] // 2, 2, ways[1] // 2)
    n = len(items)
    sem = pltpu.SemaphoreType.DMA
    low = jnp.bfloat16
    chips = sizes[0] * sizes[1] * sizes[2]
    frames, tokens = kept[0]["n1"].shape[0], text.shape[0]
    most = [max(s for _, m, _, s, _ in items if m == member) for member in range(members)]
    vmem = pltpu.VMEM

    def part(item, phase):
        _, member, _, size, order = item
        order = order[::-1]
        left = tuple(sizes[axis] for axis in range(3) if axis not in order[: phase + 1])
        return vmem((sizes[order[phase]] - 1, *left, 2 * rows[member], size), low)

    scratch = [
        vmem((3, frames, D), low),
        vmem((8, frames, D), low),
        vmem(text.shape, low),
        vmem((2, tokens, D), low),
        vmem((frames, FF), low),
        vmem((2, frames, D), low),
        vmem((2, 3, frames, D // 2), low),
    ]
    scratch += [vmem((2, chips * 2 * rows[m], most[m]), low) for m in range(members)]
    scratch += [vmem((chips * 2 * rows[m], s), low) for _, m, _, s, _ in items]
    scratch += [part(item, phase) for phase in range(3) for item in items]
    scratch += [vmem((2 * rows[m], s), jnp.float32) for _, m, _, s, _ in items]
    scratch += [sem((layers, members, 11))] + [sem((n,))] * 2 + [sem((n, max(sizes)))] * 6 + [sem((n,))] * 3
    flat = [text] + [k[name] for k in kept for name in ACTS]
    return pl.pallas_call(
        functools.partial(scatter_kernel, ways, rows, halves, items, layers),
        out_shape=[
            jax.ShapeDtypeStruct((layers, rows[m], 2 * halves[m]), jnp.float32) for m in range(members)
        ],
        in_specs=[pl.BlockSpec(memory_space=pl.ANY)] * len(flat),
        out_specs=[pl.BlockSpec(memory_space=pl.ANY)] * members,
        scratch_shapes=scratch,
        compiler_params=pltpu.CompilerParams(
            collective_id=number, has_side_effects=True, vmem_limit_bytes=VMEM_LIMIT
        ),
    )(*flat)


def to_low(values):
    return values.astype(jnp.bfloat16)


def dense(left, right):
    return jnp.dot(left, right, preferred_element_type=jnp.float32)


def dense_back(left, right):
    return lax.dot_general(left, right, (((1,), (1,)), ((), ())), preferred_element_type=jnp.float32)


def weight_grad(left, right):
    return lax.dot_general(left, right, (((0,), (0,)), ((), ())), preferred_element_type=jnp.float32)


def noise_level(steps):
    phase = (steps.astype(jnp.float32) / 1000.0 + 0.008) / 1.008 * (math.pi / 2)
    return jnp.cos(phase) ** 2


def time_features(steps):
    half_width = FREQS // 2
    frequency = jnp.exp(-math.log(10000.0) * jnp.arange(half_width, dtype=jnp.float32) / half_width)
    angles = steps.astype(jnp.float32)[:, None] * frequency[None, :]
    return jnp.concatenate([jnp.cos(angles), jnp.sin(angles)], -1)


ROOT = math.sqrt(2.0 / math.pi)
CUBE = 0.044715
CHUNK = 64
WIDE = 512


def dot_nn(left, right):
    return lax.dot_general(left, right, (((1,), (0,)), ((), ())), preferred_element_type=jnp.float32)


def dot_nt(left, right):
    return lax.dot_general(left, right, (((1,), (1,)), ((), ())), preferred_element_type=jnp.float32)


def dot_tn(left, right):
    return lax.dot_general(left, right, (((0,), (0,)), ((), ())), preferred_element_type=jnp.float32)


def over_rows(count, step):
    @pl.loop(0, count // CHUNK)
    def _(index):
        step(pl.ds(pl.multiple_of(index * CHUNK, CHUNK), CHUNK))


def over_columns(count, width, step):
    @pl.loop(0, count // width)
    def _(index):
        step(pl.multiple_of(index * width, width))


def scaled(values):
    centred = values - jnp.mean(values, -1, keepdims=True)
    factor = lax.rsqrt(jnp.mean(centred * centred, -1, keepdims=True) + EPSILON)
    return centred * factor, factor


def norm_pull(normed, factor, grad):
    middle = jnp.mean(grad, -1, keepdims=True)
    along = jnp.mean(grad * normed, -1, keepdims=True)
    return factor * (grad - middle - normed * along)


def row_sum(values):
    return jnp.sum(values, 0, keepdims=True)


def probabilities(query, key, keep):
    scores = dot_nt(query, key) * HEAD_DIM ** (-0.5)
    scores = jnp.where(keep, scores, NEGATIVE)
    shifted = jnp.exp(scores - jnp.max(scores, -1, keepdims=True))
    return shifted * (1.0 / jnp.sum(shifted, -1, keepdims=True))


def attend(q_at, k_at, v_at, keep, store):
    first = lax.broadcasted_iota(jnp.int32, (1, 2 * HEAD_DIM), 1) < HEAD_DIM

    def pair(index):
        query, key, value = q_at(index), k_at(index), v_at(index)
        zero = jnp.zeros_like(query)
        out_a = dot_nn(to_low(probabilities(jnp.where(first, query, zero), key, keep)), value)
        out_b = dot_nn(to_low(probabilities(jnp.where(first, zero, query), key, keep)), value)
        store(index, to_low(jnp.where(first, out_a, out_b)))

    for index in range(HEADS // 2):
        pair(index)


def attend_back(q_at, k_at, v_at, grad_at, keep, store):
    first = lax.broadcasted_iota(jnp.int32, (1, 2 * HEAD_DIM), 1) < HEAD_DIM

    def pair(index):
        query, key, value, grad = q_at(index), k_at(index), v_at(index), grad_at(index)
        zero = jnp.zeros_like(query)
        parts = []
        for mine in (first, jnp.logical_not(first)):
            probs = probabilities(jnp.where(mine, query, zero), key, keep)
            grad_value = dot_tn(to_low(probs), grad)
            grad_probs = dot_nt(jnp.where(mine, grad, zero), value)
            inner = jnp.sum(probs * grad_probs, -1, keepdims=True)
            grad_scores = to_low(probs * (grad_probs - inner))
            grad_query = dot_nn(grad_scores, key) * HEAD_DIM ** (-0.5)
            grad_key = dot_tn(grad_scores, query) * HEAD_DIM ** (-0.5)
            parts.append((grad_query, grad_key, grad_value))
        store(index, *(to_low(jnp.where(first, a, b)) for a, b in zip(*parts)))

    for index in range(HEADS // 2):
        pair(index)


def tile_of(ref, base):
    return lambda index: ref[:, base + index * 2 * HEAD_DIM : base + (index + 1) * 2 * HEAD_DIM]


SAVED = (
    ("stream", D, jnp.float32),
    ("n1", D, jnp.bfloat16),
    ("qkv", 3 * D, jnp.bfloat16),
    ("mixed1", D, jnp.bfloat16),
    ("branch1", D, jnp.float32),
    ("stream2", D, jnp.float32),
    ("n2", D, jnp.bfloat16),
    ("cq", D, jnp.bfloat16),
    ("ckv", 2 * D, jnp.bfloat16),
    ("mixed2", D, jnp.bfloat16),
    ("stream3", D, jnp.float32),
    ("n3", D, jnp.bfloat16),
    ("branch3", D, jnp.float32),
)
GRADS = (
    ("g_self", 3 * D),
    ("g_cq", D),
    ("g_pre", FF),
    ("g_ckv", 2 * D),
    ("g_one", D),
    ("g_cross", D),
    ("g_three", D),
)
PARTS = ("qkv", "cq", "up", "text", "ao", "co", "down")
KEPT = ("n1", "n2", "n3", "mixed1", "mixed2", "hidden") + tuple(name for name, _ in GRADS)


class Names:
    def __init__(self, **refs):
        self.__dict__.update(refs)


def block_forward(s, hidden, result, mods, text, frame_keep, text_keep, w, need, done, emit):
    frames = s.stream.shape[0]

    def norm_one(rows):
        normed, _ = scaled(s.stream[rows, :])
        s.n1[rows, :] = to_low(normed * (1.0 + mods[1:2, :]) + mods[0:1, :])

    over_rows(frames, norm_one)
    emit("n1", s.n1)
    need("qkv")

    def project(column):
        cols = pl.ds(column, 256)
        s.qkv[:, cols] = to_low(dot_nn(s.n1[...], w.win[:, cols]))

    over_columns(3 * D, 256, project)
    done("qkv")

    def mix_one(index, value):
        s.mixed1[:, index * 128 : (index + 1) * 128] = value

    attend(tile_of(s.qkv, 0), tile_of(s.qkv, D), tile_of(s.qkv, 2 * D), frame_keep, mix_one)
    emit("mixed1", s.mixed1)
    need("ao")

    def branch_one(column):
        cols = pl.ds(column, 256)
        branch = dot_nn(s.mixed1[...], w.wout[0:D, cols])
        s.branch1[:, cols] = branch
        s.stream2[:, cols] = s.stream[:, cols] + mods[2:3, cols] * branch

    over_columns(D, 256, branch_one)
    done("ao")

    def norm_two(rows):
        normed, _ = scaled(s.stream2[rows, :])
        s.n2[rows, :] = to_low(normed * mods[6:7, :])

    over_rows(frames, norm_two)
    emit("n2", s.n2)
    need("cq")

    def project_cross(column):
        cols = pl.ds(column, 256)
        s.cq[:, cols] = to_low(dot_nn(s.n2[...], w.win[:, pl.ds(3 * D + column, 256)]))

    over_columns(D, 256, project_cross)
    done("cq")
    need("text")

    def project_text(column):
        cols = pl.ds(column, 256)
        s.ckv[:, cols] = to_low(dot_nn(text[...], w.wtext[:, cols]))

    over_columns(2 * D, 256, project_text)
    done("text")

    def mix_two(index, value):
        s.mixed2[:, index * 128 : (index + 1) * 128] = value

    attend(tile_of(s.cq, 0), tile_of(s.ckv, 0), tile_of(s.ckv, D), text_keep, mix_two)
    emit("mixed2", s.mixed2)
    need("co")

    def branch_two(column):
        cols = pl.ds(column, 256)
        s.stream3[:, cols] = s.stream2[:, cols] + dot_nn(s.mixed2[...], w.wout[D : 2 * D, cols])

    over_columns(D, 256, branch_two)
    done("co")

    def norm_three(rows):
        normed, _ = scaled(s.stream3[rows, :])
        s.n3[rows, :] = to_low(normed * (1.0 + mods[4:5, :]) + mods[3:4, :])

    over_rows(frames, norm_three)
    emit("n3", s.n3)
    need("up")

    def expand(column):
        upper = dot_nn(s.n3[...], w.win[:, pl.ds(4 * D + column, WIDE)])
        tanh = jnp.tanh(ROOT * (upper + CUBE * (upper * upper * upper)))
        hidden[:, pl.ds(column, WIDE)] = to_low(0.5 * upper * (1.0 + tanh))

    over_columns(FF, WIDE, expand)
    done("up")
    emit("hidden", hidden)
    need("down")

    def branch_three(column):
        cols = pl.ds(column, 256)
        branch = dot_nn(hidden[...], w.wout[2 * D :, cols])
        s.branch3[:, cols] = branch
        result[:, cols] = s.stream3[:, cols] + mods[5:6, cols] * branch

    over_columns(D, 256, branch_three)
    done("down")


def block_backward(s, g, grad, mods, grad_mods, inner, mixed, frame_keep, text_keep, w, need, done, emit):
    frames = s.stream.shape[0]
    grad_mods[...] = jnp.zeros_like(grad_mods)

    def gate_three(rows):
        grad_out = grad[rows, :]
        g.g_three[rows, :] = to_low(grad_out * mods[5:6, :])
        grad_mods[5:6, :] += row_sum(grad_out * s.branch3[rows, :])

    over_rows(frames, gate_three)
    emit("g_three", g.g_three)
    need("down")
    need("up")

    def shrink(column):
        wide = pl.ds(column, WIDE)
        back = dot_nt(g.g_three[...], w.wout[pl.ds(2 * D + column, WIDE), :])
        upper = dot_nn(s.n3[...], w.win[:, pl.ds(4 * D + column, WIDE)])
        square = upper * upper
        tanh = jnp.tanh(ROOT * (upper + CUBE * (square * upper)))
        slope = 0.5 * (1.0 + tanh) + (0.5 * ROOT) * upper * (1.0 - tanh * tanh) * (1.0 + (3.0 * CUBE) * square)
        g.g_pre[:, wide] = to_low(back * slope)

    over_columns(FF, WIDE, shrink)
    done("down")
    emit("g_pre", g.g_pre)

    def inner_three(column):
        inner[:, pl.ds(column, 256)] = dot_nt(g.g_pre[...], w.win[pl.ds(column, 256), 4 * D :])

    over_columns(D, 256, inner_three)
    done("up")

    def pull_three(rows):
        normed, factor = scaled(s.stream3[rows, :])
        back = inner[rows, :]
        grad_mods[3:4, :] += row_sum(back)
        grad_mods[4:5, :] += row_sum(back * normed)
        total = grad[rows, :] + norm_pull(normed, factor, back * (1.0 + mods[4:5, :]))
        grad[rows, :] = total
        g.g_cross[rows, :] = to_low(total)

    over_rows(frames, pull_three)
    emit("g_cross", g.g_cross)
    need("co")

    def back_cross(column):
        mixed[:, pl.ds(column, 256)] = to_low(dot_nt(g.g_cross[...], w.wout[pl.ds(D + column, 256), :]))

    over_columns(D, 256, back_cross)
    done("co")

    def store_cross(index, grad_query, grad_key, grad_value):
        cols = slice(index * 128, (index + 1) * 128)
        g.g_cq[:, cols] = grad_query
        g.g_ckv[:, cols] = grad_key
        g.g_ckv[:, D + index * 128 : D + (index + 1) * 128] = grad_value

    attend_back(
        tile_of(s.cq, 0), tile_of(s.ckv, 0), tile_of(s.ckv, D), tile_of(mixed, 0), text_keep, store_cross
    )
    emit("g_cq", g.g_cq)
    emit("g_ckv", g.g_ckv)
    need("cq")

    def inner_two(column):
        inner[:, pl.ds(column, 256)] = dot_nt(g.g_cq[...], w.win[pl.ds(column, 256), 3 * D : 4 * D])

    over_columns(D, 256, inner_two)
    done("cq")

    def pull_two(rows):
        normed, factor = scaled(s.stream2[rows, :])
        back = inner[rows, :]
        grad_mods[6:7, :] += row_sum(back * normed)
        total = grad[rows, :] + norm_pull(normed, factor, back * mods[6:7, :])
        grad[rows, :] = total
        g.g_one[rows, :] = to_low(total * mods[2:3, :])
        grad_mods[2:3, :] += row_sum(total * s.branch1[rows, :])

    over_rows(frames, pull_two)
    emit("g_one", g.g_one)
    need("ao")

    def back_self(column):
        mixed[:, pl.ds(column, 256)] = to_low(dot_nt(g.g_one[...], w.wout[pl.ds(column, 256), :]))

    over_columns(D, 256, back_self)
    done("ao")

    def store_self(index, grad_query, grad_key, grad_value):
        cols = slice(index * 128, (index + 1) * 128)
        g.g_self[:, cols] = grad_query
        g.g_self[:, D + index * 128 : D + (index + 1) * 128] = grad_key
        g.g_self[:, 2 * D + index * 128 : 2 * D + (index + 1) * 128] = grad_value

    attend_back(
        tile_of(s.qkv, 0), tile_of(s.qkv, D), tile_of(s.qkv, 2 * D), tile_of(mixed, 0), frame_keep, store_self
    )
    emit("g_self", g.g_self)
    need("qkv")

    def inner_one(column):
        inner[:, pl.ds(column, 256)] = dot_nt(g.g_self[...], w.win[pl.ds(column, 256), : 3 * D])

    over_columns(D, 256, inner_one)
    done("qkv")

    def pull_one(rows):
        normed, factor = scaled(s.stream[rows, :])
        back = inner[rows, :]
        grad_mods[0:1, :] += row_sum(back)
        grad_mods[1:2, :] += row_sum(back * normed)
        grad[rows, :] = grad[rows, :] + norm_pull(normed, factor, back * (1.0 + mods[1:2, :]))

    over_rows(frames, pull_one)


def model_kernel(*refs):
    refs = list(refs)

    def take(count):
        taken = refs[:count]
        del refs[:count]
        return taken

    lengths, factor_ref, stream_ref, mods_ref, final_mods, text, noise, head = take(8)
    weights = [take(3) for _ in range(LAYERS)]
    loss_ref, grad_ref, grad_mods_ref, grad_final, grad_head = take(5)
    kept_out = [dict(zip(KEPT, take(len(KEPT)))) for _ in range(LAYERS)]
    win, wtext, wout = take(3)
    saved = [Names(**dict(zip((name for name, *_ in SAVED), take(len(SAVED))))) for _ in range(LAYERS)]
    g = Names(**dict(zip((name for name, _ in GRADS), take(len(GRADS)))))
    hidden, inner, mixed, final_low = take(4)
    load_sem, keep_sem = refs
    w = Names(win=win, wtext=wtext, wout=wout)
    frames, tokens = stream_ref.shape[0], text.shape[0]
    frame_keep = lax.broadcasted_iota(jnp.int32, (1, frames), 1) < lengths[0]
    text_keep = lax.broadcasted_iota(jnp.int32, (1, tokens), 1) < lengths[1]

    def load(layer, part):
        w_in, w_text, w_out = weights[layer]
        source, target = {
            "qkv": (w_in.at[:, : 3 * D], win.at[:, : 3 * D]),
            "cq": (w_in.at[:, 3 * D : 4 * D], win.at[:, 3 * D : 4 * D]),
            "up": (w_in.at[:, 4 * D :], win.at[:, 4 * D :]),
            "text": (w_text, wtext),
            "ao": (w_out.at[:D], wout.at[:D]),
            "co": (w_out.at[D : 2 * D], wout.at[D : 2 * D]),
            "down": (w_out.at[2 * D :], wout.at[2 * D :]),
        }[part]
        return pltpu.make_async_copy(source, target, load_sem.at[PARTS.index(part)])

    flying = {}

    def keep(layer):
        def emit(name, ref):
            copy = pltpu.make_async_copy(
                ref, kept_out[layer][name], keep_sem.at[layer, KEPT.index(name)]
            )
            copy.start()
            flying[name, layer] = copy

        return emit

    def settle(layer, names):
        for name in names:
            copy = flying.pop((name, layer), None)
            if copy is not None:
                copy.wait()

    nothing = lambda part: None
    for part in ("qkv", "ao", "cq", "text", "co", "up", "down"):
        load(0, part).start()
    over_rows(frames, lambda rows: saved[0].stream.__setitem__((rows, slice(None)), stream_ref[rows, :]))
    for layer in range(LAYERS):
        last = layer == LAYERS - 1
        if layer > 0:
            settle(layer - 1, ("hidden",))
        block_forward(
            saved[layer], hidden, grad_ref if last else saved[layer + 1].stream,
            mods_ref.at[layer], text, frame_keep, text_keep, w,
            lambda part: load(layer, part).wait(),
            nothing if last else (lambda part: load(layer + 1, part).start()),
            keep(layer),
        )

    def norm_final(rows):
        normed, _ = scaled(grad_ref[rows, :])
        final_low[rows, :] = to_low(normed * (1.0 + final_mods[1:2, :]) + final_mods[0:1, :])

    over_rows(frames, norm_final)
    error = dot_nn(final_low[...], head[...]) - noise[...]
    counted = lax.broadcasted_iota(jnp.int32, (frames, 1), 0) < lengths[0]
    error = jnp.where(counted, error, 0.0)
    loss_ref[...] = jnp.broadcast_to(row_sum(error * error), loss_ref.shape)
    grad_pred = to_low(error * factor_ref[0])
    grad_head[...] = dot_tn(final_low[...], grad_pred)
    inner[...] = dot_nt(grad_pred, head[...])
    grad_final[...] = jnp.zeros_like(grad_final)

    def pull_final(rows):
        normed, factor = scaled(grad_ref[rows, :])
        back = inner[rows, :]
        grad_final[0:1, :] += row_sum(back)
        grad_final[1:2, :] += row_sum(back * normed)
        grad_ref[rows, :] = norm_pull(normed, factor, back * (1.0 + final_mods[1:2, :]))

    over_rows(frames, pull_final)
    for layer in reversed(range(LAYERS)):
        last = layer == LAYERS - 1
        if not last:
            settle(layer + 1, [name for name, _ in GRADS])
        block_backward(
            saved[layer], g, grad_ref, mods_ref.at[layer], grad_mods_ref.at[layer], inner, mixed,
            frame_keep, text_keep, w,
            nothing if last else (lambda part: load(layer, part).wait()),
            nothing if layer == 0 else (lambda part: load(layer - 1, part).start()),
            keep(layer),
        )
    for layer in range(LAYERS):
        settle(layer, KEPT)


def run_model(stream, mods, final_mods, text, noise, head, lengths, factor, weights):
    frames, tokens = stream.shape[0], text.shape[0]
    low, full = jnp.bfloat16, jnp.float32
    widths = {**{name: width for name, width, _ in SAVED}, **dict(GRADS), "hidden": FF}

    def height(name):
        return tokens if name in ("ckv", "g_ckv") else frames

    kept = [jax.ShapeDtypeStruct((height(name), widths[name]), low) for name in KEPT]
    shape = jax.ShapeDtypeStruct
    here, there = pl.BlockSpec(memory_space=pltpu.VMEM), pl.BlockSpec(memory_space=pl.ANY)
    scalar = pl.BlockSpec(memory_space=pltpu.SMEM)
    out = pl.pallas_call(
        model_kernel,
        out_shape=[
            shape((8, noise.shape[1]), full),
            shape((frames, D), full),
            shape((LAYERS, 8, D), full),
            shape((8, D), full),
            shape((D, noise.shape[1]), full),
        ]
        + kept * LAYERS,
        in_specs=[scalar, scalar] + [here] * 6 + [there] * (3 * LAYERS),
        out_specs=[here] * 5 + [there] * (len(KEPT) * LAYERS),
        scratch_shapes=[pltpu.VMEM((D, JOINT), low), pltpu.VMEM((text.shape[1], 2 * D), low), pltpu.VMEM((2 * D + FF, D), low)]
        + [pltpu.VMEM((height(name), width), kind) for name, width, kind in SAVED] * LAYERS
        + [pltpu.VMEM((height(name), width), low) for name, width in GRADS]
        + [
            pltpu.VMEM((frames, FF), low),
            pltpu.VMEM((frames, D), full),
            pltpu.VMEM((frames, D), low),
            pltpu.VMEM((frames, D), low),
            pltpu.SemaphoreType.DMA((len(PARTS),)),
            pltpu.SemaphoreType.DMA((LAYERS, len(KEPT))),
        ],
        compiler_params=pltpu.CompilerParams(vmem_limit_bytes=VMEM_LIMIT),
    )(lengths, factor, stream, mods, final_mods, text, noise, head, *[w for layer in weights for w in layer])
    head_part, rest = out[:5], out[5:]
    count = len(KEPT)
    return head_part, [dict(zip(KEPT, rest[l * count : (l + 1) * count])) for l in range(LAYERS)]


def adam_update(weight, grad, first, second, rate):
    first_new = BETA_ONE * first + (1.0 - BETA_ONE) * grad
    second_new = BETA_TWO * second + (1.0 - BETA_TWO) * grad * grad
    first_hat = first_new / (1.0 - BETA_ONE**STEP)
    second_hat = second_new / (1.0 - BETA_TWO**STEP)
    weight_new = weight - rate * (
        first_hat / (jnp.sqrt(second_hat) + ADAM_EPSILON) + WEIGHT_DECAY * weight
    )
    return (first_new, second_new, weight_new)


def tiles(values, lead=()):
    flat = values.reshape(lead + (-1,))
    short = -flat.shape[-1] % 1024
    flat = jnp.pad(flat, [(0, 0)] * len(lead) + [(0, short)])
    return flat.reshape(lead + (-1, 128))


def body(
    ways,
    clean_latent,
    noise,
    text_feats,
    text_lengths,
    timesteps,
    valid_frames,
    w_in,
    w_text,
    w_out,
    gains,
    w_lead,
    w_head,
    first_in,
    second_in,
    first_text,
    second_text,
    first_out,
    second_out,
    first_gains,
    second_gains,
    first_lead,
    second_lead,
    first_head,
    second_head,
):
    count = ways[0] * ways[1]
    own = w_head.shape[0]
    channels = noise.shape[-1]
    clean_latent, noise, text_low = clean_latent[0], noise[0], text_feats[0]
    frames, caption = clean_latent.shape[0], text_low.shape[0]
    frame_keep = lax.iota(jnp.int32, frames) < valid_frames[0]
    text_keep = lax.iota(jnp.int32, caption) < text_lengths[0]
    rows = [w_in.shape[1], w_text.shape[1], w_out.shape[1]]
    halves = [JOINT // 2, D, D // 2]
    aligned = all(height % 8 == 0 for height in rows) and ways[0] % 2 == 0 and ways[1] % 2 == 0

    def to_all(values, number):
        if aligned:
            return exchange(values, ways, True, number)
        return lax.all_gather(values, ALL, axis=0, tiled=False)

    def to_each(values, number):
        if aligned:
            return exchange(values, ways, False, number)
        return lax.all_to_all(values, ALL, 0, 0, tiled=True)

    sinus = time_features(timesteps)
    lead_low, head_low = to_low(w_lead), to_low(w_head)
    small = jnp.concatenate(
        [
            lead_low[FREQS:].astype(jnp.float32).reshape(-1),
            head_low[:, 3 * D :].astype(jnp.float32).reshape(-1),
            to_low(gains).astype(jnp.float32).reshape(-1),
        ]
    )
    facts = jnp.concatenate([to_low(sinus).astype(jnp.float32)[0], valid_frames.astype(jnp.float32)])
    packed = to_all(jnp.concatenate([tiles(facts), tiles(small)], 0), 3).reshape(count, -1)
    facts_size = 1024
    sinus_all = to_low(packed[:, :FREQS])
    frame_count = jnp.sum(packed[:, FREQS])
    small_all = packed[:, facts_size:]
    at = channels * own
    lead_in = to_low(small_all[:, :at].reshape(count, channels, own).transpose(1, 0, 2).reshape(channels, D))
    head_pred = to_low(small_all[:, at : 2 * at].reshape(D, channels))
    gains_all = small_all[:, 2 * at : 2 * at + LAYERS * own].reshape(count, LAYERS, own)
    gains_all = gains_all.transpose(1, 0, 2).reshape(LAYERS, D)

    act_time, pull_time = jax.vjp(jax.nn.silu, dense(sinus_all, lead_low[:FREQS]))
    act_low = to_low(act_time)
    temb_part = dense(act_low, head_low[:, :D]).reshape(count, count, own).transpose(1, 0, 2)
    temb = jnp.sum(to_each(tiles(temb_part, (count,)), 4), 0).reshape(-1)[:D].reshape(count, own)
    cond, pull_cond = jax.vjp(jax.nn.silu, temb)
    cond_low = to_low(cond)
    mod_low = jnp.concatenate(
        [to_low(w_in[layer, :, JOINT:]) for layer in range(LAYERS)] + [head_low[:, D : 3 * D]], 1
    )
    mod_part = dense(cond_low, mod_low)
    mods = jnp.sum(to_each(tiles(mod_part, (count,)), 5), 0).reshape(-1)[: mod_low.shape[1]]

    if aligned:
        items = plan(halves, range(LAYERS), GATHER_PATTERN)
        weights = gather_weights([w_in, w_text, w_out], halves, ways, 1, items)
    else:
        weights = [
            [
                lax.all_gather(to_low(shard[layer]), ALL, axis=0, tiled=True)
                for shard in (w_in[:, :, :JOINT], w_text, w_out)
            ]
            for layer in range(LAYERS)
        ]

    level = noise_level(timesteps)
    noisy_low = to_low(jnp.sqrt(level) * clean_latent + jnp.sqrt(1.0 - level) * noise)
    stream = dense(noisy_low, lead_in)
    block_mods = jnp.concatenate(
        [mods[: LAYERS * MOD].reshape(LAYERS, 6, D), gains_all[:, None], jnp.zeros((LAYERS, 1, D))], 1
    )
    final_mods = jnp.pad(mods[LAYERS * MOD :].reshape(2, D), [(0, 6), (0, 0)])
    short = [(0, 0), (0, 128 - channels)]
    (loss_lanes, grad_stream, grad_blocks, grad_final, grad_pred_w), kept = run_model(
        stream,
        block_mods,
        final_mods,
        text_low,
        jnp.pad(noise, short),
        jnp.pad(head_pred, short),
        jnp.concatenate([valid_frames, text_lengths]),
        (2.0 / frame_count).reshape(1),
        weights,
    )
    loss_part = jnp.sum(loss_lanes[0])
    grad_pred_w = grad_pred_w[:, :channels]
    grad_mods = [grad_blocks[:, :6].reshape(-1), grad_final[:2].reshape(-1)]
    grad_gains = grad_blocks[:, 6]
    grad_in_w = weight_grad(noisy_low, to_low(grad_stream))

    mods_all = to_all(tiles(to_low(jnp.concatenate(grad_mods)).astype(jnp.float32)), 6)
    mods_all = to_low(mods_all.reshape(count, -1)[:, : mod_low.shape[1]])
    grad_mod_w = weight_grad(cond_low, mods_all)
    (grad_temb,) = pull_cond(dense_back(mods_all, mod_low))
    small_grads = jnp.concatenate(
        [
            grad_in_w.reshape(channels, count, own).transpose(1, 0, 2).reshape(count, -1),
            grad_pred_w.reshape(count, -1),
            grad_gains.reshape(LAYERS, count, own).transpose(1, 0, 2).reshape(count, -1),
        ],
        1,
    )
    temb_tile = tiles(to_low(grad_temb).astype(jnp.float32))
    sent = jnp.concatenate(
        [jnp.broadcast_to(temb_tile[None], (count,) + temb_tile.shape), tiles(small_grads, (count,))], 1
    )
    got = to_each(sent, 7).reshape(count, -1)
    temb_all = to_low(got[:, :D].reshape(count, count, own).transpose(1, 0, 2).reshape(count, D))
    small_sum = jnp.sum(got[:, temb_tile.size :], 0)
    grad_time_two = weight_grad(act_low, temb_all)
    (grad_pre_time,) = pull_time(dense_back(temb_all, head_low[:, :D]))
    grad_time_one = weight_grad(sinus_all, to_low(grad_pre_time))

    if aligned:
        items = plan(halves, list(reversed(range(LAYERS))), SCATTER_PATTERN)
        sums = scatter_grads(kept, text_low, rows, halves, ways, 2, items)
    else:
        sums = [[], [], []]
        for k in kept:
            joint = [weight_grad(k[a], k[b]) for a, b in (("n1", "g_self"), ("n2", "g_cq"), ("n3", "g_pre"))]
            back = [weight_grad(k[a], k[b]) for a, b in (("mixed1", "g_one"), ("mixed2", "g_cross"), ("hidden", "g_three"))]
            grads = (jnp.concatenate(joint, 1), weight_grad(text_low, k["g_ckv"]), jnp.concatenate(back, 0))
            for member, grad in enumerate(grads):
                sums[member].append(lax.psum_scatter(grad, ALL, scatter_dimension=0, tiled=True))
        sums = [jnp.stack(part) for part in sums]
    mod_grads = grad_mod_w[:, : LAYERS * MOD].reshape(own, LAYERS, MOD).transpose(1, 0, 2)
    grad_list = [
        jnp.concatenate([sums[0], mod_grads], 2),
        sums[1],
        sums[2],
        small_sum[2 * at : 2 * at + LAYERS * own].reshape(LAYERS, own),
        jnp.concatenate([grad_time_one, small_sum[:at].reshape(channels, own)], 0),
        jnp.concatenate(
            [grad_time_two, grad_mod_w[:, LAYERS * MOD :], small_sum[at : 2 * at].reshape(own, channels)], 1
        ),
    ]
    local_squares = sum((jnp.sum(item * item) for item in grad_list))
    totals = jnp.sum(to_all(tiles(jnp.stack([loss_part, local_squares])), 8), 0).reshape(-1)
    loss_sum = totals[0]
    grad_norm = jnp.sqrt(totals[1])
    factor = CLIP_NORM / jnp.maximum(grad_norm, CLIP_NORM)
    params = (w_in, w_text, w_out, gains, w_lead, w_head)
    firsts = (first_in, first_text, first_out, first_gains, first_lead, first_head)
    seconds = (second_in, second_text, second_out, second_gains, second_lead, second_head)
    rates = (LEARN_RATE, LEARN_RATE, LEARN_RATE, GAIN_RATE, LEARN_RATE, LEARN_RATE)
    results = []
    for weight, grad, first, second, rate in zip(params, grad_list, firsts, seconds, rates):
        results.extend(adam_update(weight, grad * factor, first, second, rate))
    return (loss_sum, frame_count, grad_norm, *results)


def solution(mesh):
    ways = (mesh.shape["dp"], mesh.shape["fsdp"])
    clips = [P(ALL, None, None)] * 3 + [P(ALL)] * 3
    weights = [P(None, ALL, None)] * 3 + [P(None, ALL)] * 2 + [P(ALL, None)]
    moments = [spec for spec in weights for _ in range(2)]
    results = [spec for spec in weights for _ in range(3)]
    return jax.shard_map(
        functools.partial(body, ways),
        mesh=mesh,
        in_specs=tuple(clips + weights + moments),
        out_specs=tuple([P()] * 3 + results),
        check_vma=False,
    )
```

time: 870 us -> 726 us (0.83)
  matrix products: 193 us -> 3.62 us
  Pallas kernels: 515 us -> 647 us
  other arithmetic: 76.3 us -> 36.1 us
  local copies, waits for them, and re-layouts: 60.1 us -> 20.8 us
    pallas_call x0 -> x1, Pallas kernels: none -> 130 us  [run_model(): pl.pallas_call(model_kernel, out_shape=[shape((8, noise.shape[1]), full),...]
    dot_general x19 -> x4, matrix products: 47 us -> 2 us  [dense(): return jnp.dot(left, right, preferred_element_type=jnp.float32)]
    dot_general x14 -> x1, matrix products: 45.1 us -> 0.31 us  [dense_back(): lax.dot_general(left, right, (((1,), (1,)), ((), ())), preferred_element_...]
    dot_general x19 -> x4, matrix products: 43.5 us -> 1.31 us  [weight_grad(): lax.dot_general(left, right, (((0,), (0,)), ((), ())), preferred_element_...]
    dot_general x20 -> x0, matrix products: 39.9 us -> none  [the longest x4 16.3 us: attention_back(): jnp.einsum('qhd,khd->hqk', grad_heads, split_heads(values), preferred_ele...]
    unnamed x621 -> x45, local copies, waits for them, and re-layouts: 26.9 us -> 8.15 us
    sub x4 -> x0, matrix products: 17.8 us -> none  [attention(): shifted = jnp.exp(scores - jnp.max(scores, -1, keepdims=True))]
    convert_element_type x18 -> x9, local copies, waits for them, and re-layouts: 16.4 us -> 1.56 us  [to_low(): return values.astype(jnp.bfloat16)]
where the time goes in v2:
time: 726 us; the launch traced here: 718 us
  Pallas kernels  647 us (89%)
  other arithmetic  36.1 us (5%)
  local copies, waits for them, and re-layouts  20.8 us (3%)
  between operations  10.2 us (1%)
    pallas_call x1, Pallas kernels, gather_weights(): pl.pallas_call(functools.partial(gather_kernel, ways, rows, halves, items...  199 us
    pallas_call x1, Pallas kernels, scatter_grads(): pl.pallas_call(functools.partial(scatter_kernel, ways, rows, halves, item...  193 us
    pallas_call x1, Pallas kernels, run_model(): pl.pallas_call(model_kernel, out_shape=[shape((8, noise.shape[1]), full),...  130 us
    pallas_call x6, Pallas kernels, exchange(): pl.pallas_call(functools.partial(exchange_kernel, ways, shared), out_shap...  126 us

profile of v2, /device:TPU:0, one launch (start us, length us, event | category | flops | bytes accessed | tf_op | source)
XLA Modules:
  0.0 717.9 jit_solution(15509017186671054243)
XLA Ops:
  9.4 13.7 %shard_map.391 = f32[32,16,128]{2,1,0:T(8,128)} custom-call(f32[16,128]{1,0:T(8,128)} %pad_maximum_fusion.9.x_ref), custom_call_target="tpu_custom_call" | custom-call | tf_op jit(solution)/shard_map/pallas_call | solution.py:121
  23.1 1.0 copy.99
  24.3 1.0 copy.98
  30.3 11.7 %shard_map.392 = f32[32,8,128]{2,1,0:T(8,128)} custom-call(f32[32,8,128]{2,1,0:T(8,128)} %bitcast.119), custom_call_target="tpu_custom_call" | custom-call | tf_op jit(solution)/shard_map/pallas_call | solution.py:121
  43.1 1.3 fusion.22.refs_2_
  45.0 1.4 copy.75
  46.4 32.5 %shard_map.393 = f32[32,88,128]{2,1,0:T(8,128)} custom-call(f32[32,88,128]{2,1,0:T(8,128)} %bitcast.100), custom_call_target="tpu_custom_call" | custom-call | tf_op jit(solution)/shard_map/pallas_call | solution.py:121
  78.9 1.4 reduce_sum.110
  81.7 199.1 %shard_map.394 = (bf16[4,2,2,48,6144]{4,3,2,1,0:T(8,128)(2,1)}, bf16[4,2,2,64,1536]{4,3,2,1,0:T(8,128)(2,1)}, bf16[4,2,2,288,768]{4,3,2,1,0:T(8,128)(2,1)}, bf16...) custom-call(f32[2,24,10752]{2,1,0:T(8,128)} %refs_0_.1, ...), custom_call_target="tpu_custom_call" | custom-call | tf_op jit(solution)/shard_map/pallas_call | solution.py:266
  280.8 129.5 %shard_map.395 = (f32[8,128]{1,0:T(8,128)}, f32[320,768]{1,0:T(8,128)}, f32[2,8,768]{2,1,0:T(8,128)}, f32[8,768]{1,0:T(8,128)}, f32[768,128]{1,0:T(8,128)}, /*in...) custom-call(s32[2]{0:T(128)} %pad_add_fusion.refs_0_, ...), custom_call_target="tpu_custom_call" | custom-call | tf_op jit(solution)/shard_map/pallas_call | solution.py:1070
  410.3 1.3 slice_reduce_fusion.3
  414.9 1.2 reshape.242
  416.1 1.3 convert_bitcast_fusion
  418.8 34.7 %shard_map.397 = f32[32,88,128]{2,1,0:T(8,128)} custom-call(f32[88,128]{1,0:T(8,128)} %fusion.20.x_ref), custom_call_target="tpu_custom_call" | custom-call | tf_op jit(solution)/shard_map/pallas_call | solution.py:121
  453.5 1.5 convert.52
  456.4 21.2 %shard_map.398 = f32[32,16,128]{2,1,0:T(8,128)} custom-call(f32[32,16,128]{2,1,0:T(8,128)} %pad_maximum_fusion.2.x_ref), custom_call_target="tpu_custom_call" | custom-call | tf_op jit(solution)/shard_map/pallas_call | solution.py:121
  477.5 1.0 copy.97
  482.6 192.9 %shard_map.396 = (f32[2,24,6144]{2,1,0:T(8,128)}, f32[2,32,1536]{2,1,0:T(8,128)}, f32[2,144,768]{2,1,0:T(8,128)}) custom-call(bf16[256,1024]{1,0:T(8,128)(2,1)} %bitcast.111, bf16[320,768]{1,0:T(8,128)(2,1)} %get-tuple-element.68.refs_1_, bf16[320,768]{1,0:T(8,128)(2,1)} %get-tuple-element.69.refs_2_, bf16[320,768]{1,0:T(8,128)(2,1)} %get-tuple-element.70.refs_3_, ...), custom_call_target="tpu_custom_call" | custom-call | tf_op jit(solution)/shard_map/pallas_call | solution.py:567
  675.5 2.1 multiply_reduce_fusion.1
  677.6 1.7 multiply_reduce_fusion.2
  679.3 1.1 multiply_reduce_fusion
  684.4 1.3 fusion.44.x_ref
  685.7 11.8 %shard_map.399 = f32[32,8,128]{2,1,0:T(8,128)} custom-call(f32[8,128]{1,0:T(8,128)} %fusion.44.x_ref), custom_call_target="tpu_custom_call" | custom-call | tf_op jit(solution)/shard_map/pallas_call | solution.py:121
  697.5 1.5 reduce_sum.119
  699.1 1.3 fusion.66
  702.5 1.4 multiply_subtract_fusion.5
  703.8 1.5 multiply_subtract_fusion.4
  705.4 2.1 multiply_subtract_fusion.3
  707.5 1.2 multiply_subtract_fusion.2
  708.7 2.0 multiply_subtract_fusion.1
  710.8 1.0 copy-done.5
  712.5 3.9 multiply_subtract_fusion
  (126 shorter events, 26.1 us)
Async XLA Ops:
  28.6 15.8 %copy-start = (f32[2,24,10752]{2,1,0:T(8,128)S(1)}, f32[2,24,10752]{2,1,0:T(8,128)}, u32[]{:S(2)}) copy-start(f32[2,24,10752]{2,1,0:T(8,128)} %refs_0_.1) | copy-start | bytes 6193156
  479.6 2.9 copy-start.15
  480.7 1.8 copy-start.16
  675.5 3.9 copy-start.2
  675.5 29.8 %copy-start.9 = (f32[24,2324]{1,0:T(8,128)S(1)}, f32[24,2324]{1,0:T(8,128)}, u32[]{:S(2)}) copy-start(f32[24,2324]{1,0:T(8,128)} %param.35) | copy-start | bytes 669316
  675.5 29.8 %copy-start.14 = (f32[24,2324]{1,0:T(8,128)S(1)}, f32[24,2324]{1,0:T(8,128)}, u32[]{:S(2)}) copy-start(f32[24,2324]{1,0:T(8,128)} %param.47) | copy-start | bytes 669316
  679.3 28.1 %copy-start.7 = (f32[2,32,1536]{2,1,0:T(8,128)S(1)}, f32[2,32,1536]{2,1,0:T(8,128)}, u32[]{:S(2)}) copy-start(f32[2,32,1536]{2,1,0:T(8,128)} %refs_1_.1) | copy-start | bytes 1179652
  679.3 28.1 %copy-start.8 = (f32[2,32,1536]{2,1,0:T(8,128)S(1)}, f32[2,32,1536]{2,1,0:T(8,128)}, u32[]{:S(2)}) copy-start(f32[2,32,1536]{2,1,0:T(8,128)} %get-tuple-element.97) | copy-start | bytes 1179652
  702.5 5.0 copy-start.12
  702.5 5.0 copy-start.13
  705.3 3.4 copy-start.3
  705.3 3.4 copy-start.4
  705.3 3.3 copy-start.10
  705.4 3.3 copy-start.11
  708.7 2.1 copy-start.1
  708.7 3.2 copy-start.5
  708.7 3.8 copy-start.6

commit v3 on v2

--- a/solution.py
+++ b/solution.py
@@ -74,67 +74,195 @@
     )
 
 
-def exchange_kernel(ways, shared, x_ref, out_ref, send_sem, recv_sem):
-    dp_ways, fsdp_ways = ways
-    count = dp_ways * fsdp_ways
-    me = lax.axis_index("dp") * fsdp_ways + lax.axis_index("fsdp")
-
-    def device(index):
-        return (index // fsdp_ways, lax.rem(index, fsdp_ways))
-
+def greet_all(ways, me):
+    count = ways[0] * ways[1]
     barrier = pltpu.get_barrier_semaphore()
     for step in range(1, count):
         pl.semaphore_signal(
-            barrier, inc=1, device_id=device(lax.rem(me + step, count)), device_id_type=MESH
+            barrier, inc=1, device_id=numbered(ways, lax.rem(me + step, count)), device_id_type=MESH
         )
     pl.semaphore_wait(barrier, count - 1)
 
-    def copy(step):
-        other = lax.rem(me + step, count)
-        return remote(
-            x_ref if shared else x_ref.at[other],
-            out_ref.at[me],
-            send_sem.at[step],
-            recv_sem.at[step],
-            device(other),
-        )
-
-    for step in range(1, count):
-        copy(step).start()
-    out_ref[me] = x_ref[...] if shared else x_ref[me]
-    for step in range(1, count):
-        origin = lax.rem(me + count - step, count)
-        remote(
-            x_ref if shared else x_ref.at[0],
-            out_ref.at[origin],
-            send_sem.at[step],
-            recv_sem.at[step],
-            device(origin),
-        ).wait_recv()
-    for step in range(1, count):
-        copy(step).wait_send()
-
-
-def exchange(values, ways, shared, number):
-    count = ways[0] * ways[1]
-    tile = values.shape if shared else values.shape[1:]
-    return pl.pallas_call(
-        functools.partial(exchange_kernel, ways, shared),
-        out_shape=jax.ShapeDtypeStruct((count,) + tile, values.dtype),
-        in_specs=[pl.BlockSpec(memory_space=pltpu.VMEM)],
-        out_specs=pl.BlockSpec(memory_space=pltpu.VMEM),
-        scratch_shapes=[pltpu.SemaphoreType.DMA((count,)), pltpu.SemaphoreType.DMA((count,))],
-        compiler_params=pltpu.CompilerParams(
-            collective_id=number, has_side_effects=True, vmem_limit_bytes=VMEM_LIMIT
-        ),
-    )(values)
-
-
-def gather_kernel(ways, rows, halves, items, layers, *refs):
+
+def numbered(ways, index):
+    return (index // ways[1], lax.rem(index, ways[1]))
+
+
+ROUNDS = ("core", 2, 1, 0)
+
+
+class Hops:
+    def __init__(self, sizes, spot, core):
+        self.sizes, self.spot, self.core = sizes, spot, core
+
+    def count(self, axis):
+        return 2 if axis == "core" else self.sizes[axis]
+
+    def place(self, axis):
+        return self.core if axis == "core" else self.spot[axis]
+
+    def other(self, axis, steps):
+        if axis == "core":
+            return 1 - self.core, device_at(self.spot, 1 - self.core)
+        spot = moved(self.spot, axis, self.sizes[axis], steps)
+        return spot[axis], device_at(spot, self.core)
+
+
+def sum_steps(hops, totals, landed, send_sem, recv_sem, sent):
+    first = [sum(hops.count(axis) - 1 for axis in ROUNDS[:turn]) for turn in range(len(ROUNDS))]
+
+    def copies(turn):
+        axis = ROUNDS[turn]
+        return [
+            remote(
+                totals.at[turn], landed.at[first[turn] + steps - 1],
+                send_sem.at[turn, steps - 1], recv_sem.at[turn, steps - 1], hops.other(axis, steps)[1],
+            )
+            for steps in range(1, hops.count(axis))
+        ]
+
+    def begin(turn):
+        for copy in copies(turn):
+            copy.start()
+            sent.append(copy)
+
+    def go_on(turn):
+        for copy in copies(turn):
+            copy.wait_recv()
+        total = totals[turn]
+        for steps in range(1, hops.count(ROUNDS[turn])):
+            total = total + landed[first[turn] + steps - 1]
+        totals[turn + 1] = total
+        if turn + 1 < len(ROUNDS):
+            begin(turn + 1)
+
+    return [lambda: begin(0)] + [functools.partial(go_on, turn) for turn in range(len(ROUNDS))]
+
+
+def split_steps(hops, rows, landed, out, send_sem, recv_sem, sent):
+    places = {"core": 3, 2: 2, 1: 1, 0: 0}
+
+    def index(turn, place_on):
+        at = [slice(None)] * 4
+        for early in ROUNDS[:turn]:
+            at[places[early]] = hops.place(early)
+        at[places[ROUNDS[turn]]] = place_on
+        return tuple(at)
+
+    def copies(turn):
+        axis = ROUNDS[turn]
+        made = []
+        for steps in range(1, hops.count(axis)):
+            place_on, device = hops.other(axis, steps)
+            made.append(
+                remote(
+                    rows.at[index(turn, place_on)], landed[turn].at[steps - 1],
+                    send_sem.at[turn, steps - 1], recv_sem.at[turn, steps - 1], device,
+                )
+            )
+        return made
+
+    def begin(turn):
+        for copy in copies(turn):
+            copy.start()
+            sent.append(copy)
+
+    def go_on(turn):
+        for copy in copies(turn):
+            copy.wait_recv()
+        axis = ROUNDS[turn]
+        mine = rows.at[index(turn, hops.place(axis))]
+        others = range(hops.count(axis) - 1)
+        if turn == 3:
+            out[...] = sum((landed[turn][k] for k in others), mine[...])
+        else:
+
+            @pl.loop(0, hops.sizes[0])
+            def _(z):
+                mine[z] = sum((landed[turn][k, z] for k in others), mine[z])
+
+            begin(turn + 1)
+
+    return [lambda: begin(0)] + [functools.partial(go_on, turn) for turn in range(len(ROUNDS))]
+
+
+def split_shapes(sizes, tile):
+    z, y, x = sizes
+    return [
+        pltpu.VMEM((1, z, y, x) + tile, jnp.float32),
+        pltpu.VMEM((x - 1, z, y) + tile, jnp.float32),
+        pltpu.VMEM((y - 1, z) + tile, jnp.float32),
+        pltpu.VMEM((z - 1,) + tile, jnp.float32),
+    ]
+
+
+def spread_steps(hops, rows, send_sem, recv_sem, sent):
+    turns = (0, 2, 1, "core")
+    places = {"core": 3, 2: 2, 1: 1, 0: 0}
+
+    def index(turn, place_on):
+        at = [hops.spot[0], hops.spot[1], hops.spot[2], hops.core]
+        for early in turns[:turn]:
+            at[places[early]] = slice(None)
+        at[places[turns[turn]]] = place_on
+        return tuple(at)
+
+    def copies(turn, origin):
+        axis = turns[turn]
+        made = []
+        for steps in range(1, hops.count(axis)):
+            device = hops.other(axis, steps)[1]
+            place_on = hops.other(axis, hops.count(axis) - steps)[0] if origin else hops.place(axis)
+            part = rows.at[index(turn, place_on)]
+            made.append(remote(part, part, send_sem.at[turn, steps - 1], recv_sem.at[turn, steps - 1], device))
+        return made
+
+    def begin(turn):
+        for copy in copies(turn, False):
+            copy.start()
+            sent.append(copy)
+
+    def go_on(turn):
+        for copy in copies(turn, True):
+            copy.wait_recv()
+        if turn + 1 < len(turns):
+            begin(turn + 1)
+
+    return [lambda: begin(0)] + [functools.partial(go_on, turn) for turn in range(len(turns))]
+
+
+def sigmoid(values):
+    return 1.0 / (1.0 + jnp.exp(-values))
+
+
+def chosen(me, own, width):
+    shape = (D, width)
+    row, column = (lax.broadcasted_iota(jnp.int32, shape, axis) for axis in range(2))
+    return jnp.logical_and(row == me * own + column, column < own).astype(jnp.float32)
+
+
+SHARE = 32
+MOD_ROWS = (LAYERS * MOD + 2 * D) // 128
+MOD_TILE = (-(-MOD_ROWS // 8) * 8, 128)
+
+
+def gather_kernel(ways, rows, halves, items, layers, own, *refs):
     members = len(rows)
-    shards = refs[:members]
-    fulls = refs[members : members + members * layers]
-    rest = refs[members + members * layers :]
+    refs = list(refs)
+
+    def take(count):
+        taken = refs[:count]
+        del refs[:count]
+        return taken
+
+    shards = take(members)
+    facts_in, lead_own, head_own, mod_own = take(4)
+    fulls = take(members * layers)
+    facts, pre_time, temb_own, mods = take(4)
+    totals, landed, mod_parts = take(3)
+    mod_landed = take(4)
+    facts_send, facts_recv, sum_send, sum_recv, split_send, split_recv = take(6)
+    rest = refs
     stages = rest[:members]
     blocks = rest[members : 2 * members]
     pre_send, pre_recv, own_sem, put_sem, *sends, c_send, c_recv = rest[2 * members :]
@@ -142,7 +270,19 @@
     sizes, spot, core = place(ways)
     z, y, x = spot
     partner = device_at(spot, 1 - core)
-    greet_peers(sizes, spot, core)
+    count = ways[0] * ways[1]
+    me = lax.axis_index("dp") * ways[1] + lax.axis_index("fsdp")
+    greet_all(ways, me)
+
+    def facts_copy(step):
+        return remote(
+            facts_in, facts.at[me], facts_send.at[step], facts_recv.at[step],
+            numbered(ways, lax.rem(me + step, count)),
+        )
+
+    for step in range(1, count):
+        facts_copy(step).start()
+    facts[me] = facts_in[...]
 
     def full(layer, member):
         return fulls[layer * members + member]
@@ -239,57 +379,112 @@
             land = region(i, 2, lax.rem(spot[axis] + sizes[axis] - steps, sizes[axis]), 1 - core)
             remote(land, land, c_send.at[i, steps], c_recv.at[i, steps], partner).wait_recv()
 
+    hops = Hops(sizes, spot, core)
+
+    def time_layers():
+        for step in range(1, count):
+            origin = lax.rem(me + count - step, count)
+            remote(
+                facts_in, facts.at[origin], facts_send.at[step], facts_recv.at[step], numbered(ways, origin)
+            ).wait_recv()
+        value = dot_nn(to_low(facts[:, 0, :]), lead_own[:128, :]) + dot_nn(to_low(facts[:, 1, :]), lead_own[128:, :])
+        pre_time[...] = value
+        totals[0] = dot_nn(to_low(value * sigmoid(value))[:, :SHARE], head_own[...])
+        sums[0]()
+
+    def modulation():
+        temb = lax.dot_general(
+            totals[4], chosen(me, own, 128), (((1,), (0,)), ((), ())),
+            precision=lax.Precision.HIGHEST, preferred_element_type=jnp.float32,
+        )
+        temb_own[...] = temb
+        cond = to_low(temb * sigmoid(temb))[:, :SHARE]
+        mod_parts[:, MOD_ROWS:, :] = jnp.zeros((count, MOD_TILE[0] - MOD_ROWS, 128), jnp.float32)
+        for j in range(0, MOD_ROWS, 4):
+            part = dot_nn(cond, mod_own[:, j * 128 : (j + 4) * 128])
+            for k in range(4):
+                mod_parts[:, j + k, :] = part[:, k * 128 : (k + 1) * 128]
+        splits[0]()
+
+    sums = sum_steps(hops, totals, landed, sum_send, sum_recv, sent_all)
+    splits = split_steps(
+        hops, mod_parts.reshape(sizes + (2,) + MOD_TILE), mod_landed, mods, split_send, split_recv, sent_all
+    )
+    side = [time_layers] + sums[1:] + [modulation] + splits[1:]
     for i, phase in schedule(items, GATHER_LAGS):
+        if phase == 1 and side:
+            side.pop(0)()
         if phase > 0:
             finish(i, phase - 1)
         if phase < 3:
             start(i, phase)
     for i in range(len(items)):
         c_wait(i)
+    for step in side:
+        step()
     for layer in range(layers):
         for member in range(members):
             own_put(layer, member)
+    for step in range(1, count):
+        facts_copy(step).wait_send()
     for sent, _ in pre:
         sent.wait_send()
     for copy in sent_all:
         copy.wait_send()
 
 
-def gather_weights(shards, halves, ways, number, items):
+def gather_weights(shards, facts, lead_own, head_own, mod_own, own, halves, ways, number, items):
     layers = shards[0].shape[0]
     rows = [s.shape[1] for s in shards]
     members = len(shards)
     sizes = (ways[0] // 2, 2, ways[1] // 2)
+    devices = ways[0] * ways[1]
     count = layers * members
     n = len(items)
-    sem = pltpu.SemaphoreType.DMA
+    sem, vmem, full = pltpu.SemaphoreType.DMA, pltpu.VMEM, jnp.float32
+    here, there = pl.BlockSpec(memory_space=pltpu.VMEM), pl.BlockSpec(memory_space=pl.ANY)
     out = pl.pallas_call(
-        functools.partial(gather_kernel, ways, rows, halves, items, layers),
+        functools.partial(gather_kernel, ways, rows, halves, items, layers, own),
         out_shape=[
             jax.ShapeDtypeStruct(sizes + (2 * rows[m], 2 * halves[m]), jnp.bfloat16)
             for _ in range(layers)
             for m in range(members)
+        ]
+        + [
+            jax.ShapeDtypeStruct((devices,) + facts.shape, full),
+            jax.ShapeDtypeStruct((devices, 128), full),
+            jax.ShapeDtypeStruct((devices, 128), full),
+            jax.ShapeDtypeStruct(MOD_TILE, full),
         ],
-        in_specs=[pl.BlockSpec(memory_space=pl.ANY)] * members,
-        out_specs=[pl.BlockSpec(memory_space=pl.ANY)] * count,
-        scratch_shapes=[pltpu.VMEM((layers, 2 * rows[m], halves[m]), jnp.float32) for m in range(members)]
-        + [pltpu.VMEM((layers, 2 * rows[m], halves[m]), jnp.bfloat16) for m in range(members)]
+        in_specs=[there] * members + [here] * 4,
+        out_specs=[there] * count + [here] * 4,
+        scratch_shapes=[
+            vmem((len(ROUNDS) + 1, devices, D), full),
+            vmem((sizes[0] + sizes[1] + sizes[2] - 2, devices, D), full),
+            vmem((devices,) + MOD_TILE, full),
+        ]
+        + split_shapes(sizes, MOD_TILE)
+        + [sem((devices,))] * 2
+        + [sem((len(ROUNDS), max(sizes)))] * 4
+        + [vmem((layers, 2 * rows[m], halves[m]), full) for m in range(members)]
+        + [vmem((layers, 2 * rows[m], halves[m]), jnp.bfloat16) for m in range(members)]
         + [sem((count,))] * 4
         + [sem((n, max(sizes)))] * 8,
         compiler_params=pltpu.CompilerParams(
             collective_id=number, has_side_effects=True, vmem_limit_bytes=VMEM_LIMIT
         ),
-    )(*shards)
-    return [
+    )(*shards, facts, lead_own, head_own, mod_own)
+    weights = [
         [out[l * members + m].reshape(-1, 2 * halves[m]) for m in range(members)] for l in range(layers)
     ]
+    return weights, *out[count:]
 
 
 ORDERS = ((0, 2, 1), (0, 1, 2), (2, 0, 1), (1, 0, 2))
-GATHER_LAGS = ((-3.0, 0.0, 2.0, 4.0), (-3.0, 0.0, 2.0, 4.0))
-SCATTER_LAGS = ((-2.0, 0.0, 2.0, 4.0, 6.0), (-2.0, 0.0, 2.0, 4.0, 6.0))
-GATHER_PATTERN = (0, 1)
-SCATTER_PATTERN = (0, 1)
+GATHER_LAGS = ((-1.5, 0.0, 3.0, 7.5), (-3.0, 0.0, 2.0, 6.5))
+SCATTER_LAGS = ((-2.0, 0.0, 4.5, 7.5, 9.0), (-2.0, 0.0, 4.5, 6.5, 9.5))
+GATHER_PATTERN = (1, 0, 1, 2, 1, 1, 0, 1, 0, 1, 2, 1, 2, 1, 3, 1, 2, 1)
+SCATTER_PATTERN = GATHER_PATTERN[::-1]
 
 
 def schedule(items, lags):
@@ -310,10 +505,11 @@
     return items
 
 
+RINGS = (2, 1, 1)
 ACTS = ("n1", "n2", "n3", "mixed1", "mixed2", "hidden", "g_self", "g_cq", "g_pre", "g_ckv", "g_one", "g_cross", "g_three")
 
 
-def scatter_kernel(ways, rows, halves, items, layers, *refs):
+def scatter_kernel(ways, rows, halves, items, layers, own, *refs):
     members = len(rows)
     n = len(items)
     rest = list(refs)
@@ -325,12 +521,18 @@
 
     (text_in,) = take(1)
     acts = [dict(zip(ACTS, take(len(ACTS)))) for _ in range(layers)]
+    mods_in, small_in, loss_in, facts, pre_time, temb_own, head_own, mod_own = take(8)
     outs = take(members)
+    grad_mod, grad_time_one, grad_time_two, small_out, final = take(5)
+    all_mods, small_rows, totals, landed, squares = take(5)
+    small_landed = take(4)
+    spread_send, spread_recv, sum_send, sum_recv, split_send, split_recv, end_send, end_recv = take(8)
+    ends, end_landed = take(2)
     lefts, rights, text, right_text, hidden, mixes, right_out = take(7)
     ring = take(members)
     whole = take(n)
     parts = [take(n) for _ in range(3)]
-    sums = take(n)
+    partial = take(n)
     load_sem, c_send, c_recv, *sems, e_send, e_recv, o_sem = rest
     sends, recvs = sems[0::2], sems[1::2]
     sizes, spot, core = place(ways)
@@ -338,6 +540,61 @@
     greet_peers(sizes, spot, core)
     frames = hidden.shape[0]
     sent_all = []
+    me = lax.axis_index("dp") * ways[1] + lax.axis_index("fsdp")
+    hops = Hops(sizes, spot, core)
+    squares[...] = jnp.zeros_like(squares)
+
+    def count_squares(value):
+        squares[...] += jnp.broadcast_to(jnp.sum(value * value, (0, 1), keepdims=True), squares.shape)
+
+    temb = temb_own[...]
+    share = sigmoid(temb)
+    cond = to_low(temb * share)[:, :SHARE]
+    gate = sigmoid(pre_time[...])
+    act = to_low(pre_time[...] * gate)[:, :SHARE]
+    slope_temb = (share * (1.0 + temb * (1.0 - share)))[:, :SHARE]
+    slope_time = (gate * (1.0 + pre_time[...] * (1.0 - gate)))[:, :SHARE]
+    all_mods[me] = mods_in[...]
+    sums = sum_steps(hops, totals, landed, sum_send, sum_recv, sent_all)
+    spreads = spread_steps(
+        hops, all_mods.reshape(sizes + (2,) + MOD_TILE), spread_send, spread_recv, sent_all
+    )
+    tile = tuple(small_in.shape[1:])
+    splits = split_steps(
+        hops, small_rows.reshape(sizes + (2,) + tile), small_landed, small_out, split_send, split_recv, sent_all
+    )
+
+    def begin_small():
+        small_rows[...] = small_in[...]
+        splits[0]()
+
+    def modulation_back():
+        back = jnp.zeros((all_mods.shape[0], SHARE), jnp.float32)
+        for j in range(MOD_ROWS):
+            cols = slice(j * 128, (j + 1) * 128)
+            grad = to_low(all_mods[:, j, :])
+            back = back + dot_nt(grad, mod_own[:, cols])
+            grad_mod[:, cols] = dot_tn(cond, grad)
+        grad_temb = to_low(back * slope_temb)
+        pick = to_low(chosen(me, own, SHARE))
+        totals[0] = dot_nt(grad_temb, pick)
+        for column in range(0, MOD_ROWS * 128, MOD):
+            count_squares(grad_mod[:, column : min(column + MOD, MOD_ROWS * 128)])
+        sums[0]()
+
+    def time_back():
+        grad_temb = to_low(totals[4])
+        grad_time_two[...] = dot_tn(act, grad_temb)
+        grad_time = to_low(dot_nt(grad_temb, head_own[...]) * slope_time)
+        for j in range(2):
+            grad_time_one[j * 128 : (j + 1) * 128, :] = dot_tn(to_low(facts[:, j, :]), grad_time)
+        count_squares(grad_time_two[...])
+        count_squares(grad_time_one[...])
+        count_squares(small_out[...])
+
+    side = [spreads[0], begin_small]
+    side += [step for pair in zip(spreads[1:], splits[1:]) for step in pair]
+    side += [modulation_back] + sums[1:] + [time_back]
 
     def send(copy):
         copy.start()
@@ -414,14 +671,14 @@
 
     def c_copy(i):
         member, size = items[i][1], items[i][3]
-        slot = ring_at[i] % 2
+        slot = ring_at[i] % RINGS[member]
         return remote(ring[member].at[slot, :, pl.ds(0, size)], whole[i], c_send.at[i], c_recv.at[i], partner)
 
     def give(i):
         member, size = items[i][1], items[i][3]
-        slot = ring_at[i] % 2
-        if ring_at[i] >= 2:
-            c_copy(used[member][ring_at[i] - 2]).wait_send()
+        slot = ring_at[i] % RINGS[member]
+        if ring_at[i] >= RINGS[member]:
+            c_copy(used[member][ring_at[i] - RINGS[member]]).wait_send()
         target = ring[member].at[slot]
 
         def store(at, value):
@@ -473,7 +730,7 @@
 
     def owned(i, side):
         height = rows[items[i][1]]
-        return sums[i].at[pl.ds(pl.multiple_of(side * height, 8), height)]
+        return partial[i].at[pl.ds(pl.multiple_of(side * height, 8), height)]
 
     def e_copy(i):
         layer, member = items[i][:2]
@@ -500,7 +757,9 @@
             return value
 
         if phase == 2:
-            sums[i][...] = total((Ellipsis,))
+            pieces_sum = total((Ellipsis,))
+            partial[i][...] = pieces_sum
+            count_squares(pieces_sum)
             e_copy(i).start()
             o_copy(i).start()
         else:
@@ -516,23 +775,32 @@
         if step == 0:
             give(i)
             continue
+        if step in (1, 2) and side:
+            side.pop(0)()
         if step == 1:
             combine(i)
         else:
             finish(i, step - 2)
         if step < 4:
             start(i, step - 1)
+    for step in side:
+        step()
+    lane = lax.broadcasted_iota(jnp.int32, squares.shape, 0)
+    ends[0] = jnp.where(lane == 0, squares[...], loss_in[...])
+    for step in sum_steps(hops, ends, end_landed, end_send, end_recv, sent_all):
+        step()
+    final[...] = ends[len(ROUNDS)]
     for i in range(n):
         e_copy(i).wait()
         o_copy(i).wait()
     for member in range(members):
-        for i in used[member][-2:]:
+        for i in used[member][-RINGS[member] :]:
             c_copy(i).wait_send()
     for copy in sent_all:
         copy.wait_send()
 
 
-def scatter_grads(kept, text, rows, halves, ways, number, items):
+def scatter_grads(kept, text, rest, own, rows, halves, ways, number, items):
     layers, members = len(kept), len(rows)
     sizes = (ways[0] // 2, 2, ways[1] // 2)
     n = len(items)
@@ -549,7 +817,19 @@
         left = tuple(sizes[axis] for axis in range(3) if axis not in order[: phase + 1])
         return vmem((sizes[order[phase]] - 1, *left, 2 * rows[member], size), low)
 
+    full, devices = jnp.float32, 2 * chips
+    tile = tuple(rest[1].shape[1:])
+    sums = sem((len(ROUNDS), max(sizes)))
     scratch = [
+        vmem((devices,) + MOD_TILE, full),
+        vmem((devices,) + tile, full),
+        vmem((len(ROUNDS) + 1, devices, D), full),
+        vmem((sizes[0] + sizes[1] + sizes[2] - 2, devices, D), full),
+        vmem((8, 128), full),
+    ]
+    scratch += split_shapes(sizes, tile) + [sums] * 8
+    scratch += [vmem((len(ROUNDS) + 1, 8, 128), full), vmem((sizes[0] + sizes[1] + sizes[2] - 2, 8, 128), full)]
+    scratch += [
         vmem((3, frames, D), low),
         vmem((8, frames, D), low),
         vmem(text.shape, low),
@@ -558,24 +838,32 @@
         vmem((2, frames, D), low),
         vmem((2, 3, frames, D // 2), low),
     ]
-    scratch += [vmem((2, chips * 2 * rows[m], most[m]), low) for m in range(members)]
+    scratch += [vmem((RINGS[m], chips * 2 * rows[m], most[m]), low) for m in range(members)]
     scratch += [vmem((chips * 2 * rows[m], s), low) for _, m, _, s, _ in items]
     scratch += [part(item, phase) for phase in range(3) for item in items]
     scratch += [vmem((2 * rows[m], s), jnp.float32) for _, m, _, s, _ in items]
     scratch += [sem((layers, members, 11))] + [sem((n,))] * 2 + [sem((n, max(sizes)))] * 6 + [sem((n,))] * 3
     flat = [text] + [k[name] for k in kept for name in ACTS]
+    here, there = pl.BlockSpec(memory_space=vmem), pl.BlockSpec(memory_space=pl.ANY)
     return pl.pallas_call(
-        functools.partial(scatter_kernel, ways, rows, halves, items, layers),
+        functools.partial(scatter_kernel, ways, rows, halves, items, layers, own),
         out_shape=[
-            jax.ShapeDtypeStruct((layers, rows[m], 2 * halves[m]), jnp.float32) for m in range(members)
+            jax.ShapeDtypeStruct((layers, rows[m], 2 * halves[m]), full) for m in range(members)
+        ]
+        + [
+            jax.ShapeDtypeStruct((SHARE, MOD_ROWS * 128), full),
+            jax.ShapeDtypeStruct((FREQS, SHARE), full),
+            jax.ShapeDtypeStruct((SHARE, D), full),
+            jax.ShapeDtypeStruct(tile, full),
+            jax.ShapeDtypeStruct((8, 128), full),
         ],
-        in_specs=[pl.BlockSpec(memory_space=pl.ANY)] * len(flat),
-        out_specs=[pl.BlockSpec(memory_space=pl.ANY)] * members,
+        in_specs=[there] * len(flat) + [here] * len(rest),
+        out_specs=[there] * members + [here] * 5,
         scratch_shapes=scratch,
         compiler_params=pltpu.CompilerParams(
             collective_id=number, has_side_effects=True, vmem_limit_bytes=VMEM_LIMIT
         ),
-    )(*flat)
+    )(*flat, *rest)
 
 
 def to_low(values):
@@ -1151,17 +1439,7 @@
     text_keep = lax.iota(jnp.int32, caption) < text_lengths[0]
     rows = [w_in.shape[1], w_text.shape[1], w_out.shape[1]]
     halves = [JOINT // 2, D, D // 2]
-    aligned = all(height % 8 == 0 for height in rows) and ways[0] % 2 == 0 and ways[1] % 2 == 0
-
-    def to_all(values, number):
-        if aligned:
-            return exchange(values, ways, True, number)
-        return lax.all_gather(values, ALL, axis=0, tiled=False)
-
-    def to_each(values, number):
-        if aligned:
-            return exchange(values, ways, False, number)
-        return lax.all_to_all(values, ALL, 0, 0, tiled=True)
+    aligned = own <= SHARE and all(height % 8 == 0 for height in rows) and all(way % 2 == 0 for way in ways)
 
     sinus = time_features(timesteps)
     lead_low, head_low = to_low(w_lead), to_low(w_head)
@@ -1173,32 +1451,19 @@
         ]
     )
     facts = jnp.concatenate([to_low(sinus).astype(jnp.float32)[0], valid_frames.astype(jnp.float32)])
-    packed = to_all(jnp.concatenate([tiles(facts), tiles(small)], 0), 3).reshape(count, -1)
-    facts_size = 1024
-    sinus_all = to_low(packed[:, :FREQS])
-    frame_count = jnp.sum(packed[:, FREQS])
-    small_all = packed[:, facts_size:]
-    at = channels * own
-    lead_in = to_low(small_all[:, :at].reshape(count, channels, own).transpose(1, 0, 2).reshape(channels, D))
-    head_pred = to_low(small_all[:, at : 2 * at].reshape(D, channels))
-    gains_all = small_all[:, 2 * at : 2 * at + LAYERS * own].reshape(count, LAYERS, own)
-    gains_all = gains_all.transpose(1, 0, 2).reshape(LAYERS, D)
-
-    act_time, pull_time = jax.vjp(jax.nn.silu, dense(sinus_all, lead_low[:FREQS]))
-    act_low = to_low(act_time)
-    temb_part = dense(act_low, head_low[:, :D]).reshape(count, count, own).transpose(1, 0, 2)
-    temb = jnp.sum(to_each(tiles(temb_part, (count,)), 4), 0).reshape(-1)[:D].reshape(count, own)
-    cond, pull_cond = jax.vjp(jax.nn.silu, temb)
-    cond_low = to_low(cond)
+    facts = jnp.concatenate([tiles(facts), tiles(small)], 0)
     mod_low = jnp.concatenate(
         [to_low(w_in[layer, :, JOINT:]) for layer in range(LAYERS)] + [head_low[:, D : 3 * D]], 1
     )
-    mod_part = dense(cond_low, mod_low)
-    mods = jnp.sum(to_each(tiles(mod_part, (count,)), 5), 0).reshape(-1)[: mod_low.shape[1]]
-
     if aligned:
+        lead_own = jnp.pad(lead_low[:FREQS], [(0, 0), (0, 128 - own)])
+        head_own = jnp.pad(head_low[:, :D], [(0, SHARE - own), (0, 0)])
+        mod_own = jnp.pad(mod_low, [(0, SHARE - own), (0, 0)])
         items = plan(halves, range(LAYERS), GATHER_PATTERN)
-        weights = gather_weights([w_in, w_text, w_out], halves, ways, 1, items)
+        weights, packed, pre_time, temb, mods = gather_weights(
+            [w_in, w_text, w_out], facts, lead_own, head_own, mod_own, own, halves, ways, 1, items
+        )
+        mods = mods.reshape(-1)
     else:
         weights = [
             [
@@ -1207,6 +1472,22 @@
             ]
             for layer in range(LAYERS)
         ]
+        packed = lax.all_gather(facts, ALL, axis=0, tiled=False)
+        sinus_all = to_low(packed.reshape(count, -1)[:, :FREQS])
+        pre_time = dense(sinus_all, lead_low[:FREQS])
+        act_low = to_low(jax.nn.silu(pre_time))
+        temb = dense(act_low, head_low[:, :D]).reshape(count, count, own).transpose(1, 0, 2)
+        temb = jnp.sum(lax.all_to_all(temb, ALL, 0, 0, tiled=True), 0)
+        cond_low = to_low(jax.nn.silu(temb))
+        mods = jnp.sum(lax.all_to_all(dense(cond_low, mod_low)[:, None], ALL, 0, 0, tiled=True), 0)[0]
+    packed = packed.reshape(count, -1)
+    frame_count = jnp.sum(packed[:, FREQS])
+    small_all = packed[:, 1024:]
+    at = channels * own
+    lead_in = to_low(small_all[:, :at].reshape(count, channels, own).transpose(1, 0, 2).reshape(channels, D))
+    head_pred = to_low(small_all[:, at : 2 * at].reshape(D, channels))
+    gains_all = small_all[:, 2 * at : 2 * at + LAYERS * own].reshape(count, LAYERS, own)
+    gains_all = gains_all.transpose(1, 0, 2).reshape(LAYERS, D)
 
     level = noise_level(timesteps)
     noisy_low = to_low(jnp.sqrt(level) * clean_latent + jnp.sqrt(1.0 - level) * noise)
@@ -1214,7 +1495,7 @@
     block_mods = jnp.concatenate(
         [mods[: LAYERS * MOD].reshape(LAYERS, 6, D), gains_all[:, None], jnp.zeros((LAYERS, 1, D))], 1
     )
-    final_mods = jnp.pad(mods[LAYERS * MOD :].reshape(2, D), [(0, 6), (0, 0)])
+    final_mods = jnp.pad(mods[LAYERS * MOD : LAYERS * MOD + 2 * D].reshape(2, D), [(0, 6), (0, 0)])
     short = [(0, 0), (0, 128 - channels)]
     (loss_lanes, grad_stream, grad_blocks, grad_final, grad_pred_w), kept = run_model(
         stream,
@@ -1227,38 +1508,36 @@
         (2.0 / frame_count).reshape(1),
         weights,
     )
-    loss_part = jnp.sum(loss_lanes[0])
     grad_pred_w = grad_pred_w[:, :channels]
-    grad_mods = [grad_blocks[:, :6].reshape(-1), grad_final[:2].reshape(-1)]
-    grad_gains = grad_blocks[:, 6]
+    grad_mods = jnp.concatenate([grad_blocks[:, :6].reshape(-1), grad_final[:2].reshape(-1)])
     grad_in_w = weight_grad(noisy_low, to_low(grad_stream))
-
-    mods_all = to_all(tiles(to_low(jnp.concatenate(grad_mods)).astype(jnp.float32)), 6)
-    mods_all = to_low(mods_all.reshape(count, -1)[:, : mod_low.shape[1]])
-    grad_mod_w = weight_grad(cond_low, mods_all)
-    (grad_temb,) = pull_cond(dense_back(mods_all, mod_low))
     small_grads = jnp.concatenate(
         [
             grad_in_w.reshape(channels, count, own).transpose(1, 0, 2).reshape(count, -1),
             grad_pred_w.reshape(count, -1),
-            grad_gains.reshape(LAYERS, count, own).transpose(1, 0, 2).reshape(count, -1),
+            grad_blocks[:, 6].reshape(LAYERS, count, own).transpose(1, 0, 2).reshape(count, -1),
         ],
         1,
     )
-    temb_tile = tiles(to_low(grad_temb).astype(jnp.float32))
-    sent = jnp.concatenate(
-        [jnp.broadcast_to(temb_tile[None], (count,) + temb_tile.shape), tiles(small_grads, (count,))], 1
-    )
-    got = to_each(sent, 7).reshape(count, -1)
-    temb_all = to_low(got[:, :D].reshape(count, count, own).transpose(1, 0, 2).reshape(count, D))
-    small_sum = jnp.sum(got[:, temb_tile.size :], 0)
-    grad_time_two = weight_grad(act_low, temb_all)
-    (grad_pre_time,) = pull_time(dense_back(temb_all, head_low[:, :D]))
-    grad_time_one = weight_grad(sinus_all, to_low(grad_pre_time))
-
     if aligned:
         items = plan(halves, list(reversed(range(LAYERS))), SCATTER_PATTERN)
-        sums = scatter_grads(kept, text_low, rows, halves, ways, 2, items)
+        rest = [
+            tiles(to_low(grad_mods).astype(jnp.float32)),
+            tiles(small_grads, (count,)),
+            loss_lanes,
+            packed.reshape(count, -1, 128),
+            pre_time,
+            temb,
+            head_own,
+            mod_own,
+        ]
+        *sums, grad_mod_w, grad_time_one, grad_time_two, small_sum, final = scatter_grads(
+            kept, text_low, rest, own, rows, halves, ways, 2, items
+        )
+        grad_mod_w, grad_time_two = grad_mod_w[:own], grad_time_two[:own]
+        grad_time_one = grad_time_one[:, :own]
+        small_sum = small_sum.reshape(-1)
+        loss_sum, squares = jnp.sum(final[1]), final[0, 0]
     else:
         sums = [[], [], []]
         for k in kept:
@@ -1268,6 +1547,17 @@
             for member, grad in enumerate(grads):
                 sums[member].append(lax.psum_scatter(grad, ALL, scatter_dimension=0, tiled=True))
         sums = [jnp.stack(part) for part in sums]
+        mods_all = lax.all_gather(to_low(grad_mods), ALL, axis=0, tiled=False)
+        grad_mod_w = weight_grad(cond_low, mods_all)
+        _, pull_cond = jax.vjp(jax.nn.silu, temb)
+        (grad_temb,) = pull_cond(dense_back(mods_all, mod_low))
+        grad_temb = lax.all_gather(to_low(grad_temb), ALL, axis=0, tiled=False)
+        grad_temb = grad_temb.transpose(1, 0, 2).reshape(count, D)
+        grad_time_two = weight_grad(act_low, grad_temb)
+        _, pull_time = jax.vjp(jax.nn.silu, pre_time)
+        (grad_pre_time,) = pull_time(dense_back(grad_temb, head_low[:, :D]))
+        grad_time_one = weight_grad(sinus_all, to_low(grad_pre_time))
+        small_sum = jnp.sum(lax.all_to_all(small_grads, ALL, 0, 0, tiled=True), 0)
     mod_grads = grad_mod_w[:, : LAYERS * MOD].reshape(own, LAYERS, MOD).transpose(1, 0, 2)
     grad_list = [
         jnp.concatenate([sums[0], mod_grads], 2),
@@ -1279,10 +1569,10 @@
             [grad_time_two, grad_mod_w[:, LAYERS * MOD :], small_sum[at : 2 * at].reshape(own, channels)], 1
         ),
     ]
-    local_squares = sum((jnp.sum(item * item) for item in grad_list))
-    totals = jnp.sum(to_all(tiles(jnp.stack([loss_part, local_squares])), 8), 0).reshape(-1)
-    loss_sum = totals[0]
-    grad_norm = jnp.sqrt(totals[1])
+    if not aligned:
+        local = jnp.stack([jnp.sum(loss_lanes[0]), sum((jnp.sum(item * item) for item in grad_list))])
+        loss_sum, squares = jnp.sum(lax.all_gather(local, ALL, axis=0, tiled=False), 0)
+    grad_norm = jnp.sqrt(squares)
     factor = CLIP_NORM / jnp.maximum(grad_norm, CLIP_NORM)
     params = (w_in, w_text, w_out, gains, w_lead, w_head)
     firsts = (first_in, first_text, first_out, first_gains, first_lead, first_head)

time: 726 us -> 615 us (0.85)
  Pallas kernels: 647 us -> 558 us
  other arithmetic: 36.1 us -> 20.9 us
    pallas_call x6 -> x0, Pallas kernels: 126 us -> none  [exchange(): pl.pallas_call(functools.partial(exchange_kernel, ways, shared), out_shap...]
    pallas_call x1, Pallas kernels: 193 us -> 228 us  [scatter_grads(): pl.pallas_call(functools.partial(scatter_kernel, ways, rows, halves, item...]
    reduce_sum x11 -> x1, other arithmetic: 12.1 us -> 1.28 us  [body(): loss_sum, squares = (jnp.sum(final[1]), final[0, 0])]
where the time goes in v3:
time: 615 us; the launch traced here: 611 us
  Pallas kernels  558 us (91%)
  local copies, waits for them, and re-layouts  24 us (4%)
  other arithmetic  20.9 us (3%)
    pallas_call x1, Pallas kernels, scatter_grads(): pl.pallas_call(functools.partial(scatter_kernel, ways, rows, halves, item...  228 us
    pallas_call x1, Pallas kernels, gather_weights(): pl.pallas_call(functools.partial(gather_kernel, ways, rows, halves, items...  200 us
    pallas_call x1, Pallas kernels, run_model(): pl.pallas_call(model_kernel, out_shape=[shape((8, noise.shape[1]), full),...  130 us

profile of v3, /device:TPU:0, one launch (start us, length us, event | category | flops | bytes accessed | tf_op | source)
XLA Modules:
  0.0 610.7 jit_solution(8633046171238650145)
XLA Ops:
  5.2 0.7 slice.121
  5.9 0.8 add_convert_fusion
  7.5 1.0 convert_element_type.87
  9.9 0.9 copy.95
  11.5 1.7 convert.36
  13.2 0.9 fusion.6.refs_6_.refs_34_
  14.1 200.4 %shard_map.391 = (bf16[4,2,2,48,6144]{4,3,2,1,0:T(8,128)(2,1)}, bf16[4,2,2,64,1536]{4,3,2,1,0:T(8,128)(2,1)}, bf16[4,2,2,288,768]{4,3,2,1,0:T(8,128)(2,1)}, bf16...) custom-call(f32[2,24,10752]{2,1,0:T(8,128)} %refs_0_.1, ...), custom_call_target="tpu_custom_call" | custom-call | tf_op jit(solution)/shard_map/pallas_call | solution.py:446
  214.5 0.7 slice.104
  215.2 0.8 slice.102
  216.6 1.0 copy.126
  218.0 0.7 pad.49.refs_7_
  221.6 1.2 fusion.18.refs_2_
  222.8 129.7 %shard_map.392 = (f32[8,128]{1,0:T(8,128)}, f32[320,768]{1,0:T(8,128)}, f32[2,8,768]{2,1,0:T(8,128)}, f32[8,768]{1,0:T(8,128)}, f32[768,128]{1,0:T(8,128)}, /*in...) custom-call(s32[2]{0:T(128)} %pad_add_fusion.refs_0_, ...), custom_call_target="tpu_custom_call" | custom-call | tf_op jit(solution)/shard_map/pallas_call | solution.py:1358
  352.5 0.7 slice.141
  353.3 0.8 slice_reduce_fusion.1
  354.1 0.8 slice.140
  355.8 1.2 reshape.196
  357.0 1.3 convert_bitcast_fusion
  360.4 227.6 %shard_map.393 = (f32[2,24,6144]{2,1,0:T(8,128)}, f32[2,32,1536]{2,1,0:T(8,128)}, f32[2,144,768]{2,1,0:T(8,128)}, f32[32,10752]{1,0:T(8,128)}, f32[256,32]{1,0:T...) custom-call(bf16[256,1024]{1,0:T(8,128)(2,1)} %bitcast.80, ...), custom_call_target="tpu_custom_call" | custom-call | tf_op jit(solution)/shard_map/pallas_call | solution.py:848
  588.0 1.2 slice.111
  589.9 1.3 slice_reduce_fusion.2
  591.2 0.7 slice_multiply_fusion
  591.9 0.8 fusion.39
  593.7 1.0 copy.102
  594.7 0.9 slice.116
  596.3 0.9 slice.117
  597.2 1.3 slice.112
  598.7 1.0 multiply_subtract_fusion.3
  599.9 1.2 multiply_subtract_fusion.2
  601.4 2.0 multiply_subtract_fusion.1
  603.7 0.9 copy-done.3
  605.2 3.9 multiply_subtract_fusion
  (98 shorter events, 14.5 us)
Async XLA Ops:
  214.5 4.7 copy-start.2
  360.3 232.5 %copy-start.19 = (f32[2,24]{1,0:T(2,128)S(1)}, f32[2,24]{1,0:T(2,128)}, u32[]{:S(2)}) copy-start(f32[2,24]{1,0:T(2,128)} %param.33) | copy-start | bytes 580
  360.3 232.5 %copy-start.20 = (f32[2,24]{1,0:T(2,128)S(1)}, f32[2,24]{1,0:T(2,128)}, u32[]{:S(2)}) copy-start(f32[2,24]{1,0:T(2,128)} %param.43) | copy-start | bytes 580
  360.3 232.5 %copy-start.21 = (f32[2,24]{1,0:T(2,128)S(1)}, f32[2,24]{1,0:T(2,128)}, u32[]{:S(2)}) copy-start(f32[2,24]{1,0:T(2,128)} %param.42) | copy-start | bytes 580
  360.3 235.3 %copy-start.16 = (f32[276,24]{0,1:T(8,128)S(1)}, f32[276,24]{0,1:T(8,128)}, u32[]{:S(2)}) copy-start(f32[276,24]{0,1:T(8,128)} %param.34) | copy-start | bytes 79492
  360.3 235.3 %copy-start.17 = (f32[276,24]{0,1:T(8,128)S(1)}, f32[276,24]{0,1:T(8,128)}, u32[]{:S(2)}) copy-start(f32[276,24]{0,1:T(8,128)} %param.45) | copy-start | bytes 79492
  360.3 235.2 %copy-start.18 = (f32[276,24]{0,1:T(8,128)S(1)}, f32[276,24]{0,1:T(8,128)}, u32[]{:S(2)}) copy-start(f32[276,24]{0,1:T(8,128)} %param.44) | copy-start | bytes 79492
  595.6 3.0 copy-start.7
  595.6 3.0 copy-start.14
  595.6 3.0 copy-start.15
  597.2 2.4 copy-start.13
  598.5 1.2 copy-start.5
  598.5 1.1 copy-start.11
  598.5 1.4 copy-start.12
  598.6 2.6 copy-start.10
  598.7 2.5 copy-start.1
  598.7 2.5 copy-start.8
  598.7 2.7 copy-start.9
  599.9 3.4 copy-start.6
  601.4 2.3 copy-start
  601.4 3.2 copy-start.3
  601.4 3.9 copy-start.4

commit v4 on v3

--- a/solution.py
+++ b/solution.py
@@ -256,12 +256,17 @@
         return taken
 
     shards = take(members)
-    facts_in, lead_own, head_own, mod_own = take(4)
+    facts_in, lead_own, head_own, mod_own, lengths, text, noisy = take(7)
     fulls = take(members * layers)
-    facts, pre_time, temb_own, mods = take(4)
+    facts, pre_time, temb_own, block_mods, final_mods, small, result = take(7)
+    early = dict(zip(EARLY, take(len(EARLY))))
     totals, landed, mod_parts = take(3)
     mod_landed = take(4)
     facts_send, facts_recv, sum_send, sum_recv, split_send, split_recv = take(6)
+    mods, win, wtext, wout = take(4)
+    saved = Names(**dict(zip((name for name, *_ in SAVED), take(len(SAVED)))))
+    (hidden,) = take(1)
+    load_sem, keep_sem = take(2)
     rest = refs
     stages = rest[:members]
     blocks = rest[members : 2 * members]
@@ -411,17 +416,85 @@
         hops, mod_parts.reshape(sizes + (2,) + MOD_TILE), mod_landed, mods, split_send, split_recv, sent_all
     )
     side = [time_layers] + sums[1:] + [modulation] + splits[1:]
-    for i, phase in schedule(items, GATHER_LAGS):
-        if phase == 1 and side:
-            side.pop(0)()
+
+    def prepare():
+        small[...] = to_low(facts[:, 8 : 8 + own, :].reshape(D, 128))
+        gains = dot_nt(to_low(gain_pick().astype(jnp.float32)), small[...])
+
+        def row(piece):
+            tiles_of = [mods[piece * (D // 128) + k : piece * (D // 128) + k + 1, :] for k in range(D // 128)]
+            return jnp.concatenate(tiles_of, 1)
+
+        for layer in range(layers):
+            for j in range(6):
+                block_mods[layer, j : j + 1, :] = row(layer * 6 + j)
+            block_mods[layer, 6:7, :] = gains[layer : layer + 1, :]
+            block_mods[layer, 7:8, :] = jnp.zeros((1, D), jnp.float32)
+        final_mods[...] = jnp.zeros_like(final_mods)
+        for j in range(2):
+            final_mods[j : j + 1, :] = row(layers * 6 + j)
+        for column in range(0, D, 256):
+            saved.stream[:, column : column + 256] = dot_nt(noisy[...], small[column : column + 256, :])
+
+    def load(part):
+        return pltpu.make_async_copy(
+            *weight_parts(whole_weights, (win, wtext, wout))[part], load_sem.at[PARTS.index(part)]
+        )
+
+    def emit(name, ref):
+        pltpu.make_async_copy(ref, early[name], keep_sem.at[EARLY.index(name)]).start()
+
+    def first_block():
+        frame_keep, text_keep = keeps(lengths, noisy.shape[0], text.shape[0])
+        for part in ("qkv", "ao", "cq", "text", "co", "up", "down"):
+            load(part).start()
+        yield from block_forward(
+            saved, hidden, result, block_mods.at[0], text, frame_keep, text_keep,
+            Names(win=win, wtext=wtext, wout=wout), lambda part: load(part).wait(), lambda part: None, emit,
+        )
+        for name in NEEDED:
+            if name not in KEPT:
+                emit(name, getattr(saved, name))
+
+    whole_weights = [
+        full(0, member).reshape(sizes[0] * sizes[1] * sizes[2] * 2 * rows[member], 2 * halves[member]) for member in range(members)
+    ]
+    order = schedule(items, GATHER_LAGS)
+    turn = max(k for k, (i, _) in enumerate(order) if items[i][0] == 0) + 1
+    waited = set()
+
+    def advance(i, phase):
         if phase > 0:
             finish(i, phase - 1)
         if phase < 3:
             start(i, phase)
-    for i in range(len(items)):
-        c_wait(i)
+
+    for i, phase in order[:turn]:
+        if phase in (1, 2) and side:
+            side.pop(0)()
+        advance(i, phase)
     for step in side:
         step()
+    side = []
+    prepare()
+    for i in range(len(items)):
+        if items[i][0] == 0:
+            c_wait(i)
+            waited.add(i)
+            own_put(*items[i][:2])
+    later = list(order[turn:])
+    pace = BLOCK_PARTS / max(len(later), 1)
+    for part, _ in enumerate(first_block()):
+        if later and part >= pace * (len(order) - turn - len(later)):
+            advance(*later.pop(0))
+    for i, phase in later:
+        advance(i, phase)
+    for i in range(len(items)):
+        if i not in waited:
+            c_wait(i)
+    for name in EARLY:
+        ref = hidden if name == "hidden" else getattr(saved, name)
+        pltpu.make_async_copy(ref, early[name], keep_sem.at[EARLY.index(name)]).wait()
     for layer in range(layers):
         for member in range(members):
             own_put(layer, member)
@@ -433,7 +506,11 @@
         copy.wait_send()
 
 
-def gather_weights(shards, facts, lead_own, head_own, mod_own, own, halves, ways, number, items):
+BLOCK_PARTS = 48
+EARLY = ("n1", "n2", "n3", "mixed1", "mixed2", "hidden", "stream", "qkv", "branch1", "stream2", "cq", "ckv", "stream3", "branch3", "stats1", "stats2")
+
+
+def gather_weights(shards, facts, lead_own, head_own, mod_own, lengths, text, noisy, own, halves, ways, number, items):
     layers = shards[0].shape[0]
     rows = [s.shape[1] for s in shards]
     members = len(shards)
@@ -441,23 +518,27 @@
     devices = ways[0] * ways[1]
     count = layers * members
     n = len(items)
-    sem, vmem, full = pltpu.SemaphoreType.DMA, pltpu.VMEM, jnp.float32
+    frames, tokens = noisy.shape[0], text.shape[0]
+    sem, vmem, full, shape = pltpu.SemaphoreType.DMA, pltpu.VMEM, jnp.float32, jax.ShapeDtypeStruct
     here, there = pl.BlockSpec(memory_space=pltpu.VMEM), pl.BlockSpec(memory_space=pl.ANY)
+    scalar = pl.BlockSpec(memory_space=pltpu.SMEM)
     out = pl.pallas_call(
         functools.partial(gather_kernel, ways, rows, halves, items, layers, own),
         out_shape=[
-            jax.ShapeDtypeStruct(sizes + (2 * rows[m], 2 * halves[m]), jnp.bfloat16)
-            for _ in range(layers)
-            for m in range(members)
+            shape(sizes + (2 * rows[m], 2 * halves[m]), jnp.bfloat16) for _ in range(layers) for m in range(members)
         ]
         + [
-            jax.ShapeDtypeStruct((devices,) + facts.shape, full),
-            jax.ShapeDtypeStruct((devices, 128), full),
-            jax.ShapeDtypeStruct((devices, 128), full),
-            jax.ShapeDtypeStruct(MOD_TILE, full),
-        ],
-        in_specs=[there] * members + [here] * 4,
-        out_specs=[there] * count + [here] * 4,
+            shape((devices,) + facts.shape, full),
+            shape((devices, 128), full),
+            shape((devices, 128), full),
+            shape((layers, 8, D), full),
+            shape((8, D), full),
+            shape((D, 128), jnp.bfloat16),
+            shape((frames, D), full),
+        ]
+        + [shape(shape_of(name, frames, tokens), KINDS[name]) for name in EARLY],
+        in_specs=[there] * members + [here] * 4 + [scalar] + [here] * 2,
+        out_specs=[there] * count + [here] * 7 + [there] * len(EARLY),
         scratch_shapes=[
             vmem((len(ROUNDS) + 1, devices, D), full),
             vmem((sizes[0] + sizes[1] + sizes[2] - 2, devices, D), full),
@@ -466,6 +547,10 @@
         + split_shapes(sizes, MOD_TILE)
         + [sem((devices,))] * 2
         + [sem((len(ROUNDS), max(sizes)))] * 4
+        + [vmem(MOD_TILE, full), vmem((D, JOINT), jnp.bfloat16)]
+        + [vmem((text.shape[1], 2 * D), jnp.bfloat16), vmem((2 * D + FF, D), jnp.bfloat16)]
+        + [vmem(shape_of(name, frames, tokens), kind) for name, _, kind in SAVED]
+        + [vmem((frames, FF), jnp.bfloat16), sem((len(PARTS),)), sem((len(EARLY),))]
         + [vmem((layers, 2 * rows[m], halves[m]), full) for m in range(members)]
         + [vmem((layers, 2 * rows[m], halves[m]), jnp.bfloat16) for m in range(members)]
         + [sem((count,))] * 4
@@ -473,11 +558,11 @@
         compiler_params=pltpu.CompilerParams(
             collective_id=number, has_side_effects=True, vmem_limit_bytes=VMEM_LIMIT
         ),
-    )(*shards, facts, lead_own, head_own, mod_own)
+    )(*shards, facts, lead_own, head_own, mod_own, lengths, text, noisy)
     weights = [
         [out[l * members + m].reshape(-1, 2 * halves[m]) for m in range(members)] for l in range(layers)
     ]
-    return weights, *out[count:]
+    return weights, out[count : count + 7], dict(zip(EARLY, out[count + 7 :]))
 
 
 ORDERS = ((0, 2, 1), (0, 1, 2), (2, 0, 1), (1, 0, 2))
@@ -521,13 +606,13 @@
 
     (text_in,) = take(1)
     acts = [dict(zip(ACTS, take(len(ACTS)))) for _ in range(layers)]
-    mods_in, small_in, loss_in, facts, pre_time, temb_own, head_own, mod_own = take(8)
+    mods_in, small_in, loss_in, facts_in, pre_time, temb_own, head_own, mod_own = take(8)
     outs = take(members)
     grad_mod, grad_time_one, grad_time_two, small_out, final = take(5)
     all_mods, small_rows, totals, landed, squares = take(5)
     small_landed = take(4)
     spread_send, spread_recv, sum_send, sum_recv, split_send, split_recv, end_send, end_recv = take(8)
-    ends, end_landed = take(2)
+    ends, end_landed, backs, facts, bring_sem = take(5)
     lefts, rights, text, right_text, hidden, mixes, right_out = take(7)
     ring = take(members)
     whole = take(n)
@@ -564,22 +649,32 @@
         hops, small_rows.reshape(sizes + (2,) + tile), small_landed, small_out, split_send, split_recv, sent_all
     )
 
+    bring = [
+        pltpu.make_async_copy(small_in, small_rows, bring_sem.at[0]),
+        pltpu.make_async_copy(facts_in.at[:, 0:8], facts, bring_sem.at[1]),
+    ]
+    for copy in bring:
+        copy.start()
+
     def begin_small():
-        small_rows[...] = small_in[...]
+        for copy in bring:
+            copy.wait()
         splits[0]()
 
-    def modulation_back():
-        back = jnp.zeros((all_mods.shape[0], SHARE), jnp.float32)
-        for j in range(MOD_ROWS):
+    def modulation_part(begin, end):
+        back = jnp.zeros_like(backs) if begin == 0 else backs[...]
+        for j in range(begin, end):
             cols = slice(j * 128, (j + 1) * 128)
             grad = to_low(all_mods[:, j, :])
             back = back + dot_nt(grad, mod_own[:, cols])
             grad_mod[:, cols] = dot_tn(cond, grad)
-        grad_temb = to_low(back * slope_temb)
+        backs[...] = back
+        count_squares(grad_mod[:, begin * 128 : end * 128])
+
+    def modulation_back():
+        grad_temb = to_low(backs[...] * slope_temb)
         pick = to_low(chosen(me, own, SHARE))
         totals[0] = dot_nt(grad_temb, pick)
-        for column in range(0, MOD_ROWS * 128, MOD):
-            count_squares(grad_mod[:, column : min(column + MOD, MOD_ROWS * 128)])
         sums[0]()
 
     def time_back():
@@ -592,8 +687,17 @@
         count_squares(grad_time_one[...])
         count_squares(small_out[...])
 
-    side = [spreads[0], begin_small]
-    side += [step for pair in zip(spreads[1:], splits[1:]) for step in pair]
+    def together(*steps):
+        return lambda: [step() for step in steps]
+
+    def rest():
+        pass
+
+    side = [together(spreads[0], begin_small)]
+    for pair in zip(spreads[1:], splits[1:]):
+        side += [rest, together(*pair)]
+    parts_of = [functools.partial(modulation_part, j, j + 12) for j in range(0, MOD_ROWS, 12)]
+    side += [together(*parts_of[k : k + 2]) for k in range(0, len(parts_of), 2)]
     side += [modulation_back] + sums[1:] + [time_back]
 
     def send(copy):
@@ -775,7 +879,7 @@
         if step == 0:
             give(i)
             continue
-        if step in (1, 2) and side:
+        if step in (1, 4) and side:
             side.pop(0)()
         if step == 1:
             combine(i)
@@ -829,6 +933,7 @@
     ]
     scratch += split_shapes(sizes, tile) + [sums] * 8
     scratch += [vmem((len(ROUNDS) + 1, 8, 128), full), vmem((sizes[0] + sizes[1] + sizes[2] - 2, 8, 128), full)]
+    scratch += [vmem((devices, SHARE), full), vmem((devices, 8, 128), full), sem((2,))]
     scratch += [
         vmem((3, frames, D), low),
         vmem((8, frames, D), low),
@@ -857,7 +962,7 @@
             jax.ShapeDtypeStruct(tile, full),
             jax.ShapeDtypeStruct((8, 128), full),
         ],
-        in_specs=[there] * len(flat) + [here] * len(rest),
+        in_specs=[there] * len(flat) + [here, there, here, there] + [here] * (len(rest) - 4),
         out_specs=[there] * members + [here] * 5,
         scratch_shapes=scratch,
         compiler_params=pltpu.CompilerParams(
@@ -870,6 +975,19 @@
     return values.astype(jnp.bfloat16)
 
 
+def norm_rows(values):
+    centred = values - jnp.mean(values, -1, keepdims=True)
+    return centred * lax.rsqrt(jnp.mean(centred * centred, -1, keepdims=True) + EPSILON)
+
+
+def modulate(stream, shift, scale_part):
+    return norm_rows(stream) * (1.0 + scale_part) + shift
+
+
+def gained_norm(stream, gain):
+    return norm_rows(stream) * gain
+
+
 def dense(left, right):
     return jnp.dot(left, right, preferred_element_type=jnp.float32)
 
@@ -880,6 +998,45 @@
 
 def weight_grad(left, right):
     return lax.dot_general(left, right, (((0,), (0,)), ((), ())), preferred_element_type=jnp.float32)
+
+
+def split_heads(values):
+    return values.reshape(values.shape[0], HEADS, HEAD_DIM)
+
+
+def attention(queries, keys, values, keep):
+    scores = jnp.einsum(
+        "qhd,khd->hqk", split_heads(queries), split_heads(keys), preferred_element_type=jnp.float32
+    ) * HEAD_DIM ** (-0.5)
+    scores = jnp.where(keep[None, None, :], scores, NEGATIVE)
+    shifted = jnp.exp(scores - jnp.max(scores, -1, keepdims=True))
+    probs = shifted / jnp.sum(shifted, -1, keepdims=True)
+    mixed = jnp.einsum(
+        "hqk,khd->qhd", to_low(probs), split_heads(values), preferred_element_type=jnp.float32
+    )
+    return (to_low(mixed.reshape(queries.shape)), probs)
+
+
+def attention_back(queries, keys, values, probs, grad_mixed):
+    grad_heads = split_heads(to_low(grad_mixed))
+    grad_values = jnp.einsum(
+        "hqk,qhd->khd", to_low(probs), grad_heads, preferred_element_type=jnp.float32
+    )
+    grad_probs = jnp.einsum(
+        "qhd,khd->hqk", grad_heads, split_heads(values), preferred_element_type=jnp.float32
+    )
+    grad_scores = to_low(probs * (grad_probs - jnp.sum(probs * grad_probs, -1, keepdims=True)))
+    grad_queries = jnp.einsum(
+        "hqk,khd->qhd", grad_scores, split_heads(keys), preferred_element_type=jnp.float32
+    ) * HEAD_DIM ** (-0.5)
+    grad_keys = jnp.einsum(
+        "hqk,qhd->khd", grad_scores, split_heads(queries), preferred_element_type=jnp.float32
+    ) * HEAD_DIM ** (-0.5)
+    return (
+        grad_queries.reshape(queries.shape),
+        grad_keys.reshape(keys.shape),
+        grad_values.reshape(values.shape),
+    )
 
 
 def noise_level(steps):
@@ -894,9 +1051,123 @@
     return jnp.concatenate([jnp.cos(angles), jnp.sin(angles)], -1)
 
 
+def layer_forward(stream, modulation, text_low, frame_keep, text_keep, weights):
+    w_joint, w_textkv, w_back, gain = weights
+    normed_one, pull_one = jax.vjp(modulate, stream, modulation[:D], modulation[D : 2 * D])
+    input_one = to_low(normed_one)
+    self_proj = to_low(dense(input_one, w_joint[:, : 3 * D]))
+    mixed_one, probs_one = attention(
+        self_proj[:, :D], self_proj[:, D : 2 * D], self_proj[:, 2 * D :], frame_keep
+    )
+    branch_one = dense(mixed_one, w_back[:D])
+    stream_two = stream + modulation[2 * D : 3 * D] * branch_one
+    normed_two, pull_two = jax.vjp(gained_norm, stream_two, gain)
+    input_two = to_low(normed_two)
+    cross_query = to_low(dense(input_two, w_joint[:, 3 * D : 4 * D]))
+    cross_kv = to_low(dense(text_low, w_textkv))
+    mixed_two, probs_two = attention(cross_query, cross_kv[:, :D], cross_kv[:, D:], text_keep)
+    stream_three = stream_two + dense(mixed_two, w_back[D : 2 * D])
+    normed_three, pull_three = jax.vjp(
+        modulate, stream_three, modulation[3 * D : 4 * D], modulation[4 * D : 5 * D]
+    )
+    input_three = to_low(normed_three)
+    hidden_act, pull_act = jax.vjp(jax.nn.gelu, dense(input_three, w_joint[:, 4 * D :]))
+    hidden_low = to_low(hidden_act)
+    branch_three = dense(hidden_low, w_back[2 * D :])
+    result = stream_three + modulation[5 * D :] * branch_three
+    saved = (
+        pull_one,
+        input_one,
+        self_proj,
+        mixed_one,
+        probs_one,
+        branch_one,
+        pull_two,
+        input_two,
+        cross_query,
+        cross_kv,
+        mixed_two,
+        probs_two,
+        pull_three,
+        input_three,
+        pull_act,
+        hidden_low,
+        branch_three,
+    )
+    return (result, saved)
+
+
+def layer_backward(saved, grad_out, modulation, text_low, weights):
+    w_joint, w_textkv, w_back, gain = weights
+    (
+        pull_one,
+        input_one,
+        self_proj,
+        mixed_one,
+        probs_one,
+        branch_one,
+        pull_two,
+        input_two,
+        cross_query,
+        cross_kv,
+        mixed_two,
+        probs_two,
+        pull_three,
+        input_three,
+        pull_act,
+        hidden_low,
+        branch_three,
+    ) = saved
+    grad_three = to_low(grad_out * modulation[5 * D :])
+    grad_gate_two = jnp.sum(grad_out * branch_three, 0)
+    grad_down = weight_grad(hidden_low, grad_three)
+    (grad_pre,) = pull_act(dense_back(grad_three, w_back[2 * D :]))
+    grad_pre = to_low(grad_pre)
+    grad_up = weight_grad(input_three, grad_pre)
+    grad_inner, grad_shift_two, grad_scale_two = pull_three(dense_back(grad_pre, w_joint[:, 4 * D :]))
+    grad_stream = grad_out + grad_inner
+    grad_cross_out = to_low(grad_stream)
+    grad_co = weight_grad(mixed_two, grad_cross_out)
+    grad_cq, grad_ck, grad_cv = attention_back(
+        cross_query,
+        cross_kv[:, :D],
+        cross_kv[:, D:],
+        probs_two,
+        dense_back(grad_cross_out, w_back[D : 2 * D]),
+    )
+    grad_cq = to_low(grad_cq)
+    grad_text_w = weight_grad(text_low, to_low(jnp.concatenate([grad_ck, grad_cv], -1)))
+    grad_query_w = weight_grad(input_two, grad_cq)
+    grad_inner, grad_gain = pull_two(dense_back(grad_cq, w_joint[:, 3 * D : 4 * D]))
+    grad_stream = grad_stream + grad_inner
+    grad_one = to_low(grad_stream * modulation[2 * D : 3 * D])
+    grad_gate_one = jnp.sum(grad_stream * branch_one, 0)
+    grad_ao = weight_grad(mixed_one, grad_one)
+    grad_q, grad_k, grad_v = attention_back(
+        self_proj[:, :D],
+        self_proj[:, D : 2 * D],
+        self_proj[:, 2 * D :],
+        probs_one,
+        dense_back(grad_one, w_back[:D]),
+    )
+    grad_self = to_low(jnp.concatenate([grad_q, grad_k, grad_v], -1))
+    grad_self_w = weight_grad(input_one, grad_self)
+    grad_inner, grad_shift_one, grad_scale_one = pull_one(dense_back(grad_self, w_joint[:, : 3 * D]))
+    grad_stream = grad_stream + grad_inner
+    grad_mod = jnp.concatenate(
+        [grad_shift_one, grad_scale_one, grad_gate_one, grad_shift_two, grad_scale_two, grad_gate_two]
+    )
+    grads = (
+        jnp.concatenate([grad_self_w, grad_query_w, grad_up], 1),
+        grad_text_w,
+        jnp.concatenate([grad_ao, grad_co, grad_down], 0),
+    )
+    return (grad_stream, grad_mod, grads, grad_gain)
+
+
 ROOT = math.sqrt(2.0 / math.pi)
 CUBE = 0.044715
-CHUNK = 64
+CHUNK = 160
 WIDE = 512
 
 
@@ -919,9 +1190,9 @@
 
 
 def over_columns(count, width, step):
-    @pl.loop(0, count // width)
-    def _(index):
-        step(pl.multiple_of(index * width, width))
+    for index in range(count // width):
+        step(index * width)
+        yield
 
 
 def scaled(values):
@@ -940,51 +1211,63 @@
     return jnp.sum(values, 0, keepdims=True)
 
 
-def probabilities(query, key, keep):
-    scores = dot_nt(query, key) * HEAD_DIM ** (-0.5)
-    scores = jnp.where(keep, scores, NEGATIVE)
-    shifted = jnp.exp(scores - jnp.max(scores, -1, keepdims=True))
-    return shifted * (1.0 / jnp.sum(shifted, -1, keepdims=True))
-
-
-def attend(q_at, k_at, v_at, keep, store):
+def attend(q_at, k_at, v_at, keep, stats, store):
     first = lax.broadcasted_iota(jnp.int32, (1, 2 * HEAD_DIM), 1) < HEAD_DIM
 
-    def pair(index):
-        query, key, value = q_at(index), k_at(index), v_at(index)
+    for index in range(HEADS // 2):
+        query, key = q_at(index) * HEAD_DIM ** (-0.5), k_at(index)
         zero = jnp.zeros_like(query)
-        out_a = dot_nn(to_low(probabilities(jnp.where(first, query, zero), key, keep)), value)
-        out_b = dot_nn(to_low(probabilities(jnp.where(first, zero, query), key, keep)), value)
-        store(index, to_low(jnp.where(first, out_a, out_b)))
+        value = jnp.transpose(v_at(index))
+        outs = []
+        for head in range(2):
+            mine = jnp.where(first, query, zero) if head == 0 else jnp.where(first, zero, query)
+            scores = jnp.where(keep, dot_nt(key, mine), NEGATIVE)
+            top = jnp.max(scores, 0, keepdims=True)
+            shifted = jnp.exp(scores - top)
+            total = jnp.sum(shifted, 0, keepdims=True)
+            stats[2 * index + head : 2 * index + head + 1, :] = top + jnp.log(total)
+            probs = to_low(shifted * (1.0 / total))
+            outs.append(dot_nn(value[head * HEAD_DIM : (head + 1) * HEAD_DIM], probs))
+        store(index, jnp.transpose(to_low(jnp.concatenate(outs, 0))))
+        yield
+
+
+def attend_back(q_at, k_at, v_at, grad_at, keep, stats, store):
+    first = lax.broadcasted_iota(jnp.int32, (1, 2 * HEAD_DIM), 1) < HEAD_DIM
 
     for index in range(HEADS // 2):
-        pair(index)
-
-
-def attend_back(q_at, k_at, v_at, grad_at, keep, store):
-    first = lax.broadcasted_iota(jnp.int32, (1, 2 * HEAD_DIM), 1) < HEAD_DIM
-
-    def pair(index):
-        query, key, value, grad = q_at(index), k_at(index), v_at(index), grad_at(index)
-        zero = jnp.zeros_like(query)
-        parts = []
-        for mine in (first, jnp.logical_not(first)):
-            probs = probabilities(jnp.where(mine, query, zero), key, keep)
-            grad_value = dot_tn(to_low(probs), grad)
-            grad_probs = dot_nt(jnp.where(mine, grad, zero), value)
-            inner = jnp.sum(probs * grad_probs, -1, keepdims=True)
+        query, key = q_at(index) * HEAD_DIM ** (-0.5), k_at(index)
+        value, grad = v_at(index), grad_at(index)
+        key_turned = jnp.transpose(key * HEAD_DIM ** (-0.5))
+        zero, zero_value = jnp.zeros_like(query), jnp.zeros_like(value)
+        queries, keys, values = [], [], []
+        for head in range(2):
+            mine = jnp.where(first, query, zero) if head == 0 else jnp.where(first, zero, query)
+            mine_value = jnp.where(first, value, zero_value) if head == 0 else jnp.where(first, zero_value, value)
+            scores = jnp.where(keep, dot_nt(key, mine), NEGATIVE)
+            probs = jnp.exp(scores - stats[2 * index + head : 2 * index + head + 1, :])
+            values.append(dot_nn(to_low(probs), grad))
+            grad_probs = dot_nt(mine_value, grad)
+            inner = jnp.sum(probs * grad_probs, 0, keepdims=True)
             grad_scores = to_low(probs * (grad_probs - inner))
-            grad_query = dot_nn(grad_scores, key) * HEAD_DIM ** (-0.5)
-            grad_key = dot_tn(grad_scores, query) * HEAD_DIM ** (-0.5)
-            parts.append((grad_query, grad_key, grad_value))
-        store(index, *(to_low(jnp.where(first, a, b)) for a, b in zip(*parts)))
-
-    for index in range(HEADS // 2):
-        pair(index)
+            keys.append(dot_nn(grad_scores, query))
+            queries.append(dot_nn(key_turned[head * HEAD_DIM : (head + 1) * HEAD_DIM], grad_scores))
+        store(
+            index,
+            jnp.transpose(to_low(jnp.concatenate(queries, 0))),
+            to_low(jnp.where(first, *keys)),
+            to_low(jnp.where(first, *values)),
+        )
+        yield
 
 
 def tile_of(ref, base):
     return lambda index: ref[:, base + index * 2 * HEAD_DIM : base + (index + 1) * 2 * HEAD_DIM]
+
+
+def run(steps):
+    for _ in steps:
+        pass
 
 
 SAVED = (
@@ -1001,6 +1284,8 @@
     ("stream3", D, jnp.float32),
     ("n3", D, jnp.bfloat16),
     ("branch3", D, jnp.float32),
+    ("stats1", None, jnp.float32),
+    ("stats2", None, jnp.float32),
 )
 GRADS = (
     ("g_self", 3 * D),
@@ -1015,6 +1300,9 @@
 KEPT = ("n1", "n2", "n3", "mixed1", "mixed2", "hidden") + tuple(name for name, _ in GRADS)
 
 
+NEEDED = ("stream", "qkv", "branch1", "stream2", "cq", "ckv", "stream3", "n3", "branch3", "stats1", "stats2")
+
+
 class Names:
     def __init__(self, **refs):
         self.__dict__.update(refs)
@@ -1028,6 +1316,7 @@
         s.n1[rows, :] = to_low(normed * (1.0 + mods[1:2, :]) + mods[0:1, :])
 
     over_rows(frames, norm_one)
+    yield
     emit("n1", s.n1)
     need("qkv")
 
@@ -1035,13 +1324,13 @@
         cols = pl.ds(column, 256)
         s.qkv[:, cols] = to_low(dot_nn(s.n1[...], w.win[:, cols]))
 
-    over_columns(3 * D, 256, project)
+    yield from over_columns(3 * D, 256, project)
     done("qkv")
 
     def mix_one(index, value):
         s.mixed1[:, index * 128 : (index + 1) * 128] = value
 
-    attend(tile_of(s.qkv, 0), tile_of(s.qkv, D), tile_of(s.qkv, 2 * D), frame_keep, mix_one)
+    yield from attend(tile_of(s.qkv, 0), tile_of(s.qkv, D), tile_of(s.qkv, 2 * D), frame_keep, s.stats1, mix_one)
     emit("mixed1", s.mixed1)
     need("ao")
 
@@ -1051,7 +1340,7 @@
         s.branch1[:, cols] = branch
         s.stream2[:, cols] = s.stream[:, cols] + mods[2:3, cols] * branch
 
-    over_columns(D, 256, branch_one)
+    yield from over_columns(D, 256, branch_one)
     done("ao")
 
     def norm_two(rows):
@@ -1059,6 +1348,7 @@
         s.n2[rows, :] = to_low(normed * mods[6:7, :])
 
     over_rows(frames, norm_two)
+    yield
     emit("n2", s.n2)
     need("cq")
 
@@ -1066,7 +1356,7 @@
         cols = pl.ds(column, 256)
         s.cq[:, cols] = to_low(dot_nn(s.n2[...], w.win[:, pl.ds(3 * D + column, 256)]))
 
-    over_columns(D, 256, project_cross)
+    yield from over_columns(D, 256, project_cross)
     done("cq")
     need("text")
 
@@ -1074,13 +1364,13 @@
         cols = pl.ds(column, 256)
         s.ckv[:, cols] = to_low(dot_nn(text[...], w.wtext[:, cols]))
 
-    over_columns(2 * D, 256, project_text)
+    yield from over_columns(2 * D, 256, project_text)
     done("text")
 
     def mix_two(index, value):
         s.mixed2[:, index * 128 : (index + 1) * 128] = value
 
-    attend(tile_of(s.cq, 0), tile_of(s.ckv, 0), tile_of(s.ckv, D), text_keep, mix_two)
+    yield from attend(tile_of(s.cq, 0), tile_of(s.ckv, 0), tile_of(s.ckv, D), text_keep, s.stats2, mix_two)
     emit("mixed2", s.mixed2)
     need("co")
 
@@ -1088,7 +1378,7 @@
         cols = pl.ds(column, 256)
         s.stream3[:, cols] = s.stream2[:, cols] + dot_nn(s.mixed2[...], w.wout[D : 2 * D, cols])
 
-    over_columns(D, 256, branch_two)
+    yield from over_columns(D, 256, branch_two)
     done("co")
 
     def norm_three(rows):
@@ -1096,6 +1386,7 @@
         s.n3[rows, :] = to_low(normed * (1.0 + mods[4:5, :]) + mods[3:4, :])
 
     over_rows(frames, norm_three)
+    yield
     emit("n3", s.n3)
     need("up")
 
@@ -1104,7 +1395,7 @@
         tanh = jnp.tanh(ROOT * (upper + CUBE * (upper * upper * upper)))
         hidden[:, pl.ds(column, WIDE)] = to_low(0.5 * upper * (1.0 + tanh))
 
-    over_columns(FF, WIDE, expand)
+    yield from over_columns(FF, WIDE, expand)
     done("up")
     emit("hidden", hidden)
     need("down")
@@ -1115,7 +1406,7 @@
         s.branch3[:, cols] = branch
         result[:, cols] = s.stream3[:, cols] + mods[5:6, cols] * branch
 
-    over_columns(D, 256, branch_three)
+    yield from over_columns(D, 256, branch_three)
     done("down")
 
 
@@ -1129,6 +1420,7 @@
         grad_mods[5:6, :] += row_sum(grad_out * s.branch3[rows, :])
 
     over_rows(frames, gate_three)
+    yield
     emit("g_three", g.g_three)
     need("down")
     need("up")
@@ -1142,14 +1434,14 @@
         slope = 0.5 * (1.0 + tanh) + (0.5 * ROOT) * upper * (1.0 - tanh * tanh) * (1.0 + (3.0 * CUBE) * square)
         g.g_pre[:, wide] = to_low(back * slope)
 
-    over_columns(FF, WIDE, shrink)
+    yield from over_columns(FF, WIDE, shrink)
     done("down")
     emit("g_pre", g.g_pre)
 
     def inner_three(column):
         inner[:, pl.ds(column, 256)] = dot_nt(g.g_pre[...], w.win[pl.ds(column, 256), 4 * D :])
 
-    over_columns(D, 256, inner_three)
+    yield from over_columns(D, 256, inner_three)
     done("up")
 
     def pull_three(rows):
@@ -1162,13 +1454,14 @@
         g.g_cross[rows, :] = to_low(total)
 
     over_rows(frames, pull_three)
+    yield
     emit("g_cross", g.g_cross)
     need("co")
 
     def back_cross(column):
         mixed[:, pl.ds(column, 256)] = to_low(dot_nt(g.g_cross[...], w.wout[pl.ds(D + column, 256), :]))
 
-    over_columns(D, 256, back_cross)
+    yield from over_columns(D, 256, back_cross)
     done("co")
 
     def store_cross(index, grad_query, grad_key, grad_value):
@@ -1177,8 +1470,8 @@
         g.g_ckv[:, cols] = grad_key
         g.g_ckv[:, D + index * 128 : D + (index + 1) * 128] = grad_value
 
-    attend_back(
-        tile_of(s.cq, 0), tile_of(s.ckv, 0), tile_of(s.ckv, D), tile_of(mixed, 0), text_keep, store_cross
+    yield from attend_back(
+        tile_of(s.cq, 0), tile_of(s.ckv, 0), tile_of(s.ckv, D), tile_of(mixed, 0), text_keep, s.stats2, store_cross
     )
     emit("g_cq", g.g_cq)
     emit("g_ckv", g.g_ckv)
@@ -1187,7 +1480,7 @@
     def inner_two(column):
         inner[:, pl.ds(column, 256)] = dot_nt(g.g_cq[...], w.win[pl.ds(column, 256), 3 * D : 4 * D])
 
-    over_columns(D, 256, inner_two)
+    yield from over_columns(D, 256, inner_two)
     done("cq")
 
     def pull_two(rows):
@@ -1200,13 +1493,14 @@
         grad_mods[2:3, :] += row_sum(total * s.branch1[rows, :])
 
     over_rows(frames, pull_two)
+    yield
     emit("g_one", g.g_one)
     need("ao")
 
     def back_self(column):
         mixed[:, pl.ds(column, 256)] = to_low(dot_nt(g.g_one[...], w.wout[pl.ds(column, 256), :]))
 
-    over_columns(D, 256, back_self)
+    yield from over_columns(D, 256, back_self)
     done("ao")
 
     def store_self(index, grad_query, grad_key, grad_value):
@@ -1215,8 +1509,8 @@
         g.g_self[:, D + index * 128 : D + (index + 1) * 128] = grad_key
         g.g_self[:, 2 * D + index * 128 : 2 * D + (index + 1) * 128] = grad_value
 
-    attend_back(
-        tile_of(s.qkv, 0), tile_of(s.qkv, D), tile_of(s.qkv, 2 * D), tile_of(mixed, 0), frame_keep, store_self
+    yield from attend_back(
+        tile_of(s.qkv, 0), tile_of(s.qkv, D), tile_of(s.qkv, 2 * D), tile_of(mixed, 0), frame_keep, s.stats1, store_self
     )
     emit("g_self", g.g_self)
     need("qkv")
@@ -1224,7 +1518,7 @@
     def inner_one(column):
         inner[:, pl.ds(column, 256)] = dot_nt(g.g_self[...], w.win[pl.ds(column, 256), : 3 * D])
 
-    over_columns(D, 256, inner_one)
+    yield from over_columns(D, 256, inner_one)
     done("qkv")
 
     def pull_one(rows):
@@ -1235,9 +1529,56 @@
         grad[rows, :] = grad[rows, :] + norm_pull(normed, factor, back * (1.0 + mods[1:2, :]))
 
     over_rows(frames, pull_one)
-
-
-def model_kernel(*refs):
+    yield
+
+
+def heights(frames, tokens):
+    return {name: tokens if name in ("ckv", "g_ckv") else 16 if name in ("stats1", "stats2") else frames for name in WIDTHS}
+
+
+WIDTHS = {**{name: width for name, width, _ in SAVED}, **dict(GRADS), "hidden": FF}
+KINDS = {**{name: kind for name, _, kind in SAVED}, **{name: jnp.bfloat16 for name, _ in GRADS}, "hidden": jnp.bfloat16}
+
+
+def shape_of(name, frames, tokens):
+    return (heights(frames, tokens)[name], WIDTHS[name] or frames)
+
+
+def weight_parts(source, target):
+    (w_in, w_text, w_out), (win, wtext, wout) = source, target
+    return {
+        "qkv": (w_in.at[:, : 3 * D], win.at[:, : 3 * D]),
+        "cq": (w_in.at[:, 3 * D : 4 * D], win.at[:, 3 * D : 4 * D]),
+        "up": (w_in.at[:, 4 * D :], win.at[:, 4 * D :]),
+        "text": (w_text, wtext),
+        "ao": (w_out.at[:D], wout.at[:D]),
+        "co": (w_out.at[D : 2 * D], wout.at[D : 2 * D]),
+        "down": (w_out.at[2 * D :], wout.at[2 * D :]),
+    }
+
+
+def keeps(lengths, frames, tokens):
+    return (
+        lax.broadcasted_iota(jnp.int32, (frames, 1), 0) < lengths[0],
+        lax.broadcasted_iota(jnp.int32, (tokens, 1), 0) < lengths[1],
+    )
+
+
+def lanes(first, count):
+    lane = lax.broadcasted_iota(jnp.int32, (1, 128), 1)
+    return jnp.logical_and(lane >= first, lane < first + count)
+
+
+def gain_pick():
+    row, lane = (lax.broadcasted_iota(jnp.int32, (8, 128), axis) for axis in range(2))
+    return jnp.logical_and(row < LAYERS, lane == GAIN_LANE + row)
+
+
+LEAD_LANE = 32
+GAIN_LANE = 64
+
+
+def model_kernel(channels, *refs):
     refs = list(refs)
 
     def take(count):
@@ -1245,32 +1586,33 @@
         del refs[:count]
         return taken
 
-    lengths, factor_ref, stream_ref, mods_ref, final_mods, text, noise, head = take(8)
+    lengths, facts, stream_ref, mods_ref, final_mods, text, noise, noisy, small = take(9)
     weights = [take(3) for _ in range(LAYERS)]
-    loss_ref, grad_ref, grad_mods_ref, grad_final, grad_head = take(5)
-    kept_out = [dict(zip(KEPT, take(len(KEPT)))) for _ in range(LAYERS)]
+    early = [dict(zip(NEEDED, take(len(NEEDED)))) for _ in range(LAYERS - 1)]
+    end_ref, grad_small, grad_tile = take(3)
+    kept_out = [dict(zip(KEPT if layer == LAYERS - 1 else GRAD_NAMES, take(len(KEPT) if layer == LAYERS - 1 else len(GRADS)))) for layer in range(LAYERS)]
     win, wtext, wout = take(3)
-    saved = [Names(**dict(zip((name for name, *_ in SAVED), take(len(SAVED))))) for _ in range(LAYERS)]
+    saved = [Names(**dict(zip((name for name, *_ in SAVED), take(len(SAVED)))))]
+    for _ in range(LAYERS - 1):
+        saved.insert(0, Names(**dict(zip(NEEDED, take(len(NEEDED))))))
     g = Names(**dict(zip((name for name, _ in GRADS), take(len(GRADS)))))
-    hidden, inner, mixed, final_low = take(4)
-    load_sem, keep_sem = refs
+    hidden, inner, mixed, final_low, grad_ref, grad_mods_ref, grad_final = take(7)
+    load_sem, keep_sem, early_sem = refs
     w = Names(win=win, wtext=wtext, wout=wout)
-    frames, tokens = stream_ref.shape[0], text.shape[0]
-    frame_keep = lax.broadcasted_iota(jnp.int32, (1, frames), 1) < lengths[0]
-    text_keep = lax.broadcasted_iota(jnp.int32, (1, tokens), 1) < lengths[1]
+    frames, tokens = noisy.shape[0], text.shape[0]
+    frame_keep, text_keep = keeps(lengths, frames, tokens)
+    last = LAYERS - 1
 
     def load(layer, part):
-        w_in, w_text, w_out = weights[layer]
-        source, target = {
-            "qkv": (w_in.at[:, : 3 * D], win.at[:, : 3 * D]),
-            "cq": (w_in.at[:, 3 * D : 4 * D], win.at[:, 3 * D : 4 * D]),
-            "up": (w_in.at[:, 4 * D :], win.at[:, 4 * D :]),
-            "text": (w_text, wtext),
-            "ao": (w_out.at[:D], wout.at[:D]),
-            "co": (w_out.at[D : 2 * D], wout.at[D : 2 * D]),
-            "down": (w_out.at[2 * D :], wout.at[2 * D :]),
-        }[part]
-        return pltpu.make_async_copy(source, target, load_sem.at[PARTS.index(part)])
+        return pltpu.make_async_copy(
+            *weight_parts(weights[layer], (win, wtext, wout))[part], load_sem.at[PARTS.index(part)]
+        )
+
+    def early_copies(layer):
+        return [
+            pltpu.make_async_copy(early[layer][name], getattr(saved[layer], name), early_sem.at[layer, j])
+            for j, name in enumerate(NEEDED)
+        ]
 
     flying = {}
 
@@ -1290,34 +1632,37 @@
             if copy is not None:
                 copy.wait()
 
-    nothing = lambda part: None
+    def nothing(part):
+        pass
+
     for part in ("qkv", "ao", "cq", "text", "co", "up", "down"):
-        load(0, part).start()
-    over_rows(frames, lambda rows: saved[0].stream.__setitem__((rows, slice(None)), stream_ref[rows, :]))
-    for layer in range(LAYERS):
-        last = layer == LAYERS - 1
-        if layer > 0:
-            settle(layer - 1, ("hidden",))
+        load(last, part).start()
+    for layer in range(last):
+        for copy in early_copies(layer):
+            copy.start()
+    over_rows(frames, lambda rows: saved[last].stream.__setitem__((rows, slice(None)), stream_ref[rows, :]))
+    run(
         block_forward(
-            saved[layer], hidden, grad_ref if last else saved[layer + 1].stream,
-            mods_ref.at[layer], text, frame_keep, text_keep, w,
-            lambda part: load(layer, part).wait(),
-            nothing if last else (lambda part: load(layer + 1, part).start()),
-            keep(layer),
+            saved[last], hidden, grad_ref, mods_ref.at[last], text, frame_keep, text_keep, w,
+            lambda part: load(last, part).wait(), nothing, keep(last),
         )
+    )
 
     def norm_final(rows):
         normed, _ = scaled(grad_ref[rows, :])
         final_low[rows, :] = to_low(normed * (1.0 + final_mods[1:2, :]) + final_mods[0:1, :])
 
     over_rows(frames, norm_final)
-    error = dot_nn(final_low[...], head[...]) - noise[...]
     counted = lax.broadcasted_iota(jnp.int32, (frames, 1), 0) < lengths[0]
-    error = jnp.where(counted, error, 0.0)
-    loss_ref[...] = jnp.broadcast_to(row_sum(error * error), loss_ref.shape)
-    grad_pred = to_low(error * factor_ref[0])
-    grad_head[...] = dot_tn(final_low[...], grad_pred)
-    inner[...] = dot_nt(grad_pred, head[...])
+    error = dot_nn(final_low[...], small[...]) - noise[...]
+    error = jnp.where(jnp.logical_and(counted, lanes(0, channels)), error, 0.0)
+    row, lane = (lax.broadcasted_iota(jnp.int32, end_ref.shape, axis) for axis in range(2))
+    own = jnp.where(jnp.logical_and(row == 2, lane == 0), jnp.full(end_ref.shape, lengths[0].astype(jnp.float32)), 0.0)
+    end_ref[...] = jnp.where(row == 1, jnp.broadcast_to(row_sum(error * error), end_ref.shape), own)
+    factor = 2.0 / jnp.sum(facts[:, 2, :], (0, 1), keepdims=True)
+    grad_pred = to_low(error * factor)
+    grad_small[...] = dot_tn(final_low[...], grad_pred)
+    inner[...] = dot_nt(grad_pred, small[...])
     grad_final[...] = jnp.zeros_like(grad_final)
 
     def pull_final(rows):
@@ -1329,60 +1674,90 @@
 
     over_rows(frames, pull_final)
     for layer in reversed(range(LAYERS)):
-        last = layer == LAYERS - 1
-        if not last:
+        if layer < last:
             settle(layer + 1, [name for name, _ in GRADS])
-        block_backward(
-            saved[layer], g, grad_ref, mods_ref.at[layer], grad_mods_ref.at[layer], inner, mixed,
-            frame_keep, text_keep, w,
-            nothing if last else (lambda part: load(layer, part).wait()),
-            nothing if layer == 0 else (lambda part: load(layer - 1, part).start()),
-            keep(layer),
+            for copy in early_copies(layer):
+                copy.wait()
+        run(
+            block_backward(
+                saved[layer], g, grad_ref, mods_ref.at[layer], grad_mods_ref.at[layer], inner, mixed,
+                frame_keep, text_keep, w,
+                nothing if layer == last else (lambda part: load(layer, part).wait()),
+                nothing if layer == 0 else (lambda part: load(layer - 1, part).start()),
+                keep(layer),
+            )
         )
+    over_rows(frames, lambda rows: final_low.__setitem__((rows, slice(None)), to_low(grad_ref[rows, :])))
+    gains = jnp.concatenate(
+        [grad_mods_ref[layer, 6:7, :] for layer in range(LAYERS)] + [jnp.zeros((8 - LAYERS, D), jnp.float32)], 0
+    )
+    grad_small[...] += dot_tn(final_low[...], noisy[...]) + lax.dot_general(
+        gains, gain_pick().astype(jnp.float32), (((0,), (0,)), ((), ())),
+        precision=lax.Precision.HIGHEST, preferred_element_type=jnp.float32,
+    )
+    grad_tile[...] = jnp.zeros_like(grad_tile)
+    pieces = [(grad_mods_ref.at[layer], j) for layer in range(LAYERS) for j in range(6)]
+    pieces += [(grad_final, j) for j in range(2)]
+    for p, (ref, j) in enumerate(pieces):
+        for k in range(D // 128):
+            part = ref[j : j + 1, k * 128 : (k + 1) * 128]
+            at = p * (D // 128) + k
+            grad_tile[at : at + 1, :] = to_low(part).astype(jnp.float32)
     for layer in range(LAYERS):
         settle(layer, KEPT)
 
 
-def run_model(stream, mods, final_mods, text, noise, head, lengths, factor, weights):
-    frames, tokens = stream.shape[0], text.shape[0]
+GRAD_NAMES = tuple(name for name, _ in GRADS)
+
+
+def run_model(lengths, facts, stream, mods, final_mods, text, noise, noisy, small, weights, early, channels):
+    frames, tokens = noisy.shape[0], text.shape[0]
     low, full = jnp.bfloat16, jnp.float32
-    widths = {**{name: width for name, width, _ in SAVED}, **dict(GRADS), "hidden": FF}
-
-    def height(name):
-        return tokens if name in ("ckv", "g_ckv") else frames
-
-    kept = [jax.ShapeDtypeStruct((height(name), widths[name]), low) for name in KEPT]
     shape = jax.ShapeDtypeStruct
     here, there = pl.BlockSpec(memory_space=pltpu.VMEM), pl.BlockSpec(memory_space=pl.ANY)
     scalar = pl.BlockSpec(memory_space=pltpu.SMEM)
+
+    def names(layer):
+        return KEPT if layer == LAYERS - 1 else GRAD_NAMES
+
+    def vmem(name):
+        return pltpu.VMEM(shape_of(name, frames, tokens), KINDS[name])
+
+    kept = [shape(shape_of(name, frames, tokens), low) for layer in range(LAYERS) for name in names(layer)]
+    early_flat = [layer[name] for layer in early for name in NEEDED]
     out = pl.pallas_call(
-        model_kernel,
-        out_shape=[
-            shape((8, noise.shape[1]), full),
-            shape((frames, D), full),
-            shape((LAYERS, 8, D), full),
-            shape((8, D), full),
-            shape((D, noise.shape[1]), full),
-        ]
-        + kept * LAYERS,
-        in_specs=[scalar, scalar] + [here] * 6 + [there] * (3 * LAYERS),
-        out_specs=[here] * 5 + [there] * (len(KEPT) * LAYERS),
+        functools.partial(model_kernel, channels),
+        out_shape=[shape((8, 128), full), shape((D, 128), full), shape(MOD_TILE, full)] + kept,
+        in_specs=[scalar] + [here] * 8 + [there] * (3 * LAYERS + len(early_flat)),
+        out_specs=[here] * 3 + [there] * len(kept),
         scratch_shapes=[pltpu.VMEM((D, JOINT), low), pltpu.VMEM((text.shape[1], 2 * D), low), pltpu.VMEM((2 * D + FF, D), low)]
-        + [pltpu.VMEM((height(name), width), kind) for name, width, kind in SAVED] * LAYERS
-        + [pltpu.VMEM((height(name), width), low) for name, width in GRADS]
+        + [vmem(name) for name, *_ in SAVED]
+        + [vmem(name) for name in NEEDED] * (LAYERS - 1)
+        + [vmem(name) for name, _ in GRADS]
         + [
             pltpu.VMEM((frames, FF), low),
             pltpu.VMEM((frames, D), full),
             pltpu.VMEM((frames, D), low),
             pltpu.VMEM((frames, D), low),
+            pltpu.VMEM((frames, D), full),
+            pltpu.VMEM((LAYERS, 8, D), full),
+            pltpu.VMEM((8, D), full),
             pltpu.SemaphoreType.DMA((len(PARTS),)),
             pltpu.SemaphoreType.DMA((LAYERS, len(KEPT))),
+            pltpu.SemaphoreType.DMA((LAYERS, len(NEEDED))),
         ],
         compiler_params=pltpu.CompilerParams(vmem_limit_bytes=VMEM_LIMIT),
-    )(lengths, factor, stream, mods, final_mods, text, noise, head, *[w for layer in weights for w in layer])
-    head_part, rest = out[:5], out[5:]
-    count = len(KEPT)
-    return head_part, [dict(zip(KEPT, rest[l * count : (l + 1) * count])) for l in range(LAYERS)]
+    )(
+        lengths, facts, stream, mods, final_mods, text, noise, noisy, small,
+        *[w for layer in weights for w in layer], *early_flat,
+    )
+    rest = list(out[3:])
+    made = []
+    for layer in range(LAYERS):
+        count = len(names(layer))
+        made.append(dict(zip(names(layer), rest[:count])))
+        rest = rest[count:]
+    return out[:3], made
 
 
 def adam_update(weight, grad, first, second, rate):
@@ -1396,11 +1771,256 @@
     return (first_new, second_new, weight_new)
 
 
+def adam_kernel(layers, *refs):
+    refs = list(refs)
+
+    def take(count):
+        taken = refs[:count]
+        del refs[:count]
+        return taken
+
+    final, grad_mod, time_two, small = take(4)
+    sums = take(3)
+    given = [take(3) for _ in range(4)]
+    results = [take(3) for _ in range(4)]
+    held = [take(3) for _ in range(4)]
+    grads = take(3)
+    load_sem, grad_sem, store_sem = refs
+    own = held[3][0].shape[0]
+    groups = [(member, layer) for layer in range(layers) for member in (0, 2)] + [(1, None), (3, None)]
+
+    def at(ref, layer):
+        return ref if layer is None else ref.at[layer]
+
+    def loads(number):
+        member, layer = groups[number]
+        copies = [
+            pltpu.make_async_copy(at(given[member][j], layer), at(held[member][j], layer), load_sem.at[number, j])
+            for j in range(3)
+        ]
+        if member < 3:
+            copies.append(
+                pltpu.make_async_copy(at(sums[member], layer), at(grads[member], layer), grad_sem.at[number])
+            )
+        return copies
+
+    def stores(number):
+        member, layer = groups[number]
+        return [
+            pltpu.make_async_copy(
+                at(held[member][(j + 1) % 3], layer), at(results[member][j], layer), store_sem.at[number, j]
+            )
+            for j in range(3)
+        ]
+
+    for number in range(len(groups)):
+        for copy in loads(number):
+            copy.start()
+    factor = CLIP_NORM / jnp.maximum(jnp.sqrt(final[0:1, 0:1]), CLIP_NORM)
+
+    def update(member, index, grad):
+        weight, first, second = held[member]
+        first_new, second_new, weight_new = adam_update(
+            weight[index], grad * factor, first[index], second[index], LEARN_RATE
+        )
+        first[index], second[index], weight[index] = first_new, second_new, weight_new
+
+    for number, (member, layer) in enumerate(groups):
+        for copy in loads(number):
+            copy.wait()
+        if member == 0:
+            for column in range(0, JOINT, 1536):
+                cols = slice(column, column + 1536)
+                update(0, (layer, slice(None), cols), grads[0][layer, :, cols])
+            for column in range(0, MOD, 1536):
+                start = layer * MOD + column
+                update(
+                    0, (layer, slice(None), slice(JOINT + column, JOINT + column + 1536)),
+                    grad_mod[:own, start : start + 1536],
+                )
+        elif member == 2:
+            for row in range(0, held[2][0].shape[1], 48):
+                rows = slice(row, row + 48)
+                update(2, (layer, rows), grads[2][layer, rows])
+        elif member == 1:
+            for other in range(layers):
+                for column in range(0, 2 * D, D):
+                    index = (other, slice(None), slice(column, column + D))
+                    update(1, index, grads[1][index])
+        else:
+            update(3, (slice(None), slice(0, D)), time_two[:own, :])
+            update(3, (slice(None), slice(D, 3 * D)), grad_mod[:own, layers * MOD : layers * MOD + 2 * D])
+            tail = held[3][0].shape[1] - 3 * D
+            update(3, (slice(None), slice(3 * D, 3 * D + tail)), small[:, :tail])
+        for copy in stores(number):
+            copy.start()
+    for number in range(len(groups)):
+        for copy in stores(number):
+            copy.wait()
+
+
+def run_adam(final, grad_mod, time_two, small, sums, given):
+    here, there = pl.BlockSpec(memory_space=pltpu.VMEM), pl.BlockSpec(memory_space=pl.ANY)
+    layers = given[0][0].shape[0]
+    full = jnp.float32
+    shapes = [group[0].shape for group in given]
+    count = 2 * layers + 2
+    sem = pltpu.SemaphoreType.DMA
+    out = pl.pallas_call(
+        functools.partial(adam_kernel, layers),
+        out_shape=[jax.ShapeDtypeStruct(shape, full) for shape in shapes for _ in range(3)],
+        in_specs=[here] * 4 + [there] * 15,
+        out_specs=[there] * 12,
+        scratch_shapes=[pltpu.VMEM(shape, full) for shape in shapes for _ in range(3)]
+        + [pltpu.VMEM(item.shape, full) for item in sums]
+        + [sem((count, 3)), sem((count,)), sem((count, 3))],
+        compiler_params=pltpu.CompilerParams(vmem_limit_bytes=VMEM_LIMIT),
+    )(final, grad_mod, time_two, small, *sums, *[item for group in given for item in group])
+    return [out[3 * k : 3 * k + 3] for k in range(4)]
+
+
 def tiles(values, lead=()):
     flat = values.reshape(lead + (-1,))
     short = -flat.shape[-1] % 1024
     flat = jnp.pad(flat, [(0, 0)] * len(lead) + [(0, short)])
     return flat.reshape(lead + (-1, 128))
+
+
+def fast_grads(ways, clean_latent, noise, text_low, text_lengths, timesteps, valid_frames, w_in, w_text, w_out, gains, w_lead, w_head):
+    count = ways[0] * ways[1]
+    own, channels = w_head.shape[0], noise.shape[-1]
+    rows = [w_in.shape[1], w_text.shape[1], w_out.shape[1]]
+    halves = [JOINT // 2, D, D // 2]
+    lead_low, head_low = to_low(w_lead), to_low(w_head)
+    mod_low = jnp.concatenate(
+        [to_low(w_in[layer, :, JOINT:]) for layer in range(LAYERS)] + [head_low[:, D : 3 * D]], 1
+    )
+    sinus = time_features(timesteps)
+    facts = jnp.concatenate([to_low(sinus).astype(jnp.float32)[0], valid_frames.astype(jnp.float32)])
+    wide = [(0, 0), (0, LEAD_LANE - channels)]
+    small = jnp.concatenate(
+        [
+            jnp.pad(head_low[:, 3 * D :].astype(jnp.float32), wide),
+            jnp.pad(lead_low[FREQS:].astype(jnp.float32).T, wide),
+            jnp.pad(to_low(gains).astype(jnp.float32).T, [(0, 0), (0, 128 - GAIN_LANE - LAYERS)]),
+        ],
+        1,
+    )
+    lead_own = jnp.pad(lead_low[:FREQS], [(0, 0), (0, 128 - own)])
+    head_own = jnp.pad(head_low[:, :D], [(0, SHARE - own), (0, 0)])
+    mod_own = jnp.pad(mod_low, [(0, SHARE - own), (0, 0)])
+    level = noise_level(timesteps)
+    noisy = jnp.sqrt(level) * clean_latent + jnp.sqrt(1.0 - level) * noise
+    noisy = jnp.pad(to_low(noisy), [(0, 0), (LEAD_LANE, 128 - LEAD_LANE - channels)])
+    lengths = jnp.concatenate([valid_frames, text_lengths])
+    items = plan(halves, range(LAYERS), GATHER_PATTERN)
+    weights, given, early = gather_weights(
+        [w_in, w_text, w_out], jnp.concatenate([tiles(facts), small], 0), lead_own, head_own, mod_own,
+        lengths, text_low, noisy, own, halves, ways, 1, items,
+    )
+    packed, pre_time, temb, block_mods, final_mods, small, stream = given
+    (ends, grad_small, grad_tile), kept = run_model(
+        lengths, packed, stream, block_mods, final_mods, text_low,
+        jnp.pad(noise, [(0, 0), (0, 128 - channels)]), noisy, small, weights, [early], channels,
+    )
+    kept[0] = {**early, **kept[0]}
+    items = plan(halves, list(reversed(range(LAYERS))), SCATTER_PATTERN)
+    rest = [grad_tile, grad_small.reshape(count, own, 128), ends, packed, pre_time, temb, head_own, mod_own]
+    *sums, grad_mod_w, grad_time_one, grad_time_two, small_sum, final = scatter_grads(
+        kept, text_low, rest, own, rows, halves, ways, 2, items
+    )
+    lead_grad = jnp.concatenate([grad_time_one[:, :own], small_sum[:, LEAD_LANE : LEAD_LANE + channels].T], 0)
+    gain_grad = small_sum[:, GAIN_LANE : GAIN_LANE + LAYERS].T
+    grads = (gain_grad, lead_grad), (final, grad_mod_w, grad_time_two, small_sum, sums)
+    return jnp.sum(final[1]), final[2, 0], jnp.sqrt(final[0, 0]), grads
+
+
+def plain_grads(ways, clean_latent, noise, text_low, text_lengths, timesteps, valid_frames, w_in, w_text, w_out, gains, w_lead, w_head):
+    count = ways[0] * ways[1]
+    own, channels = w_head.shape[0], noise.shape[-1]
+    frame_keep = lax.iota(jnp.int32, clean_latent.shape[0]) < valid_frames[0]
+    text_keep = lax.iota(jnp.int32, text_low.shape[0]) < text_lengths[0]
+
+    def to_all(values):
+        return lax.all_gather(values, ALL, axis=0, tiled=True)
+
+    def by_columns(values):
+        return values.transpose(1, 0, 2).reshape(values.shape[1], -1)
+
+    lead_low, head_low = to_low(w_lead), to_low(w_head)
+    frame_count = jnp.sum(to_all(valid_frames)).astype(jnp.float32)
+    sinus_all = to_low(time_features(to_all(timesteps)))
+    lead_in = by_columns(to_all(lead_low[None, FREQS:]))
+    head_pred = to_all(head_low[:, 3 * D :])
+    gains_all = by_columns(to_all(to_low(gains)[None])).astype(jnp.float32)
+    act_time, pull_time = jax.vjp(jax.nn.silu, dense(sinus_all, lead_low[:FREQS]))
+    act_low = to_low(act_time)
+    temb = dense(act_low, head_low[:, :D]).reshape(count, count, own).transpose(1, 0, 2)
+    temb = jnp.sum(lax.all_to_all(temb, ALL, 0, 0, tiled=True), 0)
+    cond, pull_cond = jax.vjp(jax.nn.silu, temb)
+    cond_low = to_low(cond)
+    mod_low = jnp.concatenate(
+        [to_low(w_in[layer, :, JOINT:]) for layer in range(LAYERS)] + [head_low[:, D : 3 * D]], 1
+    )
+    mods = jnp.sum(lax.all_to_all(dense(cond_low, mod_low)[:, None], ALL, 0, 0, tiled=True), 0)[0]
+    weights = [
+        [to_all(to_low(shard[layer])) for shard in (w_in[:, :, :JOINT], w_text, w_out)] for layer in range(LAYERS)
+    ]
+    level = noise_level(timesteps)
+    noisy_low = to_low(jnp.sqrt(level) * clean_latent + jnp.sqrt(1.0 - level) * noise)
+    stream = dense(noisy_low, lead_in)
+    saved = []
+    for layer in range(LAYERS):
+        stream, kept = layer_forward(
+            stream, mods[layer * MOD : (layer + 1) * MOD], text_low, frame_keep, text_keep,
+            (*weights[layer], gains_all[layer]),
+        )
+        saved.append(kept)
+    final_mod = mods[LAYERS * MOD :]
+    normed_final, pull_final = jax.vjp(modulate, stream, final_mod[:D], final_mod[D:])
+    final_low = to_low(normed_final)
+    error = dense(final_low, head_pred) - noise
+    loss_part = jnp.sum(jnp.where(frame_keep[:, None], error * error, 0.0))
+    grad_pred = to_low(jnp.where(frame_keep[:, None], error * (2.0 / frame_count), 0.0))
+    grad_pred_w = weight_grad(final_low, grad_pred)
+    grad_stream, grad_shift_f, grad_scale_f = pull_final(dense_back(grad_pred, head_pred))
+    grad_mods = [None] * LAYERS + [jnp.concatenate([grad_shift_f, grad_scale_f])]
+    big, grad_gains = [None] * LAYERS, [None] * LAYERS
+    for layer in reversed(range(LAYERS)):
+        grad_stream, grad_mods[layer], big[layer], grad_gains[layer] = layer_backward(
+            saved[layer], grad_stream, mods[layer * MOD : (layer + 1) * MOD], text_low,
+            (*weights[layer], gains_all[layer]),
+        )
+    grad_in_w = weight_grad(noisy_low, to_low(grad_stream))
+    sums = [
+        jnp.stack(
+            [lax.psum_scatter(big[layer][member], ALL, scatter_dimension=0, tiled=True) for layer in range(LAYERS)]
+        )
+        for member in range(3)
+    ]
+    mods_all = lax.all_gather(to_low(jnp.concatenate(grad_mods)), ALL, axis=0, tiled=False)
+    grad_mod_w = weight_grad(cond_low, mods_all)
+    (grad_temb,) = pull_cond(dense_back(mods_all, mod_low))
+    grad_temb = by_columns(lax.all_gather(to_low(grad_temb), ALL, axis=0, tiled=False))
+    grad_time_two = weight_grad(act_low, grad_temb)
+    (grad_pre_time,) = pull_time(dense_back(grad_temb, head_low[:, :D]))
+    grad_time_one = weight_grad(sinus_all, to_low(grad_pre_time))
+
+    def to_owner(values):
+        return lax.psum_scatter(values, ALL, scatter_dimension=0, tiled=True)
+
+    mod_grads = grad_mod_w[:, : LAYERS * MOD].reshape(own, LAYERS, MOD).transpose(1, 0, 2)
+    grad_list = [
+        jnp.concatenate([sums[0], mod_grads], 2),
+        sums[1],
+        sums[2],
+        to_owner(jnp.stack(grad_gains).T).T,
+        jnp.concatenate([grad_time_one, to_owner(grad_in_w.T).T], 0),
+        jnp.concatenate([grad_time_two, grad_mod_w[:, LAYERS * MOD :], to_owner(grad_pred_w)], 1),
+    ]
+    squares = sum((jnp.sum(item * item) for item in grad_list))
+    loss_sum, squares = lax.psum((loss_part, squares), ALL)
+    return loss_sum, frame_count, jnp.sqrt(squares), grad_list
 
 
 def body(
@@ -1430,158 +2050,30 @@
     first_head,
     second_head,
 ):
-    count = ways[0] * ways[1]
-    own = w_head.shape[0]
-    channels = noise.shape[-1]
-    clean_latent, noise, text_low = clean_latent[0], noise[0], text_feats[0]
-    frames, caption = clean_latent.shape[0], text_low.shape[0]
-    frame_keep = lax.iota(jnp.int32, frames) < valid_frames[0]
-    text_keep = lax.iota(jnp.int32, caption) < text_lengths[0]
-    rows = [w_in.shape[1], w_text.shape[1], w_out.shape[1]]
-    halves = [JOINT // 2, D, D // 2]
-    aligned = own <= SHARE and all(height % 8 == 0 for height in rows) and all(way % 2 == 0 for way in ways)
-
-    sinus = time_features(timesteps)
-    lead_low, head_low = to_low(w_lead), to_low(w_head)
-    small = jnp.concatenate(
-        [
-            lead_low[FREQS:].astype(jnp.float32).reshape(-1),
-            head_low[:, 3 * D :].astype(jnp.float32).reshape(-1),
-            to_low(gains).astype(jnp.float32).reshape(-1),
-        ]
-    )
-    facts = jnp.concatenate([to_low(sinus).astype(jnp.float32)[0], valid_frames.astype(jnp.float32)])
-    facts = jnp.concatenate([tiles(facts), tiles(small)], 0)
-    mod_low = jnp.concatenate(
-        [to_low(w_in[layer, :, JOINT:]) for layer in range(LAYERS)] + [head_low[:, D : 3 * D]], 1
-    )
-    if aligned:
-        lead_own = jnp.pad(lead_low[:FREQS], [(0, 0), (0, 128 - own)])
-        head_own = jnp.pad(head_low[:, :D], [(0, SHARE - own), (0, 0)])
-        mod_own = jnp.pad(mod_low, [(0, SHARE - own), (0, 0)])
-        items = plan(halves, range(LAYERS), GATHER_PATTERN)
-        weights, packed, pre_time, temb, mods = gather_weights(
-            [w_in, w_text, w_out], facts, lead_own, head_own, mod_own, own, halves, ways, 1, items
-        )
-        mods = mods.reshape(-1)
-    else:
-        weights = [
-            [
-                lax.all_gather(to_low(shard[layer]), ALL, axis=0, tiled=True)
-                for shard in (w_in[:, :, :JOINT], w_text, w_out)
-            ]
-            for layer in range(LAYERS)
-        ]
-        packed = lax.all_gather(facts, ALL, axis=0, tiled=False)
-        sinus_all = to_low(packed.reshape(count, -1)[:, :FREQS])
-        pre_time = dense(sinus_all, lead_low[:FREQS])
-        act_low = to_low(jax.nn.silu(pre_time))
-        temb = dense(act_low, head_low[:, :D]).reshape(count, count, own).transpose(1, 0, 2)
-        temb = jnp.sum(lax.all_to_all(temb, ALL, 0, 0, tiled=True), 0)
-        cond_low = to_low(jax.nn.silu(temb))
-        mods = jnp.sum(lax.all_to_all(dense(cond_low, mod_low)[:, None], ALL, 0, 0, tiled=True), 0)[0]
-    packed = packed.reshape(count, -1)
-    frame_count = jnp.sum(packed[:, FREQS])
-    small_all = packed[:, 1024:]
-    at = channels * own
-    lead_in = to_low(small_all[:, :at].reshape(count, channels, own).transpose(1, 0, 2).reshape(channels, D))
-    head_pred = to_low(small_all[:, at : 2 * at].reshape(D, channels))
-    gains_all = small_all[:, 2 * at : 2 * at + LAYERS * own].reshape(count, LAYERS, own)
-    gains_all = gains_all.transpose(1, 0, 2).reshape(LAYERS, D)
-
-    level = noise_level(timesteps)
-    noisy_low = to_low(jnp.sqrt(level) * clean_latent + jnp.sqrt(1.0 - level) * noise)
-    stream = dense(noisy_low, lead_in)
-    block_mods = jnp.concatenate(
-        [mods[: LAYERS * MOD].reshape(LAYERS, 6, D), gains_all[:, None], jnp.zeros((LAYERS, 1, D))], 1
-    )
-    final_mods = jnp.pad(mods[LAYERS * MOD : LAYERS * MOD + 2 * D].reshape(2, D), [(0, 6), (0, 0)])
-    short = [(0, 0), (0, 128 - channels)]
-    (loss_lanes, grad_stream, grad_blocks, grad_final, grad_pred_w), kept = run_model(
-        stream,
-        block_mods,
-        final_mods,
-        text_low,
-        jnp.pad(noise, short),
-        jnp.pad(head_pred, short),
-        jnp.concatenate([valid_frames, text_lengths]),
-        (2.0 / frame_count).reshape(1),
-        weights,
-    )
-    grad_pred_w = grad_pred_w[:, :channels]
-    grad_mods = jnp.concatenate([grad_blocks[:, :6].reshape(-1), grad_final[:2].reshape(-1)])
-    grad_in_w = weight_grad(noisy_low, to_low(grad_stream))
-    small_grads = jnp.concatenate(
-        [
-            grad_in_w.reshape(channels, count, own).transpose(1, 0, 2).reshape(count, -1),
-            grad_pred_w.reshape(count, -1),
-            grad_blocks[:, 6].reshape(LAYERS, count, own).transpose(1, 0, 2).reshape(count, -1),
-        ],
-        1,
-    )
-    if aligned:
-        items = plan(halves, list(reversed(range(LAYERS))), SCATTER_PATTERN)
-        rest = [
-            tiles(to_low(grad_mods).astype(jnp.float32)),
-            tiles(small_grads, (count,)),
-            loss_lanes,
-            packed.reshape(count, -1, 128),
-            pre_time,
-            temb,
-            head_own,
-            mod_own,
-        ]
-        *sums, grad_mod_w, grad_time_one, grad_time_two, small_sum, final = scatter_grads(
-            kept, text_low, rest, own, rows, halves, ways, 2, items
-        )
-        grad_mod_w, grad_time_two = grad_mod_w[:own], grad_time_two[:own]
-        grad_time_one = grad_time_one[:, :own]
-        small_sum = small_sum.reshape(-1)
-        loss_sum, squares = jnp.sum(final[1]), final[0, 0]
-    else:
-        sums = [[], [], []]
-        for k in kept:
-            joint = [weight_grad(k[a], k[b]) for a, b in (("n1", "g_self"), ("n2", "g_cq"), ("n3", "g_pre"))]
-            back = [weight_grad(k[a], k[b]) for a, b in (("mixed1", "g_one"), ("mixed2", "g_cross"), ("hidden", "g_three"))]
-            grads = (jnp.concatenate(joint, 1), weight_grad(text_low, k["g_ckv"]), jnp.concatenate(back, 0))
-            for member, grad in enumerate(grads):
-                sums[member].append(lax.psum_scatter(grad, ALL, scatter_dimension=0, tiled=True))
-        sums = [jnp.stack(part) for part in sums]
-        mods_all = lax.all_gather(to_low(grad_mods), ALL, axis=0, tiled=False)
-        grad_mod_w = weight_grad(cond_low, mods_all)
-        _, pull_cond = jax.vjp(jax.nn.silu, temb)
-        (grad_temb,) = pull_cond(dense_back(mods_all, mod_low))
-        grad_temb = lax.all_gather(to_low(grad_temb), ALL, axis=0, tiled=False)
-        grad_temb = grad_temb.transpose(1, 0, 2).reshape(count, D)
-        grad_time_two = weight_grad(act_low, grad_temb)
-        _, pull_time = jax.vjp(jax.nn.silu, pre_time)
-        (grad_pre_time,) = pull_time(dense_back(grad_temb, head_low[:, :D]))
-        grad_time_one = weight_grad(sinus_all, to_low(grad_pre_time))
-        small_sum = jnp.sum(lax.all_to_all(small_grads, ALL, 0, 0, tiled=True), 0)
-    mod_grads = grad_mod_w[:, : LAYERS * MOD].reshape(own, LAYERS, MOD).transpose(1, 0, 2)
-    grad_list = [
-        jnp.concatenate([sums[0], mod_grads], 2),
-        sums[1],
-        sums[2],
-        small_sum[2 * at : 2 * at + LAYERS * own].reshape(LAYERS, own),
-        jnp.concatenate([grad_time_one, small_sum[:at].reshape(channels, own)], 0),
-        jnp.concatenate(
-            [grad_time_two, grad_mod_w[:, LAYERS * MOD :], small_sum[at : 2 * at].reshape(own, channels)], 1
-        ),
-    ]
-    if not aligned:
-        local = jnp.stack([jnp.sum(loss_lanes[0]), sum((jnp.sum(item * item) for item in grad_list))])
-        loss_sum, squares = jnp.sum(lax.all_gather(local, ALL, axis=0, tiled=False), 0)
-    grad_norm = jnp.sqrt(squares)
+    aligned = all(shard.shape[1] % 8 == 0 for shard in (w_in, w_text, w_out)) and all(way % 2 == 0 for way in ways)
+    aligned = aligned and w_head.shape[0] <= SHARE and noise.shape[-1] <= LEAD_LANE
+    grads_of = fast_grads if aligned else plain_grads
+    loss_sum, frame_count, grad_norm, grads = grads_of(
+        ways, clean_latent[0], noise[0], text_feats[0], text_lengths, timesteps, valid_frames,
+        w_in, w_text, w_out, gains, w_lead, w_head,
+    )
     factor = CLIP_NORM / jnp.maximum(grad_norm, CLIP_NORM)
     params = (w_in, w_text, w_out, gains, w_lead, w_head)
     firsts = (first_in, first_text, first_out, first_gains, first_lead, first_head)
     seconds = (second_in, second_text, second_out, second_gains, second_lead, second_head)
     rates = (LEARN_RATE, LEARN_RATE, LEARN_RATE, GAIN_RATE, LEARN_RATE, LEARN_RATE)
-    results = []
-    for weight, grad, first, second, rate in zip(params, grad_list, firsts, seconds, rates):
-        results.extend(adam_update(weight, grad * factor, first, second, rate))
-    return (loss_sum, frame_count, grad_norm, *results)
+    results = [None] * 6
+    if aligned:
+        given = list(zip(params, firsts, seconds))
+        wide = (0, 1, 2, 5)
+        for k, made in zip(wide, run_adam(*grads[1], [given[k] for k in wide])):
+            results[k] = made
+        grads = dict(zip((3, 4), grads[0]))
+    else:
+        grads = dict(enumerate(grads))
+    for k, grad in grads.items():
+        results[k] = adam_update(params[k], grad * factor, firsts[k], seconds[k], rates[k])
+    return (loss_sum, frame_count, grad_norm, *(item for made in results for item in made))
 
 
 def solution(mesh):

time: 615 us -> 556 us (0.904)
  Pallas kernels: 558 us -> 528 us
  local copies, waits for them, and re-layouts: 24 us -> 11 us
  other arithmetic: 20.9 us -> 8.34 us
    pallas_call x1 -> x2, Pallas kernels: 130 us -> 90 us  [the longest x1 79.4 us: run_model(): pl.pallas_call(functools.partial(model_kernel, channels), out_shape=[shap...]
    pallas_call x1, Pallas kernels: 200 us -> 211 us  [gather_weights(): pl.pallas_call(functools.partial(gather_kernel, ways, rows, halves, items...]
    slice x18 -> x6, local copies, waits for them, and re-layouts: 11.6 us -> 2.25 us  [the longest x1 1.26 us: fast_grads(): return (jnp.sum(final[1]), final[2, 0], jnp.sqrt(final[0, 0]), grads)]
    sub x6 -> x2, other arithmetic: 9.29 us -> 0.67 us  [adam_update(): weight - rate * (first_hat / (jnp.sqrt(second_hat) + ADAM_EPSILON) + WEIG...]
where the time goes in v4:
time: 556 us; the launch traced here: 553 us
  Pallas kernels  528 us (95%)
  local copies, waits for them, and re-layouts  11 us (2%)
  other arithmetic  8.34 us (2%)
    pallas_call x1, Pallas kernels, scatter_grads(): pl.pallas_call(functools.partial(scatter_kernel, ways, rows, halves, item...  227 us
    pallas_call x1, Pallas kernels, gather_weights(): pl.pallas_call(functools.partial(gather_kernel, ways, rows, halves, items...  211 us
    pallas_call x1, Pallas kernels, run_model(): pl.pallas_call(functools.partial(model_kernel, channels), out_shape=[shap...  79.4 us

profile of v4, /device:TPU:0, one launch (start us, length us, event | category | flops | bytes accessed | tf_op | source)
XLA Modules:
  0.0 552.8 jit_solution(11040752254510375527)
XLA Ops:
  2.0 1.0 convert_element_type.60
  3.0 0.9 copy.90
  3.9 0.1 copy.106
  4.0 0.7 convert_element_type.62
  4.7 0.1 copy.91
  4.9 0.6 pad_maximum_fusion.refs_3_
  5.6 0.9 copy.94
  6.5 0.9 copy.93
  7.4 0.7 pad.45.refs_9_.refs_7_
  8.2 1.7 convert.21
  9.9 0.9 fusion.4.refs_6_.refs_34_
  10.8 0.6 pad.43.refs_5_.refs_33_
  12.1 0.6 pad_add_fusion.refs_7_.refs_0_
  12.7 0.6 pad.42.refs_4_
  13.3 211.0 %shard_map.391 = (bf16[4,2,2,48,6144]{4,3,2,1,0:T(8,128)(2,1)}, bf16[4,2,2,64,1536]{4,3,2,1,0:T(8,128)(2,1)}, bf16[4,2,2,288,768]{4,3,2,1,0:T(8,128)(2,1)}, bf16...) custom-call(f32[2,24,10752]{2,1,0:T(8,128)} %refs_7_.1, ...), custom_call_target="tpu_custom_call" | custom-call | tf_op jit(solution)/shard_map/pallas_call | solution.py:525
  224.3 0.7 pad.46.refs_6_
  225.0 79.4 %shard_map.392 = (f32[8,128]{1,0:T(8,128)}, f32[768,128]{1,0:T(8,128)}, f32[88,128]{1,0:T(8,128)}, bf16[320,2304]{1,0:T(8,128)(2,1)}, bf16[320,768]{1,0:T(8,128)...) custom-call(s32[2]{0:T(128)} %pad_add_fusion.refs_7_.refs_0_, ...), custom_call_target="tpu_custom_call" | custom-call | tf_op jit(solution)/shard_map/pallas_call | solution.py:1728
  304.4 227.5 %shard_map.393 = (f32[2,24,6144]{2,1,0:T(8,128)}, f32[2,32,1536]{2,1,0:T(8,128)}, f32[2,144,768]{2,1,0:T(8,128)}, f32[32,10752]{1,0:T(8,128)}, f32[256,32]{1,0:T...) custom-call(bf16[256,1024]{1,0:T(8,128)(2,1)} %bitcast.42, ...), custom_call_target="tpu_custom_call" | custom-call | tf_op jit(solution)/shard_map/pallas_call | solution.py:953
  531.9 1.0 copy.102
  532.9 0.8 slice_bitcast_fusion.2
  533.7 1.3 fusion.18
  535.7 0.7 multiply_subtract_fusion
  536.4 0.1 copy.96
  536.4 0.1 copy.97
  536.5 0.8 sqrt_add_fusion
  537.5 0.1 copy.101
  537.6 0.1 copy.100
  537.7 0.6 copy.105
  538.3 0.6 copy.103
  539.0 0.6 copy.104
  539.6 10.6 %shard_map.394 = (f32[2,24,10752]{2,1,0:T(8,128)}, f32[2,24,10752]{2,1,0:T(8,128)}, f32[2,24,10752]{2,1,0:T(8,128)}, f32[2,32,1536]{2,1,0:T(8,128)}, f32[2,32,15...) custom-call(f32[8,128]{1,0:T(8,128)} %get-tuple-element.145.refs_0_,, ...), custom_call_target="tpu_custom_call" | custom-call | tf_op jit(solution)/shard_map/pallas_call | solution.py:1869
  550.2 1.3 slice_reduce_fusion
  (29 shorter events, 0.4 us)
Async XLA Ops:
  304.3 231.3 %copy-start = (f32[276,24]{0,1:T(8,128)S(1)}, f32[276,24]{0,1:T(8,128)}, u32[]{:S(2)}) copy-start(f32[276,24]{0,1:T(8,128)} %param.34) | copy-start | bytes 79492
  304.4 231.3 %copy-start.1 = (f32[276,24]{0,1:T(8,128)S(1)}, f32[276,24]{0,1:T(8,128)}, u32[]{:S(2)}) copy-start(f32[276,24]{0,1:T(8,128)} %param.45) | copy-start | bytes 79492
  304.4 231.3 %copy-start.2 = (f32[276,24]{0,1:T(8,128)S(1)}, f32[276,24]{0,1:T(8,128)}, u32[]{:S(2)}) copy-start(f32[276,24]{0,1:T(8,128)} %param.44) | copy-start | bytes 79492
  304.4 232.0 %copy-start.4 = (f32[2,24]{1,0:T(2,128)S(1)}, f32[2,24]{1,0:T(2,128)}, u32[]{:S(2)}) copy-start(f32[2,24]{1,0:T(2,128)} %param.42) | copy-start | bytes 580
  304.4 232.1 %copy-start.5 = (f32[2,24]{1,0:T(2,128)S(1)}, f32[2,24]{1,0:T(2,128)}, u32[]{:S(2)}) copy-start(f32[2,24]{1,0:T(2,128)} %param.43) | copy-start | bytes 580
  304.4 233.1 %copy-start.3 = (f32[2,24]{1,0:T(2,128)S(1)}, f32[2,24]{1,0:T(2,128)}, u32[]{:S(2)}) copy-start(f32[2,24]{1,0:T(2,128)} %param.33) | copy-start | bytes 580

commit v5 on v4

--- a/solution.py
+++ b/solution.py
@@ -50,22 +50,6 @@
     spot = list(spot)
     spot[axis] = lax.rem(spot[axis] + steps, size)
     return tuple(spot)
-
-
-def greet_peers(sizes, spot, core):
-    barrier = pltpu.get_barrier_semaphore()
-    count = 1
-    pl.semaphore_signal(barrier, inc=1, device_id=device_at(spot, 1 - core), device_id_type=MESH)
-    for axis in range(3):
-        for steps in range(1, sizes[axis]):
-            count += 1
-            pl.semaphore_signal(
-                barrier,
-                inc=1,
-                device_id=device_at(moved(spot, axis, sizes[axis], steps), core),
-                device_id_type=MESH,
-            )
-    pl.semaphore_wait(barrier, count)
 
 
 def remote(source, target, send, recv, device):
@@ -256,9 +240,9 @@
         return taken
 
     shards = take(members)
-    facts_in, lead_own, head_own, mod_own, lengths, text, noisy = take(7)
+    w_head, facts_in, lead_turned, lengths, text, noisy = take(6)
     fulls = take(members * layers)
-    facts, pre_time, temb_own, block_mods, final_mods, small, result = take(7)
+    facts, pre_time, temb_own, block_mods, final_mods, small, result, head_own, mod_own = take(9)
     early = dict(zip(EARLY, take(len(EARLY))))
     totals, landed, mod_parts = take(3)
     mod_landed = take(4)
@@ -266,7 +250,7 @@
     mods, win, wtext, wout = take(4)
     saved = Names(**dict(zip((name for name, *_ in SAVED), take(len(SAVED)))))
     (hidden,) = take(1)
-    load_sem, keep_sem = take(2)
+    load_sem, keep_sem, mod_stage, head_stage, side_sem = take(5)
     rest = refs
     stages = rest[:members]
     blocks = rest[members : 2 * members]
@@ -386,13 +370,36 @@
 
     hops = Hops(sizes, spot, core)
 
+    bring = [
+        pltpu.make_async_copy(shards[0].at[layer, :, pl.ds(JOINT, MOD)], mod_stage.at[layer], side_sem.at[layer])
+        for layer in range(layers)
+    ]
+    bring.append(pltpu.make_async_copy(w_head.at[:, pl.ds(0, 3 * D)], head_stage, side_sem.at[layers]))
+    for copy in bring:
+        copy.start()
+
+    def low_rows(value):
+        return to_low(jnp.concatenate([value, jnp.zeros((SHARE - own, value.shape[1]), jnp.float32)], 0))
+
     def time_layers():
+        for copy in bring:
+            copy.wait()
+        head_own[...] = low_rows(head_stage[:, :D])
+        for layer in range(layers):
+            for column in range(0, MOD, D):
+                start_at = layer * MOD + column
+                mod_own[:, start_at : start_at + D] = low_rows(mod_stage[layer, :, column : column + D])
+        for column in range(0, 2 * D, D):
+            start_at = layers * MOD + column
+            mod_own[:, start_at : start_at + D] = low_rows(head_stage[:, D + column : 2 * D + column])
+        lead = lead_turned[:, :FREQS]
+        lead = to_low(jnp.concatenate([lead, jnp.zeros((128 - own, FREQS), jnp.float32)], 0))
         for step in range(1, count):
             origin = lax.rem(me + count - step, count)
             remote(
                 facts_in, facts.at[origin], facts_send.at[step], facts_recv.at[step], numbered(ways, origin)
             ).wait_recv()
-        value = dot_nn(to_low(facts[:, 0, :]), lead_own[:128, :]) + dot_nn(to_low(facts[:, 1, :]), lead_own[128:, :])
+        value = dot_nt(to_low(facts[:, 0, :]), lead[:, :128]) + dot_nt(to_low(facts[:, 1, :]), lead[:, 128:])
         pre_time[...] = value
         totals[0] = dot_nn(to_low(value * sigmoid(value))[:, :SHARE], head_own[...])
         sums[0]()
@@ -510,7 +517,7 @@
 EARLY = ("n1", "n2", "n3", "mixed1", "mixed2", "hidden", "stream", "qkv", "branch1", "stream2", "cq", "ckv", "stream3", "branch3", "stats1", "stats2")
 
 
-def gather_weights(shards, facts, lead_own, head_own, mod_own, lengths, text, noisy, own, halves, ways, number, items):
+def gather_weights(shards, w_head, facts, lead_turned, lengths, text, noisy, own, halves, ways, number, items):
     layers = shards[0].shape[0]
     rows = [s.shape[1] for s in shards]
     members = len(shards)
@@ -535,10 +542,12 @@
             shape((8, D), full),
             shape((D, 128), jnp.bfloat16),
             shape((frames, D), full),
+            shape((SHARE, D), jnp.bfloat16),
+            shape((SHARE, MOD_ROWS * 128), jnp.bfloat16),
         ]
         + [shape(shape_of(name, frames, tokens), KINDS[name]) for name in EARLY],
-        in_specs=[there] * members + [here] * 4 + [scalar] + [here] * 2,
-        out_specs=[there] * count + [here] * 7 + [there] * len(EARLY),
+        in_specs=[there] * (members + 1) + [here] * 2 + [scalar] + [here] * 2,
+        out_specs=[there] * count + [here] * 9 + [there] * len(EARLY),
         scratch_shapes=[
             vmem((len(ROUNDS) + 1, devices, D), full),
             vmem((sizes[0] + sizes[1] + sizes[2] - 2, devices, D), full),
@@ -551,6 +560,7 @@
         + [vmem((text.shape[1], 2 * D), jnp.bfloat16), vmem((2 * D + FF, D), jnp.bfloat16)]
         + [vmem(shape_of(name, frames, tokens), kind) for name, _, kind in SAVED]
         + [vmem((frames, FF), jnp.bfloat16), sem((len(PARTS),)), sem((len(EARLY),))]
+        + [vmem((layers, own, MOD), full), vmem((own, 3 * D), full), sem((layers + 1,))]
         + [vmem((layers, 2 * rows[m], halves[m]), full) for m in range(members)]
         + [vmem((layers, 2 * rows[m], halves[m]), jnp.bfloat16) for m in range(members)]
         + [sem((count,))] * 4
@@ -558,16 +568,16 @@
         compiler_params=pltpu.CompilerParams(
             collective_id=number, has_side_effects=True, vmem_limit_bytes=VMEM_LIMIT
         ),
-    )(*shards, facts, lead_own, head_own, mod_own, lengths, text, noisy)
+    )(*shards, w_head, facts, lead_turned, lengths, text, noisy)
     weights = [
         [out[l * members + m].reshape(-1, 2 * halves[m]) for m in range(members)] for l in range(layers)
     ]
-    return weights, out[count : count + 7], dict(zip(EARLY, out[count + 7 :]))
+    return weights, out[count : count + 9], dict(zip(EARLY, out[count + 9 :]))
 
 
 ORDERS = ((0, 2, 1), (0, 1, 2), (2, 0, 1), (1, 0, 2))
 GATHER_LAGS = ((-1.5, 0.0, 3.0, 7.5), (-3.0, 0.0, 2.0, 6.5))
-SCATTER_LAGS = ((-2.0, 0.0, 4.5, 7.5, 9.0), (-2.0, 0.0, 4.5, 6.5, 9.5))
+SCATTER_LAGS = ((-2.0, 0.0, 3.0, 5.0, 7.0), (-2.0, 0.0, 3.0, 5.0, 7.0))
 GATHER_PATTERN = (1, 0, 1, 2, 1, 1, 0, 1, 0, 1, 2, 1, 2, 1, 3, 1, 2, 1)
 SCATTER_PATTERN = GATHER_PATTERN[::-1]
 
@@ -622,10 +632,11 @@
     sends, recvs = sems[0::2], sems[1::2]
     sizes, spot, core = place(ways)
     partner = device_at(spot, 1 - core)
-    greet_peers(sizes, spot, core)
     frames = hidden.shape[0]
     sent_all = []
+    count = ways[0] * ways[1]
     me = lax.axis_index("dp") * ways[1] + lax.axis_index("fsdp")
+    greet_all(ways, me)
     hops = Hops(sizes, spot, core)
     squares[...] = jnp.zeros_like(squares)
 
@@ -682,7 +693,7 @@
         grad_time_two[...] = dot_tn(act, grad_temb)
         grad_time = to_low(dot_nt(grad_temb, head_own[...]) * slope_time)
         for j in range(2):
-            grad_time_one[j * 128 : (j + 1) * 128, :] = dot_tn(to_low(facts[:, j, :]), grad_time)
+            grad_time_one[:, j * 128 : (j + 1) * 128] = dot_tn(grad_time, to_low(facts[:, j, :]))
         count_squares(grad_time_two[...])
         count_squares(grad_time_one[...])
         count_squares(small_out[...])
@@ -890,10 +901,21 @@
     for step in side:
         step()
     lane = lax.broadcasted_iota(jnp.int32, squares.shape, 0)
-    ends[0] = jnp.where(lane == 0, squares[...], loss_in[...])
-    for step in sum_steps(hops, ends, end_landed, end_send, end_recv, sent_all):
-        step()
-    final[...] = ends[len(ROUNDS)]
+    ends[...] = jnp.where(lane == 0, squares[...], loss_in[...])
+    for step in range(1, count):
+        send(
+            remote(
+                ends, end_landed.at[me], end_send.at[step], end_recv.at[step],
+                numbered(ways, lax.rem(me + step, count)),
+            )
+        )
+    end_landed[me] = ends[...]
+    for step in range(1, count):
+        origin = lax.rem(me + count - step, count)
+        remote(
+            ends, end_landed.at[origin], end_send.at[step], end_recv.at[step], numbered(ways, origin)
+        ).wait_recv()
+    final[...] = jnp.sum(end_landed[...], 0)
     for i in range(n):
         e_copy(i).wait()
         o_copy(i).wait()
@@ -931,8 +953,8 @@
         vmem((sizes[0] + sizes[1] + sizes[2] - 2, devices, D), full),
         vmem((8, 128), full),
     ]
-    scratch += split_shapes(sizes, tile) + [sums] * 8
-    scratch += [vmem((len(ROUNDS) + 1, 8, 128), full), vmem((sizes[0] + sizes[1] + sizes[2] - 2, 8, 128), full)]
+    scratch += split_shapes(sizes, tile) + [sums] * 6 + [sem((devices,))] * 2
+    scratch += [vmem((8, 128), full), vmem((devices, 8, 128), full)]
     scratch += [vmem((devices, SHARE), full), vmem((devices, 8, 128), full), sem((2,))]
     scratch += [
         vmem((3, frames, D), low),
@@ -957,7 +979,7 @@
         ]
         + [
             jax.ShapeDtypeStruct((SHARE, MOD_ROWS * 128), full),
-            jax.ShapeDtypeStruct((FREQS, SHARE), full),
+            jax.ShapeDtypeStruct((SHARE, FREQS), full),
             jax.ShapeDtypeStruct((SHARE, D), full),
             jax.ShapeDtypeStruct(tile, full),
             jax.ShapeDtypeStruct((8, 128), full),
@@ -1779,15 +1801,15 @@
         del refs[:count]
         return taken
 
-    final, grad_mod, time_two, small = take(4)
+    final, grad_mod, time_one, time_two, small = take(5)
     sums = take(3)
-    given = [take(3) for _ in range(4)]
-    results = [take(3) for _ in range(4)]
-    held = [take(3) for _ in range(4)]
+    given = [take(3) for _ in range(6)]
+    results = [take(3) for _ in range(6)]
+    held = [take(3) for _ in range(6)]
     grads = take(3)
     load_sem, grad_sem, store_sem = refs
     own = held[3][0].shape[0]
-    groups = [(member, layer) for layer in range(layers) for member in (0, 2)] + [(1, None), (3, None)]
+    groups = [(member, layer) for layer in range(layers) for member in (0, 2)] + [(1, None), (3, None), (4, None), (5, None)]
 
     def at(ref, layer):
         return ref if layer is None else ref.at[layer]
@@ -1818,10 +1840,10 @@
             copy.start()
     factor = CLIP_NORM / jnp.maximum(jnp.sqrt(final[0:1, 0:1]), CLIP_NORM)
 
-    def update(member, index, grad):
+    def update(member, index, grad, rate=LEARN_RATE):
         weight, first, second = held[member]
         first_new, second_new, weight_new = adam_update(
-            weight[index], grad * factor, first[index], second[index], LEARN_RATE
+            weight[index], grad * factor, first[index], second[index], rate
         )
         first[index], second[index], weight[index] = first_new, second_new, weight_new
 
@@ -1847,6 +1869,13 @@
                 for column in range(0, 2 * D, D):
                     index = (other, slice(None), slice(column, column + D))
                     update(1, index, grads[1][index])
+        elif member == 4:
+            update(4, (slice(None), slice(0, FREQS)), time_one[:own, :])
+            tail = held[4][0].shape[1] - FREQS
+            update(4, (slice(None), slice(FREQS, FREQS + tail)), small[:, LEAD_LANE : LEAD_LANE + tail])
+        elif member == 5:
+            turned = jnp.transpose(small[...])
+            update(5, (slice(None), slice(None)), turned[GAIN_LANE : GAIN_LANE + layers, :], GAIN_RATE)
         else:
             update(3, (slice(None), slice(0, D)), time_two[:own, :])
             update(3, (slice(None), slice(D, 3 * D)), grad_mod[:own, layers * MOD : layers * MOD + 2 * D])
@@ -1859,24 +1888,24 @@
             copy.wait()
 
 
-def run_adam(final, grad_mod, time_two, small, sums, given):
+def run_adam(final, grad_mod, time_one, time_two, small, sums, given):
     here, there = pl.BlockSpec(memory_space=pltpu.VMEM), pl.BlockSpec(memory_space=pl.ANY)
     layers = given[0][0].shape[0]
     full = jnp.float32
     shapes = [group[0].shape for group in given]
-    count = 2 * layers + 2
+    count = 2 * layers + 4
     sem = pltpu.SemaphoreType.DMA
     out = pl.pallas_call(
         functools.partial(adam_kernel, layers),
         out_shape=[jax.ShapeDtypeStruct(shape, full) for shape in shapes for _ in range(3)],
-        in_specs=[here] * 4 + [there] * 15,
-        out_specs=[there] * 12,
+        in_specs=[here] * 5 + [there] * 21,
+        out_specs=[there] * 18,
         scratch_shapes=[pltpu.VMEM(shape, full) for shape in shapes for _ in range(3)]
         + [pltpu.VMEM(item.shape, full) for item in sums]
         + [sem((count, 3)), sem((count,)), sem((count, 3))],
         compiler_params=pltpu.CompilerParams(vmem_limit_bytes=VMEM_LIMIT),
-    )(final, grad_mod, time_two, small, *sums, *[item for group in given for item in group])
-    return [out[3 * k : 3 * k + 3] for k in range(4)]
+    )(final, grad_mod, time_one, time_two, small, *sums, *[item for group in given for item in group])
+    return [out[3 * k : 3 * k + 3] for k in range(6)]
 
 
 def tiles(values, lead=()):
@@ -1891,34 +1920,26 @@
     own, channels = w_head.shape[0], noise.shape[-1]
     rows = [w_in.shape[1], w_text.shape[1], w_out.shape[1]]
     halves = [JOINT // 2, D, D // 2]
-    lead_low, head_low = to_low(w_lead), to_low(w_head)
-    mod_low = jnp.concatenate(
-        [to_low(w_in[layer, :, JOINT:]) for layer in range(LAYERS)] + [head_low[:, D : 3 * D]], 1
-    )
     sinus = time_features(timesteps)
     facts = jnp.concatenate([to_low(sinus).astype(jnp.float32)[0], valid_frames.astype(jnp.float32)])
     wide = [(0, 0), (0, LEAD_LANE - channels)]
     small = jnp.concatenate(
         [
-            jnp.pad(head_low[:, 3 * D :].astype(jnp.float32), wide),
-            jnp.pad(lead_low[FREQS:].astype(jnp.float32).T, wide),
+            jnp.pad(to_low(w_head[:, 3 * D :]).astype(jnp.float32), wide),
+            jnp.pad(to_low(w_lead[FREQS:]).astype(jnp.float32).T, wide),
             jnp.pad(to_low(gains).astype(jnp.float32).T, [(0, 0), (0, 128 - GAIN_LANE - LAYERS)]),
         ],
         1,
     )
-    lead_own = jnp.pad(lead_low[:FREQS], [(0, 0), (0, 128 - own)])
-    head_own = jnp.pad(head_low[:, :D], [(0, SHARE - own), (0, 0)])
-    mod_own = jnp.pad(mod_low, [(0, SHARE - own), (0, 0)])
     level = noise_level(timesteps)
     noisy = jnp.sqrt(level) * clean_latent + jnp.sqrt(1.0 - level) * noise
     noisy = jnp.pad(to_low(noisy), [(0, 0), (LEAD_LANE, 128 - LEAD_LANE - channels)])
     lengths = jnp.concatenate([valid_frames, text_lengths])
     items = plan(halves, range(LAYERS), GATHER_PATTERN)
     weights, given, early = gather_weights(
-        [w_in, w_text, w_out], jnp.concatenate([tiles(facts), small], 0), lead_own, head_own, mod_own,
-        lengths, text_low, noisy, own, halves, ways, 1, items,
-    )
-    packed, pre_time, temb, block_mods, final_mods, small, stream = given
+        [w_in, w_text, w_out], w_head, jnp.concatenate([tiles(facts), small], 0), w_lead.T, lengths, text_low, noisy, own, halves, ways, 1, items,
+    )
+    packed, pre_time, temb, block_mods, final_mods, small, stream, head_own, mod_own = given
     (ends, grad_small, grad_tile), kept = run_model(
         lengths, packed, stream, block_mods, final_mods, text_low,
         jnp.pad(noise, [(0, 0), (0, 128 - channels)]), noisy, small, weights, [early], channels,
@@ -1929,9 +1950,7 @@
     *sums, grad_mod_w, grad_time_one, grad_time_two, small_sum, final = scatter_grads(
         kept, text_low, rest, own, rows, halves, ways, 2, items
     )
-    lead_grad = jnp.concatenate([grad_time_one[:, :own], small_sum[:, LEAD_LANE : LEAD_LANE + channels].T], 0)
-    gain_grad = small_sum[:, GAIN_LANE : GAIN_LANE + LAYERS].T
-    grads = (gain_grad, lead_grad), (final, grad_mod_w, grad_time_two, small_sum, sums)
+    grads = final, grad_mod_w, grad_time_one, grad_time_two, small_sum, sums
     return jnp.sum(final[1]), final[2, 0], jnp.sqrt(final[0, 0]), grads
 
 
@@ -2065,14 +2084,13 @@
     results = [None] * 6
     if aligned:
         given = list(zip(params, firsts, seconds))
-        wide = (0, 1, 2, 5)
-        for k, made in zip(wide, run_adam(*grads[1], [given[k] for k in wide])):
-            results[k] = made
-        grads = dict(zip((3, 4), grads[0]))
+        order = (0, 1, 2, 5, 4, 3)
+        given[4] = tuple(item.T for item in given[4])
+        for k, made in zip(order, run_adam(*grads, [given[k] for k in order])):
+            results[k] = [item.T for item in made] if k == 4 else made
     else:
-        grads = dict(enumerate(grads))
-    for k, grad in grads.items():
-        results[k] = adam_update(params[k], grad * factor, firsts[k], seconds[k], rates[k])
+        for k, grad in enumerate(grads):
+            results[k] = adam_update(params[k], grad * factor, firsts[k], seconds[k], rates[k])
     return (loss_sum, frame_count, grad_norm, *(item for made in results for item in made))
 
 

time: 556 us -> 537 us (0.966)
  Pallas kernels: 528 us -> 519 us
    pallas_call x1, Pallas kernels: 227 us -> 218 us  [scatter_grads(): pl.pallas_call(functools.partial(scatter_kernel, ways, rows, halves, item...]
where the time goes in v5:
time: 537 us; the launch traced here: 534 us
  Pallas kernels  519 us (97%)
  local copies, waits for them, and re-layouts  5.92 us (1%)
    pallas_call x1, Pallas kernels, scatter_grads(): pl.pallas_call(functools.partial(scatter_kernel, ways, rows, halves, item...  218 us
    pallas_call x1, Pallas kernels, gather_weights(): pl.pallas_call(functools.partial(gather_kernel, ways, rows, halves, items...  211 us
    pallas_call x1, Pallas kernels, run_model(): pl.pallas_call(functools.partial(model_kernel, channels), out_shape=[shap...  79.5 us
    pallas_call x1, Pallas kernels, run_adam(): pl.pallas_call(functools.partial(adam_kernel, layers), out_shape=[jax.Sha...  11.3 us

profile of v5, /device:TPU:0, one launch (start us, length us, event | category | flops | bytes accessed | tf_op | source)
XLA Modules:
  0.0 533.6 jit_solution(4582985584332563916)
XLA Ops:
  2.8 0.6 pad_add_fusion.refs_6_.refs_0_
  3.3 0.7 convert_element_type.42
  4.1 0.1 copy.45
  4.2 0.7 fusion.8
  4.9 0.7 slice.29
  5.6 0.1 fusion.7
  5.7 0.6 pad_maximum_fusion.refs_4_
  6.3 0.9 copy.47
  7.2 0.7 pad.31.refs_6_
  7.9 0.9 copy.46
  8.8 0.7 pad.30.refs_8_.refs_7_
  9.5 210.6 %shard_map.391 = (bf16[4,2,2,48,6144]{4,3,2,1,0:T(8,128)(2,1)}, bf16[4,2,2,64,1536]{4,3,2,1,0:T(8,128)(2,1)}, bf16[4,2,2,288,768]{4,3,2,1,0:T(8,128)(2,1)}, bf16...) custom-call(f32[2,24,10752]{2,1,0:T(8,128)} %refs_8_.1, ...), custom_call_target="tpu_custom_call" | custom-call | tf_op jit(solution)/shard_map/pallas_call | solution.py:532
  220.1 79.5 %shard_map.392 = (f32[8,128]{1,0:T(8,128)}, f32[768,128]{1,0:T(8,128)}, f32[88,128]{1,0:T(8,128)}, bf16[320,2304]{1,0:T(8,128)(2,1)}, bf16[320,768]{1,0:T(8,128)...) custom-call(s32[2]{0:T(128)} %pad_add_fusion.refs_6_.refs_0_, ...), custom_call_target="tpu_custom_call" | custom-call | tf_op jit(solution)/shard_map/pallas_call | solution.py:1750
  299.6 218.1 %shard_map.393 = (f32[2,24,6144]{2,1,0:T(8,128)}, f32[2,32,1536]{2,1,0:T(8,128)}, f32[2,144,768]{2,1,0:T(8,128)}, f32[32,10752]{1,0:T(8,128)}, f32[32,256]{1,0:T...) custom-call(bf16[256,1024]{1,0:T(8,128)(2,1)} %bitcast.36, ...), custom_call_target="tpu_custom_call" | custom-call | tf_op jit(solution)/shard_map/pallas_call | solution.py:975
  517.7 1.3 slice_reduce_fusion
  519.0 1.3 fusion.10
  521.0 11.3 %shard_map.394 = (f32[2,24,10752]{2,1,0:T(8,128)}, f32[2,24,10752]{2,1,0:T(8,128)}, f32[2,24,10752]{2,1,0:T(8,128)}, f32[2,32,1536]{2,1,0:T(8,128)}, f32[2,32,15...) custom-call(f32[8,128]{1,0:T(8,128)} %get-tuple-element.155.refs_0_,, ...), custom_call_target="tpu_custom_call" | custom-call | tf_op jit(solution)/shard_map/pallas_call | solution.py:1898
  (4 shorter events, 0.1 us)

commit v6 on v5

--- a/solution.py
+++ b/solution.py
@@ -453,11 +453,9 @@
 
     def first_block():
         frame_keep, text_keep = keeps(lengths, noisy.shape[0], text.shape[0])
-        for part in ("qkv", "ao", "cq", "text", "co", "up", "down"):
-            load(part).start()
         yield from block_forward(
             saved, hidden, result, block_mods.at[0], text, frame_keep, text_keep,
-            Names(win=win, wtext=wtext, wout=wout), lambda part: load(part).wait(), lambda part: None, emit,
+            Names(win=win, wtext=wtext, wout=wout), need, lambda part: None, emit,
         )
         for name in NEEDED:
             if name not in KEPT:
@@ -467,14 +465,38 @@
         full(0, member).reshape(sizes[0] * sizes[1] * sizes[2] * 2 * rows[member], 2 * halves[member]) for member in range(members)
     ]
     order = schedule(items, GATHER_LAGS)
-    turn = max(k for k, (i, _) in enumerate(order) if items[i][0] == 0) + 1
-    waited = set()
+    members_of = {"text": 1, "ao": 2, "co": 2, "down": 2}
+
+    def pieces_of(part):
+        found = []
+        for i, (layer, member, begin, _, _) in enumerate(items):
+            if layer == 0 and member == members_of.get(part, 0):
+                if part not in ("qkv", "cq") or (begin < 3 * D) == (part == "qkv"):
+                    found.append(i)
+        return found
+
+    turn = max(order.index((i, 3)) for i in pieces_of("qkv")) + 1
+    later = list(order[turn:])
+    finished, waited = set(), set()
 
     def advance(i, phase):
         if phase > 0:
             finish(i, phase - 1)
         if phase < 3:
             start(i, phase)
+        else:
+            finished.add(i)
+
+    def need(part):
+        for i in pieces_of(part):
+            while i not in finished:
+                advance(*later.pop(0))
+            if i not in waited:
+                waited.add(i)
+                c_wait(i)
+                own_put(*items[i][:2])
+        load(part).start()
+        load(part).wait()
 
     for i, phase in order[:turn]:
         if phase in (1, 2) and side:
@@ -484,12 +506,6 @@
         step()
     side = []
     prepare()
-    for i in range(len(items)):
-        if items[i][0] == 0:
-            c_wait(i)
-            waited.add(i)
-            own_put(*items[i][:2])
-    later = list(order[turn:])
     pace = BLOCK_PARTS / max(len(later), 1)
     for part, _ in enumerate(first_block()):
         if later and part >= pace * (len(order) - turn - len(later)):

time: 537 us -> 546 us (1.017)
  Pallas kernels: 519 us -> 529 us
where the time goes in v6:
time: 546 us; the launch traced here: 543 us
  Pallas kernels  529 us (97%)
  local copies, waits for them, and re-layouts  5.92 us (1%)
    pallas_call x1, Pallas kernels, scatter_grads(): pl.pallas_call(functools.partial(scatter_kernel, ways, rows, halves, item...  222 us
    pallas_call x1, Pallas kernels, gather_weights(): pl.pallas_call(functools.partial(gather_kernel, ways, rows, halves, items...  216 us
    pallas_call x1, Pallas kernels, run_model(): pl.pallas_call(functools.partial(model_kernel, channels), out_shape=[shap...  79.5 us
    pallas_call x1, Pallas kernels, run_adam(): pl.pallas_call(functools.partial(adam_kernel, layers), out_shape=[jax.Sha...  11.3 us

profile of v6, /device:TPU:0, one launch (start us, length us, event | category | flops | bytes accessed | tf_op | source)
XLA Modules:
  0.0 542.7 jit_solution(8765903142859343332)
XLA Ops:
  2.8 0.6 pad_add_fusion.refs_6_.refs_0_
  3.3 0.7 convert_element_type.42
  4.1 0.1 copy.45
  4.2 0.7 fusion.8
  4.9 0.7 slice.29
  5.6 0.1 fusion.7
  5.7 0.6 pad_maximum_fusion.refs_4_
  6.3 0.9 copy.47
  7.2 0.7 pad.31.refs_6_
  7.9 0.9 copy.46
  8.8 0.7 pad.30.refs_8_.refs_7_
  9.5 215.8 %shard_map.391 = (bf16[4,2,2,48,6144]{4,3,2,1,0:T(8,128)(2,1)}, bf16[4,2,2,64,1536]{4,3,2,1,0:T(8,128)(2,1)}, bf16[4,2,2,288,768]{4,3,2,1,0:T(8,128)(2,1)}, bf16...) custom-call(f32[2,24,10752]{2,1,0:T(8,128)} %refs_8_.1, ...), custom_call_target="tpu_custom_call" | custom-call | tf_op jit(solution)/shard_map/pallas_call | solution.py:548
  225.3 79.5 %shard_map.392 = (f32[8,128]{1,0:T(8,128)}, f32[768,128]{1,0:T(8,128)}, f32[88,128]{1,0:T(8,128)}, bf16[320,2304]{1,0:T(8,128)(2,1)}, bf16[320,768]{1,0:T(8,128)...) custom-call(s32[2]{0:T(128)} %pad_add_fusion.refs_6_.refs_0_, ...), custom_call_target="tpu_custom_call" | custom-call | tf_op jit(solution)/shard_map/pallas_call | solution.py:1766
  304.8 222.0 %shard_map.393 = (f32[2,24,6144]{2,1,0:T(8,128)}, f32[2,32,1536]{2,1,0:T(8,128)}, f32[2,144,768]{2,1,0:T(8,128)}, f32[32,10752]{1,0:T(8,128)}, f32[32,256]{1,0:T...) custom-call(bf16[256,1024]{1,0:T(8,128)(2,1)} %bitcast.36, ...), custom_call_target="tpu_custom_call" | custom-call | tf_op jit(solution)/shard_map/pallas_call | solution.py:991
  526.8 1.3 slice_reduce_fusion
  528.1 1.3 fusion.10
  530.1 11.3 %shard_map.394 = (f32[2,24,10752]{2,1,0:T(8,128)}, f32[2,24,10752]{2,1,0:T(8,128)}, f32[2,24,10752]{2,1,0:T(8,128)}, f32[2,32,1536]{2,1,0:T(8,128)}, f32[2,32,15...) custom-call(f32[8,128]{1,0:T(8,128)} %get-tuple-element.155.refs_0_,, ...), custom_call_target="tpu_custom_call" | custom-call | tf_op jit(solution)/shard_map/pallas_call | solution.py:1914
  (4 shorter events, 0.1 us)
